TPU v7x, 256 devices: a whole 4x4x8 slice. The times are simulated.
256 devices in a mesh: shot: 8 (over z), rx: 4 (over y), ry: 8 (over x, core).
Axes of the slice: x: 4, y: 4, z: 8, core: 2. Of those that a mesh axis runs over, the one named last changes fastest.
Arguments:
- traces: bfloat16 [1024, 1024, 1024], P('shot', ('rx', 'ry')), may hold values from -6 to 6
- ghost_filter: bfloat16 [64], replicated, may hold values from -0.75 to 0.75
- bands: int32 [64], replicated, may hold values from 1 to 511
Outputs:
- multiples: float32 [64, 2, 1024, 1024], P('shot', None, 'ry', 'rx')
All inputs are finite; a program needn't handle non-finite values.
Results may differ from a plain program's by a relative error of at most 0.0055.
Values may be sent and summed in bfloat16 or wider, within the bound.
No kernel may reach another device: no remote copies, remote signals or barrier semaphores. Data moves between devices by JAX's collectives and lax.ppermute only.
A program may use at most 128 MiB of HBM per device.

v0:
```python
import math

import jax
import jax.numpy as jnp
from jax import lax
from jax.sharding import PartitionSpec as P


def square_panels(left, right):
    real_left = left[:, 0]
    imag_left = left[:, 1]
    stacked_left = jnp.stack(
        [jnp.concatenate([real_left, -imag_left], -1), jnp.concatenate([imag_left, real_left], -1)],
        1,
    )
    stacked_right = jnp.concatenate([right[:, 0], right[:, 1]], 1)
    factor = -1.0 / math.sqrt(left.shape[3])
    return (
        jnp.einsum(
            "bomk,bkn->bomn", stacked_left, stacked_right, preferred_element_type=jnp.float32
        )
        * factor
    )


def local(traces, ghost_filter, bands):
    shots, receivers, samples = traces.shape
    rows = shots * receivers
    block = min(128, samples)
    blocks_per_trace = samples // block
    taps = ghost_filter.shape[0]
    lag = (
        block
        + jnp.arange(block, dtype=jnp.int32)[None, :]
        - jnp.arange(2 * block, dtype=jnp.int32)[:, None]
    )
    selector = (lag[:, :, None] == jnp.arange(taps, dtype=jnp.int32)[None, None, :]).astype(
        jnp.float32
    )
    toeplitz = jnp.sum(selector * ghost_filter.astype(jnp.float32), -1).astype(jnp.bfloat16)
    pieces = traces.reshape(rows, blocks_per_trace, block)
    earlier = jnp.concatenate([jnp.zeros((rows, 1, block), jnp.bfloat16), pieces[:, :-1]], 1)
    window = jnp.concatenate([earlier, pieces], 2)
    deghosted = jnp.einsum("rcj,ji->rci", window, toeplitz, preferred_element_type=jnp.float32)
    deghosted = deghosted.astype(jnp.bfloat16).reshape(rows, samples)
    count = bands.shape[0]
    phase = jnp.arange(samples, dtype=jnp.int32)[:, None] * bands[None, :] % samples
    angle = 2.0 * math.pi / samples * phase.astype(jnp.float32)
    table = (
        jnp.concatenate([jnp.cos(angle), -jnp.sin(angle)], 1) * (1.0 / math.sqrt(samples))
    ).astype(jnp.bfloat16)
    spectra = jnp.dot(deghosted, table, preferred_element_type=jnp.float32).astype(jnp.bfloat16)
    spectra = jnp.transpose(spectra.reshape(shots, receivers, 2, count), (3, 2, 0, 1))
    owned = lax.all_to_all(spectra, "shot", split_axis=0, concat_axis=2, tiled=True)
    order = owned.shape[2]
    rows_out = order // lax.axis_size("ry")
    cols_out = order // lax.axis_size("rx")
    row_start = lax.axis_index("ry") * rows_out
    full = lax.all_gather(owned, ("rx", "ry"), axis=3, tiled=True)
    left = lax.dynamic_slice_in_dim(full, row_start, rows_out, 2)
    right = lax.dynamic_slice_in_dim(full, lax.axis_index("rx") * cols_out, cols_out, 3)
    product = square_panels(left, right)
    return product


def solution(mesh):
    placed = (P("shot", ("rx", "ry"), None), P(), P())
    return jax.shard_map(
        local, mesh=mesh, in_specs=placed, out_specs=P("shot", None, "ry", "rx"), check_vma=False
    )
```

profile of v0, /device:TPU:1, one launch (start us, length us, event | category | flops | bytes accessed | tf_op | source)
XLA Modules:
  0.0 266.0 jit_solution(10266646878440142743)
XLA Ops:
  6.5 0.0 all-gather.2.cloned.1.call-start
  6.5 8.8 %copy.45 = bf16[512,8,8,128]{3,2,1,0:T(8,128)(2,1)} copy(bf16[512,8,8,128]{3,1,2,0:T(8,128)(2,1)} %bitcast.39) | data formatting | bytes 16777216
  15.3 7.7 %copy.25 = bf16[4096,8,128]{2,0,1:T(8,128)(2,1)} copy(bf16[4096,8,128]{2,1,0:T(8,128)(2,1)} %bitcast.34) | data formatting | bytes 16777216 | tf_op jit(solution)/shard_map/reshape | solution.py:41
  23.0 0.0 copy-start.1
  23.0 0.0 copy-start
  23.0 6.5 %slice.20 = bf16[4096,7,128]{2,0,1:T(8,128)(2,1)} slice(bf16[4096,8,128]{2,0,1:T(8,128)(2,1)} %copy.25), slice={[0:4096], [0:7], [0:128]} | slice | bytes 14680064 | tf_op jit(solution)/shard_map/slice | solution.py:42
  29.5 0.0 copy-done.1
  29.6 0.0 copy-done
  29.6 2.1 fusion.28
  31.6 2.9 %select_reduce_fusion = bf16[256,128]{1,0:T(8,128)(2,1)S(1)} fusion(f32[64]{0:T(128)S(1)} %convert_element_type.19, s32[256,128]{1,0:T(8,128)S(1)} %iota_subtract_fusion), kind=kLoop, calls=%fused_computation.15 | loop fusion | flops 6258688 | bytes 196864 | tf_op jit(solution)/shard_map/reduce_sum | solution.py:40
  34.5 11.2 %fusion.14 = bf16[4096,8,128]{0,2,1:T(8,128)(2,1)} fusion(bf16[4096,7,128]{2,0,1:T(8,128)(2,1)} %slice.20, bf16[4096,8,128]{2,0,1:T(8,128)(2,1)} %copy.25, bf16[256,128]{1,0:T(8,128)(2,1)S(1)} %select_reduce_fusion), kind=kOutput, calls=%fused_computation.17 | convolution fusion | flops 2202009600 | bytes 24182784 | tf_op jit(solution)/shard_map/rcj,ji->rci/dot_general | solution.py:44
  45.8 6.0 %convolution_convert_fusion = bf16[4096,128]{1,0:T(8,128)(2,1)S(1)} fusion(bf16[4096,1024]{0,1:T(8,128)(2,1)} %bitcast.36, f32[1024,64]{1,0:T(8,128)S(1)} %get-tuple-element.12, f32[1024,64]{1,0:T(8,128)S(1)} %get-tuple-element.11), kind=kOutput, calls=%fused_computation.18 | convolution fusion | flops 1074659328 | bytes 9961472 | tf_op jit(solution)/shard_map/dot_general | solution.py:52
  51.8 0.8 reshape.37
  52.6 2.7 %copy.28 = bf16[64,2,128,32]{2,3,1,0:T(8,128)(2,1)S(1)} copy(bf16[64,2,128,32]{0,1,3,2:T(2,128)(2,1)S(1)} %bitcast.38) | data formatting | bytes 2097152 | tf_op jit(solution)/shard_map/transpose | solution.py:53
  55.3 36.0 %all_to_all.18 = bf16[64,2,128,32]{2,3,1,0:T(8,128)(2,1)S(1)} all-to-all(bf16[64,2,128,32]{2,3,1,0:T(8,128)(2,1)S(1)} %copy.28), channel_id=1, replica_groups=mesh['shot'=8,'rx'=4,'ry'=8] {'shot'}, dimensions={0} | all-to-all | bytes 2097152 | tf_op jit(solution)/shard_map/all_to_all | solution.py:54
  91.4 0.7 copy.37
  92.0 1.3 reshape.40
  93.3 0.0 all-gather.2.cloned.1.call-update
  93.3 117.5 %all-gather.2.cloned.1.call-done = bf16[8,2,1024,1024]{2,0,1,3:T(8,128)(2,1)} async-done(((bf16[8,2,1024,32]{2,0,1,3:T(8,128)(2,1)}), bf16[8,2,1024,1024]{2,0,1,3:T(8,128)(2,1)}) %all-gather.2.cloned.1.call-update) | async-done | bytes 33554448 | tf_op jit(solution)/shard_map/all_gather | solution.py:59
  210.9 7.7 %constant_dynamic-slice_fusion = (bf16[8,1,1024,256]{2,0,1,3:T(8,128)(2,1)}, bf16[8,1,1024,256]{2,0,1,3:T(8,128)(2,1)}) fusion(bf16[8,2,1024,1024]{2,0,1,3:T(8,128)(2,1)} %all-gather.2.cloned.1.call-done, s32[]{:T(128)S(6)} %select_n.15, s32[]{:T(128)S(6)} %add.30), kind=kLoop, calls=%fused_computation.39 | loop fusion | bytes 16777224 | tf_op jit(solution)/shard_map/slice | solution.py:16
  218.5 6.9 %copy.44 = bf16[8,1,1024,256]{3,2,0,1:T(8,128)(2,1)} copy(bf16[8,1,1024,256]{2,0,1,3:T(8,128)(2,1)} %get-tuple-element.8) | data formatting | bytes 8388608
  225.4 6.8 %copy.43 = bf16[8,1,1024,256]{3,2,0,1:T(8,128)(2,1)} copy(bf16[8,1,1024,256]{2,0,1,3:T(8,128)(2,1)} %get-tuple-element.7) | data formatting | bytes 8388608
  232.2 4.5 %constant_dynamic-slice_fusion.3 = (bf16[8,1,128,1024]{2,0,1,3:T(8,128)(2,1)}, bf16[8,1,128,1024]{2,0,1,3:T(8,128)(2,1)}) fusion(bf16[8,2,1024,1024]{2,0,1,3:T(8,128)(2,1)} %all-gather.2.cloned.1.call-done, s32[]{:T(128)S(6)} %add.30, s32[]{:T(128)S(6)} %select_n.14), kind=kLoop, calls=%fused_computation.42 | loop fusion | bytes 8388616 | tf_op jit(solution)/shard_map/slice | solution.py:11
  236.8 3.2 %copy.41 = bf16[8,1,128,1024]{3,2,0,1:T(8,128)(2,1)S(1)} copy(bf16[8,1,128,1024]{2,0,1,3:T(8,128)(2,1)} %get-tuple-element.5) | data formatting | bytes 4194304
  240.0 1.5 bitcast_negate_fusion
  241.5 4.2 %copy.40 = bf16[8,1,128,1024]{3,2,0,1:T(8,128)(2,1)} copy(bf16[8,1,128,1024]{2,0,1,3:T(8,128)(2,1)} %get-tuple-element.6) | data formatting | bytes 4194304
  245.6 5.1 %maximum_bitcast_fusion.2 = (bf16[8,1,128,2048]{3,2,1,0:T(8,128)(2,1)S(1)}, bf16[8,1,128,2048]{3,2,1,0:T(8,128)(2,1)}) fusion(bf16[8,128,1024]{2,1,0:T(8,128)(2,1)} %bitcast_negate_fusion, bf16[8,128,1024]{2,1,0:T(8,128)(2,1)} %bitcast.37, bf16[8,128,1024]{2,1,0:T(8,128)(2,1)S(1)} %bitcast.35), kind=kLoop, calls=%fused_computation.19 | loop fusion | flops 16777216 | bytes 14680064 | tf_op jit(solution)/shard_map/stack | solution.py:12
  250.7 8.4 %broadcast_multiply_fusion = f32[8,2,128,256]{3,2,1,0:T(8,128)} fusion(bf16[8,1024,256]{2,1,0:T(8,128)(2,1)} %bitcast.40, bf16[8,1024,256]{2,1,0:T(8,128)(2,1)} %bitcast.41, bf16[8,1,128,2048]{3,2,1,0:T(8,128)(2,1)} %get-tuple-element.10, bf16[8,1,128,2048]{3,2,1,0:T(8,128)(2,1)S(1)} %get-tuple-element.9), kind=kOutput, calls=%fused_computation.21 | convolution fusion | flops 2168979456 | bytes 18874368 | tf_op jit(solution)/shard_map/bomk,bkn->bomn/dot_general | solution.py:19
  (3 shorter events, 0.0 us)
Async XLA Ops:
  6.5 204.3 %all-gather.2.cloned.1.call-start = ((), (), s32[]{:S(2)}) async-start(), calls=%async_computation.1 | async-start | bytes 34603008 | tf_op jit(solution)/shard_map/all_gather | solution.py:59
  23.0 6.5 %copy-start.1 = (bf16[64]{0:T(256)(128)(2,1)S(1)}, bf16[64]{0:T(256)(128)(2,1)}, u32[]{:S(2)}) copy-start(bf16[64]{0:T(256)(128)(2,1)} %param.4) | copy-start | bytes 388
  23.0 6.6 %copy-start = (s32[64]{0:T(128)S(1)}, s32[64]{0:T(128)}, u32[]{:S(2)}) copy-start(s32[64]{0:T(128)} %param.5) | copy-start | bytes 772
Sparse Core Ops, SparseCore 0:
  93.5 117.3 all-gather.1
where the time goes:
time: 267 us; the launch traced here: 266 us
  waiting for transfers between devices  118 us (44%)
  local copies, waits for them, and re-layouts  61.8 us (23%)
  blocking collectives  36 us (13%)
  matrix products  25.6 us (10%)
  between operations  13.5 us (5%)
  other arithmetic  11.5 us (4%)
    all_gather x1, waiting for transfers between devices, local(): full = lax.all_gather(owned, ('rx', 'ry'), axis=3, tiled=True)  118 us
    all_to_all x1, blocking collectives, local(): lax.all_to_all(spectra, 'shot', split_axis=0, concat_axis=2, tiled=True)  36 us
    unnamed x9, local copies, waits for them, and re-layouts  29.9 us
    dot_general x1, matrix products, local(): jnp.einsum('rcj,ji->rci', window, toeplitz, preferred_element_type=jnp.fl...  11.2 us
    dot_general x1, matrix products, square_panels(): jnp.einsum('bomk,bkn->bomn', stacked_left, stacked_right, preferred_eleme...  8.4 us
    reshape x1, local copies, waits for them, and re-layouts, local(): pieces = traces.reshape(rows, blocks_per_trace, block)  7.68 us
    slice x1, local copies, waits for them, and re-layouts, square_panels(): stacked_right = jnp.concatenate([right[:, 0], right[:, 1]], 1)  7.66 us
    slice x1, local copies, waits for them, and re-layouts, local(): pieces[:, :-1]  6.53 us
  transfers between devices with their start and end apart: 1, of which 1 were waited for; matrix products, arithmetic and copies ran while one was open for 0% of the time, Pallas kernels for 0%

commit v1 on v0

v1 whole, which is shorter than its diff:
```python
import functools
import math

import jax
import jax.numpy as jnp
from jax import lax
from jax.experimental import pallas as pl
from jax.experimental.pallas import tpu as pltpu
from jax.sharding import PartitionSpec as P

CHUNKS = 1
VMEM_LIMIT = 56 * 1024 * 1024


def filter_table(taps_ref, bands_ref, weights_ref, table_ref):
    samples = weights_ref.shape[0]
    taps = taps_ref.shape[1]
    bands = bands_ref[...]
    count = bands.shape[1]
    both = jnp.concatenate([bands, bands], 1)
    first = lax.broadcasted_iota(jnp.int32, (1, 2 * count), 1) < count
    step = 32
    index = lax.broadcasted_iota(jnp.int32, (step, 2 * count), 0)

    def angle_of(times):
        phase = lax.rem(times * both, samples)
        return (2.0 * math.pi / samples) * phase.astype(jnp.float32)

    coarse = angle_of(index * step)
    fine = angle_of(index)
    coarse_cos, coarse_sin = jnp.cos(coarse), jnp.sin(coarse)
    scale = 1.0 / math.sqrt(samples)
    fine_cos, fine_sin = jnp.cos(fine) * scale, jnp.sin(fine) * scale
    first_part = jnp.where(first, coarse_cos, -coarse_sin)
    second_part = jnp.where(first, coarse_sin, coarse_cos)
    for block in range(samples // step):
        rows = (
            first_part[block : block + 1] * fine_cos - second_part[block : block + 1] * fine_sin
        )
        table_ref[block * step : (block + 1) * step, :] = rows.astype(jnp.bfloat16)
    table_ref[samples:, :] = jnp.zeros((table_ref.shape[0] - samples, 2 * count), jnp.bfloat16)

    block = 128
    padded = jnp.concatenate(
        [taps_ref[...].astype(jnp.float32), jnp.zeros((1, 2 * block - taps), jnp.float32)], 1
    )
    band_matrix = pltpu.roll(
        jnp.broadcast_to(padded, (block, 2 * block)), 0, 1, stride=1, stride_axis=0
    ).astype(jnp.bfloat16)
    for at in range(samples // block):
        filtered = jnp.dot(
            band_matrix,
            table_ref[at * block : (at + 2) * block, :],
            preferred_element_type=jnp.float32,
        )
        high = filtered.astype(jnp.bfloat16)
        low = (filtered - high.astype(jnp.float32)).astype(jnp.bfloat16)
        weights_ref[at * block : (at + 1) * block, : 2 * count] = high
        weights_ref[at * block : (at + 1) * block, 2 * count :] = low


def front_kernel(
    place_ref, taps_ref, bands_ref, traces_ref, *rest, chunks, planes, owned
):
    outs = rest[: 2 * chunks]
    weights_ref, table_ref, picked_ref, turned_ref = rest[2 * chunks :]
    shots, receivers, samples = traces_ref.shape
    count = bands_ref.shape[1]

    @pl.when(pl.program_id(0) == 0)
    def _():
        filter_table(taps_ref, bands_ref, weights_ref, table_ref)

    group = 16
    for at in range(shots // group):
        block = traces_ref[at * group : (at + 1) * group].reshape(group * receivers, samples)
        both = jnp.dot(block, weights_ref[...], preferred_element_type=jnp.float32)
        picked_ref[at * group * receivers : (at + 1) * group * receivers, :] = (
            both[:, : 2 * count] + both[:, 2 * count :]
        )
    for receiver in range(receivers):
        turned_ref[receiver * 2 * count : (receiver + 1) * 2 * count, :] = picked_ref[
            pl.ds(receiver, shots, stride=receivers), :
        ].T
    plane, core = place_ref[0], place_ref[1]
    half = owned // 2
    per_chunk = half // chunks
    for other in range(2):
        for hop in range(planes):
            base = lax.rem(plane + hop, planes) * owned + (core ^ other) * half
            for part in range(2):
                for band in range(half):
                    lane = base + (part * count + band)
                    rows = turned_ref[pl.ds(lane, receivers, stride=2 * count), :]
                    outs[other * chunks + band // per_chunk][
                        hop, part * per_chunk + band % per_chunk
                    ] = rows.astype(jnp.bfloat16)


def front(place, taps, bands, traces, chunks, planes):
    shots, receivers, samples = traces.shape
    count = bands.shape[0]
    owned = count // planes
    block = 16
    per_chunk = owned // chunks
    out = jax.ShapeDtypeStruct((planes, per_chunk, receivers, shots), jnp.bfloat16)
    out_spec = pl.BlockSpec((planes, per_chunk, block, shots), lambda i, place: (0, 0, i, 0))
    return pl.pallas_call(
        functools.partial(front_kernel, chunks=chunks, planes=planes, owned=owned),
        out_shape=[out] * (2 * chunks),
        grid_spec=pltpu.PrefetchScalarGridSpec(
            num_scalar_prefetch=1,
            grid=(receivers // block,),
            in_specs=[
                pl.BlockSpec((1, taps.shape[0]), lambda i, place: (0, 0)),
                pl.BlockSpec((1, count), lambda i, place: (0, 0)),
                pl.BlockSpec((shots, block, samples), lambda i, place: (0, i, 0)),
            ],
            out_specs=[out_spec] * (2 * chunks),
            scratch_shapes=[
                pltpu.VMEM((samples, 4 * count), jnp.bfloat16),
                pltpu.VMEM((samples + 128, 2 * count), jnp.bfloat16),
                pltpu.VMEM((shots * block, 2 * count), jnp.float32),
                pltpu.VMEM((block * 2 * count, shots), jnp.float32),
            ],
        ),
        compiler_params=pltpu.CompilerParams(vmem_limit_bytes=VMEM_LIMIT),
        cost_estimate=pl.CostEstimate(
            flops=4 * shots * receivers * samples * count * 2,
            bytes_accessed=shots * receivers * samples * 2,
            transcendentals=0,
        ),
        name="front",
    )(place, taps.reshape(1, -1), bands.reshape(1, -1), traces)


UP = ((6, 2), (0, 2), (4, 2))
DOWN = ((1, 3), (0, 1), (4, 2))


def sort_kernel(place_ref, *refs):
    pieces = refs[:8]
    own, up_turn, down_turn, far_turn, up, down, held, sems = refs[8:]
    plane, chip = place_ref[0], place_ref[2]

    def start(copies):
        for copy in copies:
            copy.start()
        for copy in copies:
            copy.wait()

    start(
        [
            pltpu.make_async_copy(
                piece, held.at[lax.rem(plane - hop - 2 * chip + 16, 8)], sems.at[hop]
            )
            for hop, piece in enumerate(pieces)
        ]
    )
    moves = [
        (0, 2, own, 0),
        (2, 2, up_turn, 0),
        (6, 2, down_turn, 0),
        (4, 2, far_turn, 0),
    ]
    for target, order in ((up, UP), (down, DOWN)):
        at = 0
        for first, size in order:
            moves.append((first, size, target, at))
            at += size
    start(
        [
            pltpu.make_async_copy(
                held.at[pl.ds(first, size)], target.at[pl.ds(at, size)], sems.at[number]
            )
            for number, (first, size, target, at) in enumerate(moves)
        ]
    )


def sort_blocks(place, pieces):
    shape = pieces[0].shape
    two = jax.ShapeDtypeStruct((2,) + shape, jnp.bfloat16)
    six = jax.ShapeDtypeStruct((6,) + shape, jnp.bfloat16)
    hbm = pl.BlockSpec(memory_space=pl.ANY)
    return pl.pallas_call(
        sort_kernel,
        out_shape=[two, two, two, two, six, six],
        in_specs=[pl.BlockSpec(memory_space=pltpu.SMEM)] + [hbm] * 8,
        out_specs=[hbm] * 6,
        scratch_shapes=[
            pltpu.VMEM((8,) + shape, jnp.bfloat16),
            pltpu.SemaphoreType.DMA((10,)),
        ],
        compiler_params=pltpu.CompilerParams(vmem_limit_bytes=4 * 1024 * 1024),
        cost_estimate=pl.CostEstimate(flops=0, bytes_accessed=4 << 20, transcendentals=0),
        name="sort",
    )(place, *pieces)


def product_kernel(place_ref, *refs, bands):
    pieces = refs[:8]
    up_turn, down_turn, far_turn, up, down, up_far, down_far = refs[8:15]
    left_own, left_up, left_down, left_up_far, left_down_far = refs[15:20]
    keep_ref, give_ref, right, left, sems = refs[20:]
    plane, core, chip, column = (place_ref[i] for i in range(4))
    width = pieces[0].shape[1]
    copies = []

    def copy(source, target):
        copies.append(pltpu.make_async_copy(source, target, sems.at[len(copies)]))

    def into_right(source, first, size, target_chip):
        block = lax.rem(2 * target_chip + first, 8)
        start = pl.multiple_of(target_chip * width, width)
        copy(source, right.at[pl.ds(block, size), :, pl.ds(start, width), :])

    for hop, piece in enumerate(pieces):
        copy(
            piece,
            right.at[
                lax.rem(plane - hop + 8, 8), :, pl.ds(pl.multiple_of(chip * width, width), width), :
            ],
        )
    below, above, across = lax.rem(chip + 3, 4), lax.rem(chip + 1, 4), lax.rem(chip + 2, 4)
    into_right(up_turn, 2, 2, below)
    into_right(down_turn, 6, 2, above)
    into_right(far_turn, 4, 2, across)
    for source, order, target_chip in ((up, UP, below), (down, DOWN, above)):
        at = 0
        for first, size in order:
            while size:
                step = min(size, 2 - first % 2)
                into_right(source.at[pl.ds(at, step)], first, step, target_chip)
                at, first, size = at + step, first + step, size - step
    for source, order in ((up_far, UP), (down_far, DOWN)):
        at = 0
        for first, size in order:
            while size and at < 3:
                step = min(size, 2 - first % 2, 3 - at)
                into_right(source.at[pl.ds(at, step)], first, step, across)
                at, first, size = at + step, first + step, size - step
    chips = (chip, below, above, across)
    for source, slots, hop in (
        (left_own, range(4), 0),
        (left_up, range(4), 3),
        (left_down, range(4), 1),
        (left_up_far, range(2), 2),
        (left_down_far, range(2, 4), 2),
    ):
        for at, slot in enumerate(slots):
            start = lax.rem(column + hop, 4) * 4 * width + chips[slot] * width
            copy(
                source.at[at],
                left.at[:, :, pl.ds(pl.multiple_of(start, width), width), :],
            )
    for one in copies:
        one.start()
    for one in copies:
        one.wait()

    order = 8 * 128
    factor = -1.0 / math.sqrt(order)
    for band in range(bands):
        rows = [
            jnp.concatenate([right[z, part * bands + band] for z in range(8)], 1)
            for part in range(2)
        ]
        columns = [
            jnp.concatenate([left[s, part * bands + band] for s in range(2)], 1)
            for part in range(2)
        ]

        def times(a, b):
            return jnp.dot(rows[a], columns[b], preferred_element_type=jnp.float32)

        for part, value in enumerate(
            (times(0, 0) - times(1, 1), times(0, 1) + times(1, 0))
        ):
            turned = (value * factor).T
            low, high = turned[:128], turned[128:]
            keep_ref[band, part] = jnp.where(core == 0, low, high)
            give_ref[band, part] = jnp.where(core == 0, high, low)


def product(place, pieces, rest):
    parts, width, shots = pieces[0].shape
    bands = parts // 2
    receivers = 4 * width
    hbm = pl.BlockSpec(memory_space=pl.ANY)
    out = jax.ShapeDtypeStruct((bands, 2, shots, receivers), jnp.float32)
    return pl.pallas_call(
        functools.partial(product_kernel, bands=bands),
        out_shape=[out, out],
        in_specs=[pl.BlockSpec(memory_space=pltpu.SMEM)] + [hbm] * 20,
        scratch_shapes=[
            pltpu.VMEM((8, parts, receivers, shots), jnp.bfloat16),
            pltpu.VMEM((2, parts, 4 * receivers, shots), jnp.bfloat16),
            pltpu.SemaphoreType.DMA((64,)),
        ],
        compiler_params=pltpu.CompilerParams(vmem_limit_bytes=32 * 1024 * 1024),
        cost_estimate=pl.CostEstimate(
            flops=8 * bands * receivers * receivers * 1024,
            bytes_accessed=24 << 20,
            transcendentals=0,
        ),
        name="product",
    )(place, *pieces, *rest)


def local(traces, ghost_filter, bands):
    plane = lax.axis_index("shot")
    column = lax.axis_index("rx")
    row = lax.axis_index("ry")
    core, chip = row % 2, row // 2
    place = jnp.stack([plane, core, chip, column]).astype(jnp.int32)
    planes = 8
    fronts = front(place, ghost_filter, bands, traces, CHUNKS, planes)
    mine, others = fronts[:CHUNKS], fronts[CHUNKS:]

    def along_x(value, hop):
        pairs = [(i, ((i // 2 + hop) % 4) * 2 + i % 2) for i in range(8)]
        return lax.ppermute(value, "ry", pairs)

    def along_y(value, hop):
        return lax.ppermute(value, "rx", [(i, (i + hop) % 4) for i in range(4)])

    def along_z(value, hop):
        return lax.ppermute(value, "shot", [(i, (i + hop) % planes) for i in range(planes)])

    def swap(value):
        return lax.ppermute(value, "ry", [(i, i ^ 1) for i in range(8)])

    keeps, takes = [], []
    for chunk in range(CHUNKS):
        own = mine[chunk]
        theirs = swap(others[chunk])
        low = jnp.where(core == 0, own, theirs)
        high = jnp.where(core == 0, theirs, own)
        pieces = []
        for hop in range(planes):
            piece = jnp.concatenate([low[hop], high[hop]], 1)
            pieces.append(along_z(piece, hop) if hop else piece)
        own_turn, up_turn, down_turn, far_turn, up, down = sort_blocks(place, pieces)
        up_turn, down_turn, far_turn = (
            along_x(up_turn, 1),
            along_x(down_turn, -1),
            along_x(far_turn, 2),
        )
        up, down = along_x(up, 1), along_x(down, -1)
        up_far, down_far = along_x(up[:3], 1), along_x(down[:3], -1)
        left = jnp.stack([own_turn, up_turn, down_turn, far_turn])
        left_up, left_down = along_y(left, 1), along_y(left, -1)
        left_up_far, left_down_far = along_y(left_up[:2], 1), along_y(left_down[2:], -1)
        keep, give = product(
            place,
            pieces,
            (up_turn, down_turn, far_turn, up, down, up_far, down_far)
            + (left, left_up, left_down, left_up_far, left_down_far),
        )
        keeps.append(keep)
        takes.append(swap(give))
    return jnp.where(
        core == 0,
        jnp.concatenate(keeps + takes),
        jnp.concatenate(takes + keeps),
    )


def solution(mesh):
    placed = (P("shot", ("rx", "ry"), None), P(), P())
    return jax.shard_map(
        local, mesh=mesh, in_specs=placed, out_specs=P("shot", None, "ry", "rx"), check_vma=False
    )
```

time: 267 us -> 119 us (0.45)
  local copies, waits for them, and re-layouts: 61.8 us -> 0.2 us
  waiting for transfers between devices: 118 us -> 60.2 us
  starting transfers between devices: 0.01 us -> 38.2 us
  blocking collectives: 36 us -> 0 us
  matrix products: 25.6 us -> 0 us
  Pallas kernels: 0 us -> 16 us
  between operations: 13.5 us -> 0.15 us
  other arithmetic: 11.5 us -> 3.48 us
    all_gather x1 -> x0, waiting for transfers between devices: 118 us -> none  [local(): full = lax.all_gather(owned, ('rx', 'ry'), axis=3, tiled=True)]
    ppermute x0 -> x20, waiting for transfers between devices: none -> 60.2 us  [the longest x4 21.2 us: along_y(): return lax.ppermute(value, 'rx', [(i, (i + hop) % 4) for i in range(4)])]
    ppermute x0 -> x20, starting transfers between devices: none -> 38.2 us  [the longest x7 15.3 us: along_z(): lax.ppermute(value, 'shot', [(i, (i + hop) % planes) for i in range(plane...]
    all_to_all x1 -> x0, blocking collectives: 36 us -> none  [local(): lax.all_to_all(spectra, 'shot', split_axis=0, concat_axis=2, tiled=True)]
    unnamed x9 -> x2, local copies, waits for them, and re-layouts: 29.9 us -> 0.01 us
    dot_general x3 -> x0, matrix products: 25.6 us -> none  [the longest x1 11.2 us: local(): jnp.einsum('rcj,ji->rci', window, toeplitz, preferred_element_type=jnp.fl...]
    slice x3 -> x4, local copies, waits for them, and re-layouts: 18.7 us -> 0.12 us  [the longest x2 0.05 us: local(): up_far, down_far = (along_x(up[:3], 1), along_x(down[:3], -1))]
    pallas_call x0 -> x3, Pallas kernels: none -> 16 us  [the longest x1 8.71 us: front(): pl.pallas_call(functools.partial(front_kernel, chunks=chunks, planes=plan...]
  transfers between devices with their start and end apart: 1 -> 20, of which waited for: 1 -> 11; matrix products, arithmetic and copies ran while one was open for 0% -> 0% of each run, Pallas kernels for 0% -> 0%
where the time goes in v1:
time: 119 us; the launch traced here: 118 us
  waiting for transfers between devices  60.2 us (51%)
  starting transfers between devices  38.2 us (32%)
  Pallas kernels  16 us (13%)
  other arithmetic  3.48 us (3%)
    ppermute x4, waiting for transfers between devices, along_y(): return lax.ppermute(value, 'rx', [(i, (i + hop) % 4) for i in range(4)])  21.2 us
    ppermute x7, waiting for transfers between devices, along_x(): return lax.ppermute(value, 'ry', pairs)  17.6 us
    ppermute x7, waiting for transfers between devices, along_z(): lax.ppermute(value, 'shot', [(i, (i + hop) % planes) for i in range(plane...  17.5 us
    ppermute x7, starting transfers between devices, along_z(): lax.ppermute(value, 'shot', [(i, (i + hop) % planes) for i in range(plane...  15.3 us
    ppermute x7, starting transfers between devices, along_x(): return lax.ppermute(value, 'ry', pairs)  9.79 us
    pallas_call x1, Pallas kernels, front(): pl.pallas_call(functools.partial(front_kernel, chunks=chunks, planes=plan...  8.71 us
    ppermute x2, starting transfers between devices, swap(): return lax.ppermute(value, 'ry', [(i, i ^ 1) for i in range(8)])  6.74 us
    ppermute x4, starting transfers between devices, along_y(): return lax.ppermute(value, 'rx', [(i, (i + hop) % 4) for i in range(4)])  6.38 us
  transfers between devices with their start and end apart: 20, of which 11 were waited for; matrix products, arithmetic and copies ran while one was open for 0% of the time, Pallas kernels for 0%

profile of v1, /device:TPU:1, one launch (start us, length us, event | category | flops | bytes accessed | tf_op | source)
XLA Modules:
  0.0 118.2 jit_solution(2337642600150358673)
XLA Ops:
  0.0 0.6 pad_add_fusion.place_ref
  0.6 8.7 %front.1 = (bf16[8,8,32,128]{3,2,1,0:T(8,128)(2,1)}, bf16[8,8,32,128]{3,2,1,0:T(8,128)(2,1)}) custom-call(s32[4]{0:T(128)} %pad_add_fusion.place_ref, bf16[1,64]{1,0:T(2,128)(2,1)} %bitcast.46, s32[1,64]{1,0:T(1,128)} %bitcast.47, bf16[128,32,1024]{2,1,0:T(8,128)(2,1)} %traces_ref.1), custom_call_target="tpu_custom_call" | custom-call | flops 2147483648 | bytes 8388608 | tf_op jit(solution)/shard_map/front/pallas_call | solution.py:108
  9.4 3.2 %collective-permute-start = (bf16[8,8,32,128]{3,2,1,0:T(8,128)(2,1)}, bf16[8,8,32,128]{3,2,1,0:T(8,128)(2,1)S(1)}, u32[]{:S(2)}, u32[]{:S(2)}) collective-permute-start(bf16[8,8,32,128]{3,2,1,0:T(8,128)(2,1)} %get-tuple-element.16), channel_id=1, source_target_pairs={{0,1},{1,0},{2,3},{3,2},{4,5},{5,4},{6,7},{7,6},{8,9},{9,8},{10,11... | collective-permute-start | bytes 1572872 | tf_op jit(solution)/shard_map/ppermute | solution.py:332
  12.6 1.7 %collective-permute-done = bf16[8,8,32,128]{3,2,1,0:T(8,128)(2,1)S(1)} collective-permute-done((bf16[8,8,32,128]{3,2,1,0:T(8,128)(2,1)}, bf16[8,8,32,128]{3,2,1,0:T(8,128)(2,1)S(1)}, u32[]{:S(2)}, u32[]{:S(2)}) %collective-permute-start) | collective-permute-done | bytes 524320 | tf_op jit(solution)/shard_map/ppermute | solution.py:332
  14.4 1.1 broadcast_select_fusion.1
  15.5 0.1 slice_bitcast_fusion
  15.6 0.1 collective-permute-start.1
  15.7 2.9 %collective-permute-start.2 = (bf16[8,64,128]{2,1,0:T(8,128)(2,1)S(1)}, bf16[8,64,128]{2,1,0:T(8,128)(2,1)S(1)}, u32[]{:S(2)}, u32[]{:S(2)}) collective-permute-start(bf16[8,64,128]{2,1,0:T(8,128)(2,1)S(1)} %pad_maximum_fusion.3), channel_id=1, source_target_pairs={{0,64},{32,96},{64,128},{96,160},{128,192},{160,224},{192,0},{224,... | collective-permute-start | bytes 393224 | tf_op jit(solution)/shard_map/ppermute | solution.py:329
  18.7 3.8 %collective-permute-start.3 = (bf16[8,64,128]{2,1,0:T(8,128)(2,1)S(1)}, bf16[8,64,128]{2,1,0:T(8,128)(2,1)S(1)}, u32[]{:S(2)}, u32[]{:S(2)}) collective-permute-start(bf16[8,64,128]{2,1,0:T(8,128)(2,1)S(1)} %pad_maximum_fusion.4), channel_id=1, source_target_pairs={{0,96},{32,128},{64,160},{96,192},{128,224},{160,0},{192,32},{224,... | collective-permute-start | bytes 393224 | tf_op jit(solution)/shard_map/ppermute | solution.py:329
  22.5 0.6 collective-permute-start.4
  23.1 4.5 %collective-permute-start.5 = (bf16[8,64,128]{2,1,0:T(8,128)(2,1)S(1)}, bf16[8,64,128]{2,1,0:T(8,128)(2,1)S(1)}, u32[]{:S(2)}, u32[]{:S(2)}) collective-permute-start(bf16[8,64,128]{2,1,0:T(8,128)(2,1)S(1)} %pad_maximum_fusion.6), channel_id=1, source_target_pairs={{0,160},{32,192},{64,224},{96,0},{128,32},{160,64},{192,96},{224,1... | collective-permute-start | bytes 393224 | tf_op jit(solution)/shard_map/ppermute | solution.py:329
  27.6 0.0 collective-permute-done.1.refs_1_
  27.6 2.5 %collective-permute-start.6 = (bf16[8,64,128]{2,1,0:T(8,128)(2,1)S(1)}, bf16[8,64,128]{2,1,0:T(8,128)(2,1)S(1)}, u32[]{:S(2)}, u32[]{:S(2)}) collective-permute-start(bf16[8,64,128]{2,1,0:T(8,128)(2,1)S(1)} %pad_maximum_fusion.7), channel_id=1, source_target_pairs={{0,192},{32,224},{64,0},{96,32},{128,64},{160,96},{192,128},{224,1... | collective-permute-start | bytes 393224 | tf_op jit(solution)/shard_map/ppermute | solution.py:329
  30.1 0.0 collective-permute-done.2.refs_2_
  30.1 0.8 collective-permute-start.7
  31.0 8.2 %collective-permute-done.3.refs_3_ = bf16[8,64,128]{2,1,0:T(8,128)(2,1)S(1)} collective-permute-done((bf16[8,64,128]{2,1,0:T(8,128)(2,1)S(1)}, bf16[8,64,128]{2,1,0:T(8,128)(2,1)S(1)}, u32[]{:S(2)}, u32[]{:S(2)}) %collective-permute-start.3) | collective-permute-done | bytes 131104 | tf_op jit(solution)/shard_map/ppermute | solution.py:329
  39.2 0.5 collective-permute-done.4.refs_4_
  39.7 0.0 collective-permute-done.5.refs_5_
  39.7 7.9 %collective-permute-done.6.refs_6_ = bf16[8,64,128]{2,1,0:T(8,128)(2,1)S(1)} collective-permute-done((bf16[8,64,128]{2,1,0:T(8,128)(2,1)S(1)}, bf16[8,64,128]{2,1,0:T(8,128)(2,1)S(1)}, u32[]{:S(2)}, u32[]{:S(2)}) %collective-permute-start.6) | collective-permute-done | bytes 131104 | tf_op jit(solution)/shard_map/ppermute | solution.py:329
  47.6 0.8 collective-permute-done.7.refs_7_
  48.4 2.7 %sort.1 = (bf16[2,8,64,128]{3,2,1,0:T(8,128)(2,1)S(1)}, bf16[2,8,64,128]{3,2,1,0:T(8,128)(2,1)S(1)}, bf16[2,8,64,128]{3,2,1,0:T(8,128)(2,1)S(1)}, bf16[2,8,64,12...) custom-call(s32[4]{0:T(128)S(1)} %copy-done, ...), custom_call_target="tpu_custom_call" | custom-call | bytes 4194304 | tf_op jit(solution)/shard_map/sort/pallas_call | solution.py:186
  51.1 1.3 %collective-permute-start.8 = (bf16[2,8,64,128]{3,2,1,0:T(8,128)(2,1)S(1)}, bf16[2,8,64,128]{3,2,1,0:T(8,128)(2,1)S(1)}, u32[]{:S(2)}, u32[]{:S(2)}) collective-permute-start(bf16[2,8,64,128]{3,2,1,0:T(8,128)(2,1)S(1)} %get-tuple-element.17), channel_id=1, source_target_pairs={{0,2},{1,3},{2,4},{3,5},{4,6},{5,7},{6,0},{7,1},{8,10},{9,11},{10,... | collective-permute-start | bytes 786440 | tf_op jit(solution)/shard_map/ppermute | solution.py:323
  52.4 1.5 %collective-permute-start.9 = (bf16[2,8,64,128]{3,2,1,0:T(8,128)(2,1)S(1)}, bf16[2,8,64,128]{3,2,1,0:T(8,128)(2,1)S(1)}, u32[]{:S(2)}, u32[]{:S(2)}) collective-permute-start(bf16[2,8,64,128]{3,2,1,0:T(8,128)(2,1)S(1)} %get-tuple-element.18), channel_id=1, source_target_pairs={{0,6},{1,7},{2,0},{3,1},{4,2},{5,3},{6,4},{7,5},{8,14},{9,15},{10,... | collective-permute-start | bytes 786440 | tf_op jit(solution)/shard_map/ppermute | solution.py:323
  53.9 1.5 %collective-permute-start.10 = (bf16[2,8,64,128]{3,2,1,0:T(8,128)(2,1)S(1)}, bf16[2,8,64,128]{3,2,1,0:T(8,128)(2,1)S(1)}, u32[]{:S(2)}, u32[]{:S(2)}) collective-permute-start(bf16[2,8,64,128]{3,2,1,0:T(8,128)(2,1)S(1)} %get-tuple-element.19), channel_id=1, source_target_pairs={{0,4},{1,5},{2,6},{3,7},{4,0},{5,1},{6,2},{7,3},{8,12},{9,13},{10,... | collective-permute-start | bytes 786440 | tf_op jit(solution)/shard_map/ppermute | solution.py:323
  55.4 4.4 %collective-permute-done.8.refs_8_ = bf16[2,8,64,128]{3,2,1,0:T(8,128)(2,1)S(1)} collective-permute-done((bf16[2,8,64,128]{3,2,1,0:T(8,128)(2,1)S(1)}, bf16[2,8,64,128]{3,2,1,0:T(8,128)(2,1)S(1)}, u32[]{:S(2)}, u32[]{:S(2)}) %collective-permute-start.8) | collective-permute-done | bytes 262176 | tf_op jit(solution)/shard_map/ppermute | solution.py:323
  59.8 0.0 collective-permute-done.9.refs_9_
  59.8 6.6 %collective-permute-done.10.refs_10_ = bf16[2,8,64,128]{3,2,1,0:T(8,128)(2,1)S(1)} collective-permute-done((bf16[2,8,64,128]{3,2,1,0:T(8,128)(2,1)S(1)}, bf16[2,8,64,128]{3,2,1,0:T(8,128)(2,1)S(1)}, u32[]{:S(2)}, u32[]{:S(2)}) %collective-permute-start.10) | collective-permute-done | bytes 262176 | tf_op jit(solution)/shard_map/ppermute | solution.py:323
  66.4 0.1 pad_maximum_fusion.refs_15_
  66.6 2.8 %collective-permute-start.16 = (bf16[4,2,8,64,128]{4,3,2,1,0:T(8,128)(2,1)S(1)}, bf16[4,2,8,64,128]{4,3,2,1,0:T(8,128)(2,1)S(1)}, u32[]{:S(2)}, u32[]{:S(2)}) collective-permute-start(bf16[4,2,8,64,128]{4,3,2,1,0:T(8,128)(2,1)S(1)} %pad_maximum_fusion.refs_15_), channel_id=1, source_target_pairs={{0,24},{8,0},{16,8},{24,16},{1,25},{9,1},{17,9},{25,17},{2,26},{10... | collective-permute-start | bytes 3145736 | tf_op jit(solution)/shard_map/ppermute | solution.py:326
  69.4 0.0 collective-permute-start.15
  69.4 0.5 collective-permute-start.11
  69.9 2.1 %collective-permute-start.12 = (bf16[6,8,64,128]{3,2,1,0:T(8,128)(2,1)S(1)}, bf16[6,8,64,128]{3,2,1,0:T(8,128)(2,1)S(1)}, u32[]{:S(2)}, u32[]{:S(2)}) collective-permute-start(bf16[6,8,64,128]{3,2,1,0:T(8,128)(2,1)S(1)} %get-tuple-element.21), channel_id=1, source_target_pairs={{0,6},{1,7},{2,0},{3,1},{4,2},{5,3},{6,4},{7,5},{8,14},{9,15},{10,... | collective-permute-start | bytes 2359304 | tf_op jit(solution)/shard_map/ppermute | solution.py:323
  72.1 18.5 %collective-permute-done.16.refs_17_ = bf16[4,2,8,64,128]{4,3,2,1,0:T(8,128)(2,1)S(1)} collective-permute-done((bf16[4,2,8,64,128]{4,3,2,1,0:T(8,128)(2,1)S(1)}, bf16[4,2,8,64,128]{4,3,2,1,0:T(8,128)(2,1)S(1)}, u32[]{:S(2)}, u32[]{:S(2)}) %collective-permute-start.16) | collective-permute-done | bytes 1048608 | tf_op jit(solution)/shard_map/ppermute | solution.py:326
  90.6 3.5 %collective-permute-start.18 = (bf16[2,2,8,64,128]{4,3,2,1,0:T(8,128)(2,1)S(1)}, bf16[2,2,8,64,128]{4,3,2,1,0:T(8,128)(2,1)S(1)}, u32[]{:S(2)}, u32[]{:S(2)}) collective-permute-start(bf16[2,2,8,64,128]{4,3,2,1,0:T(8,128)(2,1)S(1)} %slice.99), channel_id=1, source_target_pairs={{0,24},{8,0},{16,8},{24,16},{1,25},{9,1},{17,9},{25,17},{2,26},{10... | collective-permute-start | bytes 1572872 | tf_op jit(solution)/shard_map/ppermute | solution.py:326
  94.1 0.0 collective-permute-done.15.refs_16_
  94.1 0.1 collective-permute-start.17
  94.2 0.0 collective-permute-done.11.refs_11_
  94.2 0.3 collective-permute-start.13
  94.5 0.0 collective-permute-done.12.refs_12_
  94.6 2.5 %collective-permute-start.14 = (bf16[3,8,64,128]{3,2,1,0:T(8,128)(2,1)S(1)}, bf16[3,8,64,128]{3,2,1,0:T(8,128)(2,1)S(1)}, u32[]{:S(2)}, u32[]{:S(2)}) collective-permute-start(bf16[3,8,64,128]{3,2,1,0:T(8,128)(2,1)S(1)} %slice.97), channel_id=1, source_target_pairs={{0,6},{1,7},{2,0},{3,1},{4,2},{5,3},{6,4},{7,5},{8,14},{9,15},{10,... | collective-permute-start | bytes 1179656 | tf_op jit(solution)/shard_map/ppermute | solution.py:323
  97.1 6.5 %collective-permute-done.13.refs_13_ = bf16[3,8,64,128]{3,2,1,0:T(8,128)(2,1)S(1)} collective-permute-done((bf16[3,8,64,128]{3,2,1,0:T(8,128)(2,1)S(1)}, bf16[3,8,64,128]{3,2,1,0:T(8,128)(2,1)S(1)}, u32[]{:S(2)}, u32[]{:S(2)}) %collective-permute-start.13) | collective-permute-done | bytes 393248 | tf_op jit(solution)/shard_map/ppermute | solution.py:323
  103.6 0.0 collective-permute-done.14.refs_14_
  103.7 0.0 collective-permute-done.18.refs_19_
  103.7 2.7 %collective-permute-done.17.refs_18_ = bf16[2,2,8,64,128]{4,3,2,1,0:T(8,128)(2,1)S(1)} collective-permute-done((bf16[2,2,8,64,128]{4,3,2,1,0:T(8,128)(2,1)S(1)}, bf16[2,2,8,64,128]{4,3,2,1,0:T(8,128)(2,1)S(1)}, u32[]{:S(2)}, u32[]{:S(2)}) %collective-permute-start.17) | collective-permute-done | bytes 524320 | tf_op jit(solution)/shard_map/ppermute | solution.py:326
  106.3 4.6 %product.1 = (f32[4,2,128,256]{3,2,1,0:T(8,128)S(1)}, f32[4,2,128,256]{3,2,1,0:T(8,128)S(1)}) custom-call(s32[4]{0:T(128)S(1)} %copy-done, bf16[8,64,128]{2,1,0:T(8,128)(2,1)S(1)} %pad_maximum_fusion.1.refs_0_, bf16[8,64,128]{2,1,0:T(8,128)(2,1)S(1)} %collective-permute-done.1.refs_1_, bf16[8,64,128]{2,1,0:T(8,128)(2,1)S(1)} %collective-permute-done.2.refs_2_, ...), custom_call_target="tpu_custom_call" | custom-call | flops 2147483648 | bytes 25165824 | tf_op jit(solution)/shard_map/product/pallas_call | solution.py:292
  110.9 3.5 %collective-permute-start.19 = (f32[4,2,128,256]{3,2,1,0:T(8,128)S(1)}, f32[4,2,128,256]{3,2,1,0:T(8,128)S(1)}, u32[]{:S(2)}, u32[]{:S(2)}) collective-permute-start(f32[4,2,128,256]{3,2,1,0:T(8,128)S(1)} %get-tuple-element.24), channel_id=1, source_target_pairs={{0,1},{1,0},{2,3},{3,2},{4,5},{5,4},{6,7},{7,6},{8,9},{9,8},{10,11... | collective-permute-start | bytes 3145736 | tf_op jit(solution)/shard_map/ppermute | solution.py:332
  114.4 2.3 %collective-permute-done.19 = f32[4,2,128,256]{3,2,1,0:T(8,128)S(1)} collective-permute-done((f32[4,2,128,256]{3,2,1,0:T(8,128)S(1)}, f32[4,2,128,256]{3,2,1,0:T(8,128)S(1)}, u32[]{:S(2)}, u32[]{:S(2)}) %collective-permute-start.19) | collective-permute-done | bytes 1048608 | tf_op jit(solution)/shard_map/ppermute | solution.py:332
  116.7 1.5 %maximum_select_fusion = f32[8,2,128,256]{3,2,1,0:T(8,128)} fusion(f32[4,2,128,256]{3,2,1,0:T(8,128)S(1)} %collective-permute-done.19, f32[4,2,128,256]{3,2,1,0:T(8,128)S(1)} %get-tuple-element.23, pred[]{:T(512)S(6)} %eq.4), kind=kLoop, calls=%fused_computation | loop fusion | flops 1572864 | bytes 4194305 | tf_op jit(solution)/shard_map/jit(_where)/select_n | solution.py:363
  (14 shorter events, 0.2 us)
Async XLA Ops:
  9.4 5.0 %collective-permute-start = (bf16[8,8,32,128]{3,2,1,0:T(8,128)(2,1)}, bf16[8,8,32,128]{3,2,1,0:T(8,128)(2,1)S(1)}, u32[]{:S(2)}, u32[]{:S(2)}) collective-permute-start(bf16[8,8,32,128]{3,2,1,0:T(8,128)(2,1)} %get-tuple-element.16), channel_id=1, source_target_pairs={{0,1},{1,0},{2,3},{3,2},{4,5},{5,4},{6,7},{7,6},{8,9},{9,8},{10,11... | collective-permute-start | bytes 1572872 | tf_op jit(solution)/shard_map/ppermute | solution.py:332
  15.5 32.9 %copy-start = (s32[4]{0:T(128)S(1)}, s32[4]{0:T(128)}, u32[]{:S(2)}) copy-start(s32[4]{0:T(128)} %pad_add_fusion.place_ref) | copy-start | bytes 52
  15.6 12.1 %collective-permute-start.1 = (bf16[8,64,128]{2,1,0:T(8,128)(2,1)S(1)}, bf16[8,64,128]{2,1,0:T(8,128)(2,1)S(1)}, u32[]{:S(2)}, u32[]{:S(2)}) collective-permute-start(bf16[8,64,128]{2,1,0:T(8,128)(2,1)S(1)} %pad_maximum_fusion.2), channel_id=1, source_target_pairs={{0,32},{32,64},{64,96},{96,128},{128,160},{160,192},{192,224},{224... | collective-permute-start | bytes 393224 | tf_op jit(solution)/shard_map/ppermute | solution.py:329
  15.7 14.4 %collective-permute-start.2 = (bf16[8,64,128]{2,1,0:T(8,128)(2,1)S(1)}, bf16[8,64,128]{2,1,0:T(8,128)(2,1)S(1)}, u32[]{:S(2)}, u32[]{:S(2)}) collective-permute-start(bf16[8,64,128]{2,1,0:T(8,128)(2,1)S(1)} %pad_maximum_fusion.3), channel_id=1, source_target_pairs={{0,64},{32,96},{64,128},{96,160},{128,192},{160,224},{192,0},{224,... | collective-permute-start | bytes 393224 | tf_op jit(solution)/shard_map/ppermute | solution.py:329
  18.7 20.5 %collective-permute-start.3 = (bf16[8,64,128]{2,1,0:T(8,128)(2,1)S(1)}, bf16[8,64,128]{2,1,0:T(8,128)(2,1)S(1)}, u32[]{:S(2)}, u32[]{:S(2)}) collective-permute-start(bf16[8,64,128]{2,1,0:T(8,128)(2,1)S(1)} %pad_maximum_fusion.4), channel_id=1, source_target_pairs={{0,96},{32,128},{64,160},{96,192},{128,224},{160,0},{192,32},{224,... | collective-permute-start | bytes 393224 | tf_op jit(solution)/shard_map/ppermute | solution.py:329
  22.5 17.2 %collective-permute-start.4 = (bf16[8,64,128]{2,1,0:T(8,128)(2,1)S(1)}, bf16[8,64,128]{2,1,0:T(8,128)(2,1)S(1)}, u32[]{:S(2)}, u32[]{:S(2)}) collective-permute-start(bf16[8,64,128]{2,1,0:T(8,128)(2,1)S(1)} %pad_maximum_fusion.5), channel_id=1, source_target_pairs={{0,128},{32,160},{64,192},{96,224},{128,0},{160,32},{192,64},{224,... | collective-permute-start | bytes 393224 | tf_op jit(solution)/shard_map/ppermute | solution.py:329
  23.1 16.6 %collective-permute-start.5 = (bf16[8,64,128]{2,1,0:T(8,128)(2,1)S(1)}, bf16[8,64,128]{2,1,0:T(8,128)(2,1)S(1)}, u32[]{:S(2)}, u32[]{:S(2)}) collective-permute-start(bf16[8,64,128]{2,1,0:T(8,128)(2,1)S(1)} %pad_maximum_fusion.6), channel_id=1, source_target_pairs={{0,160},{32,192},{64,224},{96,0},{128,32},{160,64},{192,96},{224,1... | collective-permute-start | bytes 393224 | tf_op jit(solution)/shard_map/ppermute | solution.py:329
  27.6 19.9 %collective-permute-start.6 = (bf16[8,64,128]{2,1,0:T(8,128)(2,1)S(1)}, bf16[8,64,128]{2,1,0:T(8,128)(2,1)S(1)}, u32[]{:S(2)}, u32[]{:S(2)}) collective-permute-start(bf16[8,64,128]{2,1,0:T(8,128)(2,1)S(1)} %pad_maximum_fusion.7), channel_id=1, source_target_pairs={{0,192},{32,224},{64,0},{96,32},{128,64},{160,96},{192,128},{224,1... | collective-permute-start | bytes 393224 | tf_op jit(solution)/shard_map/ppermute | solution.py:329
  30.1 18.3 %collective-permute-start.7 = (bf16[8,64,128]{2,1,0:T(8,128)(2,1)S(1)}, bf16[8,64,128]{2,1,0:T(8,128)(2,1)S(1)}, u32[]{:S(2)}, u32[]{:S(2)}) collective-permute-start(bf16[8,64,128]{2,1,0:T(8,128)(2,1)S(1)} %pad_maximum_fusion.8), channel_id=1, source_target_pairs={{0,224},{32,0},{64,32},{96,64},{128,96},{160,128},{192,160},{224,1... | collective-permute-start | bytes 393224 | tf_op jit(solution)/shard_map/ppermute | solution.py:329
  51.1 8.7 %collective-permute-start.8 = (bf16[2,8,64,128]{3,2,1,0:T(8,128)(2,1)S(1)}, bf16[2,8,64,128]{3,2,1,0:T(8,128)(2,1)S(1)}, u32[]{:S(2)}, u32[]{:S(2)}) collective-permute-start(bf16[2,8,64,128]{3,2,1,0:T(8,128)(2,1)S(1)} %get-tuple-element.17), channel_id=1, source_target_pairs={{0,2},{1,3},{2,4},{3,5},{4,6},{5,7},{6,0},{7,1},{8,10},{9,11},{10,... | collective-permute-start | bytes 786440 | tf_op jit(solution)/shard_map/ppermute | solution.py:323
  52.4 7.4 %collective-permute-start.9 = (bf16[2,8,64,128]{3,2,1,0:T(8,128)(2,1)S(1)}, bf16[2,8,64,128]{3,2,1,0:T(8,128)(2,1)S(1)}, u32[]{:S(2)}, u32[]{:S(2)}) collective-permute-start(bf16[2,8,64,128]{3,2,1,0:T(8,128)(2,1)S(1)} %get-tuple-element.18), channel_id=1, source_target_pairs={{0,6},{1,7},{2,0},{3,1},{4,2},{5,3},{6,4},{7,5},{8,14},{9,15},{10,... | collective-permute-start | bytes 786440 | tf_op jit(solution)/shard_map/ppermute | solution.py:323
  53.9 12.6 %collective-permute-start.10 = (bf16[2,8,64,128]{3,2,1,0:T(8,128)(2,1)S(1)}, bf16[2,8,64,128]{3,2,1,0:T(8,128)(2,1)S(1)}, u32[]{:S(2)}, u32[]{:S(2)}) collective-permute-start(bf16[2,8,64,128]{3,2,1,0:T(8,128)(2,1)S(1)} %get-tuple-element.19), channel_id=1, source_target_pairs={{0,4},{1,5},{2,6},{3,7},{4,0},{5,1},{6,2},{7,3},{8,12},{9,13},{10,... | collective-permute-start | bytes 786440 | tf_op jit(solution)/shard_map/ppermute | solution.py:323
  66.6 24.0 %collective-permute-start.16 = (bf16[4,2,8,64,128]{4,3,2,1,0:T(8,128)(2,1)S(1)}, bf16[4,2,8,64,128]{4,3,2,1,0:T(8,128)(2,1)S(1)}, u32[]{:S(2)}, u32[]{:S(2)}) collective-permute-start(bf16[4,2,8,64,128]{4,3,2,1,0:T(8,128)(2,1)S(1)} %pad_maximum_fusion.refs_15_), channel_id=1, source_target_pairs={{0,24},{8,0},{16,8},{24,16},{1,25},{9,1},{17,9},{25,17},{2,26},{10... | collective-permute-start | bytes 3145736 | tf_op jit(solution)/shard_map/ppermute | solution.py:326
  69.4 24.7 %collective-permute-start.15 = (bf16[4,2,8,64,128]{4,3,2,1,0:T(8,128)(2,1)S(1)}, bf16[4,2,8,64,128]{4,3,2,1,0:T(8,128)(2,1)S(1)}, u32[]{:S(2)}, u32[]{:S(2)}) collective-permute-start(bf16[4,2,8,64,128]{4,3,2,1,0:T(8,128)(2,1)S(1)} %pad_maximum_fusion.refs_15_), channel_id=1, source_target_pairs={{0,8},{8,16},{16,24},{24,0},{1,9},{9,17},{17,25},{25,1},{2,10},{10... | collective-permute-start | bytes 3145736 | tf_op jit(solution)/shard_map/ppermute | solution.py:326
  69.4 24.8 %collective-permute-start.11 = (bf16[6,8,64,128]{3,2,1,0:T(8,128)(2,1)S(1)}, bf16[6,8,64,128]{3,2,1,0:T(8,128)(2,1)S(1)}, u32[]{:S(2)}, u32[]{:S(2)}) collective-permute-start(bf16[6,8,64,128]{3,2,1,0:T(8,128)(2,1)S(1)} %get-tuple-element.20), channel_id=1, source_target_pairs={{0,2},{1,3},{2,4},{3,5},{4,6},{5,7},{6,0},{7,1},{8,10},{9,11},{10,... | collective-permute-start | bytes 2359304 | tf_op jit(solution)/shard_map/ppermute | solution.py:323
  69.9 24.6 %collective-permute-start.12 = (bf16[6,8,64,128]{3,2,1,0:T(8,128)(2,1)S(1)}, bf16[6,8,64,128]{3,2,1,0:T(8,128)(2,1)S(1)}, u32[]{:S(2)}, u32[]{:S(2)}) collective-permute-start(bf16[6,8,64,128]{3,2,1,0:T(8,128)(2,1)S(1)} %get-tuple-element.21), channel_id=1, source_target_pairs={{0,6},{1,7},{2,0},{3,1},{4,2},{5,3},{6,4},{7,5},{8,14},{9,15},{10,... | collective-permute-start | bytes 2359304 | tf_op jit(solution)/shard_map/ppermute | solution.py:323
  90.6 13.1 %collective-permute-start.18 = (bf16[2,2,8,64,128]{4,3,2,1,0:T(8,128)(2,1)S(1)}, bf16[2,2,8,64,128]{4,3,2,1,0:T(8,128)(2,1)S(1)}, u32[]{:S(2)}, u32[]{:S(2)}) collective-permute-start(bf16[2,2,8,64,128]{4,3,2,1,0:T(8,128)(2,1)S(1)} %slice.99), channel_id=1, source_target_pairs={{0,24},{8,0},{16,8},{24,16},{1,25},{9,1},{17,9},{25,17},{2,26},{10... | collective-permute-start | bytes 1572872 | tf_op jit(solution)/shard_map/ppermute | solution.py:326
  94.1 12.2 %collective-permute-start.17 = (bf16[2,2,8,64,128]{4,3,2,1,0:T(8,128)(2,1)S(1)}, bf16[2,2,8,64,128]{4,3,2,1,0:T(8,128)(2,1)S(1)}, u32[]{:S(2)}, u32[]{:S(2)}) collective-permute-start(bf16[2,2,8,64,128]{4,3,2,1,0:T(8,128)(2,1)S(1)} %slice.98), channel_id=1, source_target_pairs={{0,8},{8,16},{16,24},{24,0},{1,9},{9,17},{17,25},{25,1},{2,10},{10... | collective-permute-start | bytes 1572872 | tf_op jit(solution)/shard_map/ppermute | solution.py:326
  94.2 9.4 %collective-permute-start.13 = (bf16[3,8,64,128]{3,2,1,0:T(8,128)(2,1)S(1)}, bf16[3,8,64,128]{3,2,1,0:T(8,128)(2,1)S(1)}, u32[]{:S(2)}, u32[]{:S(2)}) collective-permute-start(bf16[3,8,64,128]{3,2,1,0:T(8,128)(2,1)S(1)} %slice.96), channel_id=1, source_target_pairs={{0,2},{1,3},{2,4},{3,5},{4,6},{5,7},{6,0},{7,1},{8,10},{9,11},{10,... | collective-permute-start | bytes 1179656 | tf_op jit(solution)/shard_map/ppermute | solution.py:323
  94.6 9.1 %collective-permute-start.14 = (bf16[3,8,64,128]{3,2,1,0:T(8,128)(2,1)S(1)}, bf16[3,8,64,128]{3,2,1,0:T(8,128)(2,1)S(1)}, u32[]{:S(2)}, u32[]{:S(2)}) collective-permute-start(bf16[3,8,64,128]{3,2,1,0:T(8,128)(2,1)S(1)} %slice.97), channel_id=1, source_target_pairs={{0,6},{1,7},{2,0},{3,1},{4,2},{5,3},{6,4},{7,5},{8,14},{9,15},{10,... | collective-permute-start | bytes 1179656 | tf_op jit(solution)/shard_map/ppermute | solution.py:323
  110.9 5.8 %collective-permute-start.19 = (f32[4,2,128,256]{3,2,1,0:T(8,128)S(1)}, f32[4,2,128,256]{3,2,1,0:T(8,128)S(1)}, u32[]{:S(2)}, u32[]{:S(2)}) collective-permute-start(f32[4,2,128,256]{3,2,1,0:T(8,128)S(1)} %get-tuple-element.24), channel_id=1, source_target_pairs={{0,1},{1,0},{2,3},{3,2},{4,5},{5,4},{6,7},{7,6},{8,9},{9,8},{10,11... | collective-permute-start | bytes 3145736 | tf_op jit(solution)/shard_map/ppermute | solution.py:332

commit v2 on v1

--- a/solution.py
+++ b/solution.py
@@ -9,6 +9,7 @@
 from jax.sharding import PartitionSpec as P
 
 CHUNKS = 1
+ZORDER = (3, 5, 4, 2, 6, 1, 7, 0)
 VMEM_LIMIT = 56 * 1024 * 1024
 
 
@@ -140,71 +141,102 @@
 
 def sort_kernel(place_ref, *refs):
     pieces = refs[:8]
-    own, up_turn, down_turn, far_turn, up, down, held, sems = refs[8:]
-    plane, chip = place_ref[0], place_ref[2]
-
-    def start(copies):
-        for copy in copies:
-            copy.start()
-        for copy in copies:
-            copy.wait()
-
-    start(
-        [
-            pltpu.make_async_copy(
-                piece, held.at[lax.rem(plane - hop - 2 * chip + 16, 8)], sems.at[hop]
-            )
-            for hop, piece in enumerate(pieces)
-        ]
-    )
-    moves = [
-        (0, 2, own, 0),
-        (2, 2, up_turn, 0),
-        (6, 2, down_turn, 0),
-        (4, 2, far_turn, 0),
-    ]
+    held = refs[8]
+    turns = refs[9:]
+    first = place_ref[0] - 2 * place_ref[2] + 8
+    for hop, piece in zip(ZORDER, pieces):
+        held[lax.rem(first - hop + 8, 8)] = piece[...]
+    for pair, turn in enumerate(turns):
+        turn[...] = held[2 * pair : 2 * pair + 2]
+
+
+def sort_blocks(place, pieces):
+    shape = pieces[0].shape
+    two = jax.ShapeDtypeStruct((2,) + shape, jnp.bfloat16)
+    eight = jax.ShapeDtypeStruct((8,) + shape, jnp.bfloat16)
+    vmem = pl.BlockSpec(memory_space=pltpu.VMEM)
+    return pl.pallas_call(
+        sort_kernel,
+        out_shape=[eight, two, two, two, two],
+        in_specs=[pl.BlockSpec(memory_space=pltpu.SMEM)] + [vmem] * 8,
+        out_specs=[vmem] * 5,
+        compiler_params=pltpu.CompilerParams(vmem_limit_bytes=16 * 1024 * 1024),
+        cost_estimate=pl.CostEstimate(flops=0, bytes_accessed=1 << 20, transcendentals=0),
+        name="sort",
+    )(place, *[pieces[hop] for hop in ZORDER])
+
+
+def second_kernel(held, up_turn, down_turn, far_turn, after_up, after_down, up, down, turned):
+    del after_up, after_down
     for target, order in ((up, UP), (down, DOWN)):
         at = 0
         for first, size in order:
-            moves.append((first, size, target, at))
+            target[at : at + size] = held[first : first + size]
             at += size
-    start(
-        [
-            pltpu.make_async_copy(
-                held.at[pl.ds(first, size)], target.at[pl.ds(at, size)], sems.at[number]
-            )
-            for number, (first, size, target, at) in enumerate(moves)
-        ]
-    )
-
-
-def sort_blocks(place, pieces):
-    shape = pieces[0].shape
-    two = jax.ShapeDtypeStruct((2,) + shape, jnp.bfloat16)
-    six = jax.ShapeDtypeStruct((6,) + shape, jnp.bfloat16)
+    for at, turn in enumerate((up_turn, down_turn, far_turn)):
+        turned[at] = turn[...]
+
+
+def second_step(held, turns, after):
+    block = held.shape[1:]
+    six = jax.ShapeDtypeStruct((6,) + block, jnp.bfloat16)
+    turned = jax.ShapeDtypeStruct((3, 2) + block, jnp.bfloat16)
+    vmem = pl.BlockSpec(memory_space=pltpu.VMEM)
     hbm = pl.BlockSpec(memory_space=pl.ANY)
     return pl.pallas_call(
-        sort_kernel,
-        out_shape=[two, two, two, two, six, six],
-        in_specs=[pl.BlockSpec(memory_space=pltpu.SMEM)] + [hbm] * 8,
-        out_specs=[hbm] * 6,
-        scratch_shapes=[
-            pltpu.VMEM((8,) + shape, jnp.bfloat16),
-            pltpu.SemaphoreType.DMA((10,)),
-        ],
-        compiler_params=pltpu.CompilerParams(vmem_limit_bytes=4 * 1024 * 1024),
-        cost_estimate=pl.CostEstimate(flops=0, bytes_accessed=4 << 20, transcendentals=0),
-        name="sort",
-    )(place, *pieces)
+        second_kernel,
+        out_shape=[six, six, turned],
+        in_specs=[vmem] * 4 + [hbm] * 2,
+        out_specs=[vmem] * 3,
+        compiler_params=pltpu.CompilerParams(vmem_limit_bytes=16 * 1024 * 1024),
+        cost_estimate=pl.CostEstimate(flops=0, bytes_accessed=1 << 20, transcendentals=0),
+        name="second",
+    )(held, *turns, *after)
+
+
+def third_kernel(y_up, y_down, own_down, x_up, x_down, y_up_far, y_down_far, x_up_far, x_down_far):
+    y_up_far[...] = y_up[:2]
+    y_down_far[0] = own_down[...]
+    y_down_far[1] = y_down[2]
+    x_up_far[...] = x_up[:3]
+    x_down_far[...] = x_down[:3]
+
+
+def third_step(y_up, y_down, own_down, x_up, x_down):
+    block = x_up.shape[1:]
+    two = jax.ShapeDtypeStruct((2, 2) + block, jnp.bfloat16)
+    three = jax.ShapeDtypeStruct((3,) + block, jnp.bfloat16)
+    vmem = pl.BlockSpec(memory_space=pltpu.VMEM)
+    return pl.pallas_call(
+        third_kernel,
+        out_shape=[two, two, three, three],
+        in_specs=[vmem] * 5,
+        out_specs=[vmem] * 4,
+        compiler_params=pltpu.CompilerParams(vmem_limit_bytes=16 * 1024 * 1024),
+        cost_estimate=pl.CostEstimate(flops=0, bytes_accessed=1 << 20, transcendentals=0),
+        name="third",
+    )(y_up, y_down, own_down, x_up, x_down)
+
+
+LEFTS = (
+    (2, (1, 2)),
+    (2, (0, 3)),
+    (3, (1, 2, 3)),
+    (1, (1, 2, 3)),
+    (3, (0,)),
+    (1, (0,)),
+    (0, (0,)),
+    (0, (1, 2, 3)),
+)
 
 
 def product_kernel(place_ref, *refs, bands):
-    pieces = refs[:8]
-    up_turn, down_turn, far_turn, up, down, up_far, down_far = refs[8:15]
-    left_own, left_up, left_down, left_up_far, left_down_far = refs[15:20]
-    keep_ref, give_ref, right, left, sems = refs[20:]
+    lefts = refs[: len(LEFTS)]
+    turned = refs[len(LEFTS) - 1]
+    held, up, down, up_far, down_far = refs[len(LEFTS) : -5]
+    keep_ref, give_ref, right, left, sems = refs[-5:]
     plane, core, chip, column = (place_ref[i] for i in range(4))
-    width = pieces[0].shape[1]
+    width = held.shape[2]
     copies = []
 
     def copy(source, target):
@@ -215,17 +247,12 @@
         start = pl.multiple_of(target_chip * width, width)
         copy(source, right.at[pl.ds(block, size), :, pl.ds(start, width), :])
 
-    for hop, piece in enumerate(pieces):
-        copy(
-            piece,
-            right.at[
-                lax.rem(plane - hop + 8, 8), :, pl.ds(pl.multiple_of(chip * width, width), width), :
-            ],
-        )
+    for pair in range(4):
+        into_right(held.at[pl.ds(2 * pair, 2)], 2 * pair, 2, chip)
     below, above, across = lax.rem(chip + 3, 4), lax.rem(chip + 1, 4), lax.rem(chip + 2, 4)
-    into_right(up_turn, 2, 2, below)
-    into_right(down_turn, 6, 2, above)
-    into_right(far_turn, 4, 2, across)
+    into_right(turned.at[0], 2, 2, below)
+    into_right(turned.at[1], 6, 2, above)
+    into_right(turned.at[2], 4, 2, across)
     for source, order, target_chip in ((up, UP, below), (down, DOWN, above)):
         at = 0
         for first, size in order:
@@ -241,19 +268,11 @@
                 into_right(source.at[pl.ds(at, step)], first, step, across)
                 at, first, size = at + step, first + step, size - step
     chips = (chip, below, above, across)
-    for source, slots, hop in (
-        (left_own, range(4), 0),
-        (left_up, range(4), 3),
-        (left_down, range(4), 1),
-        (left_up_far, range(2), 2),
-        (left_down_far, range(2, 4), 2),
-    ):
+    for source, (hop, slots) in zip(lefts, LEFTS):
         for at, slot in enumerate(slots):
             start = lax.rem(column + hop, 4) * 4 * width + chips[slot] * width
-            copy(
-                source.at[at],
-                left.at[:, :, pl.ds(pl.multiple_of(start, width), width), :],
-            )
+            target = left.at[:, :, pl.ds(pl.multiple_of(start, width), width), :]
+            copy(source.at[at] if len(slots) > 1 else source, target)
     for one in copies:
         one.start()
     for one in copies:
@@ -283,8 +302,8 @@
             give_ref[band, part] = jnp.where(core == 0, high, low)
 
 
-def product(place, pieces, rest):
-    parts, width, shots = pieces[0].shape
+def product(place, lefts, rights):
+    parts, width, shots = rights[0].shape[1:]
     bands = parts // 2
     receivers = 4 * width
     hbm = pl.BlockSpec(memory_space=pl.ANY)
@@ -292,7 +311,7 @@
     return pl.pallas_call(
         functools.partial(product_kernel, bands=bands),
         out_shape=[out, out],
-        in_specs=[pl.BlockSpec(memory_space=pltpu.SMEM)] + [hbm] * 20,
+        in_specs=[pl.BlockSpec(memory_space=pltpu.SMEM)] + [hbm] * (len(lefts) + len(rights)),
         scratch_shapes=[
             pltpu.VMEM((8, parts, receivers, shots), jnp.bfloat16),
             pltpu.VMEM((2, parts, 4 * receivers, shots), jnp.bfloat16),
@@ -305,7 +324,7 @@
             transcendentals=0,
         ),
         name="product",
-    )(place, *pieces, *rest)
+    )(place, *lefts, *rights)
 
 
 def local(traces, ghost_filter, bands):
@@ -337,26 +356,31 @@
         theirs = swap(others[chunk])
         low = jnp.where(core == 0, own, theirs)
         high = jnp.where(core == 0, theirs, own)
-        pieces = []
-        for hop in range(planes):
+        pieces = [None] * planes
+        for hop in ZORDER:
             piece = jnp.concatenate([low[hop], high[hop]], 1)
-            pieces.append(along_z(piece, hop) if hop else piece)
-        own_turn, up_turn, down_turn, far_turn, up, down = sort_blocks(place, pieces)
+            pieces[hop] = along_z(piece, hop) if hop else piece
+        held, own_turn, up_turn, far_turn, down_turn = sort_blocks(place, pieces)
+        own_up, own_down = along_y(own_turn, 1), along_y(own_turn, -1)
         up_turn, down_turn, far_turn = (
             along_x(up_turn, 1),
             along_x(down_turn, -1),
             along_x(far_turn, 2),
         )
+        up, down, turned = second_step(
+            held, (up_turn, down_turn, far_turn), (own_up, own_down)
+        )
+        y_up, y_down = along_y(turned, 1), along_y(turned, -1)
         up, down = along_x(up, 1), along_x(down, -1)
-        up_far, down_far = along_x(up[:3], 1), along_x(down[:3], -1)
-        left = jnp.stack([own_turn, up_turn, down_turn, far_turn])
-        left_up, left_down = along_y(left, 1), along_y(left, -1)
-        left_up_far, left_down_far = along_y(left_up[:2], 1), along_y(left_down[2:], -1)
+        y_up_far, y_down_far, x_up_far, x_down_far = third_step(
+            y_up, y_down, own_down, up, down
+        )
+        y_up_far, y_down_far = along_y(y_up_far, 1), along_y(y_down_far, -1)
+        x_up_far, x_down_far = along_x(x_up_far, 1), along_x(x_down_far, -1)
         keep, give = product(
             place,
-            pieces,
-            (up_turn, down_turn, far_turn, up, down, up_far, down_far)
-            + (left, left_up, left_down, left_up_far, left_down_far),
+            (y_up_far, y_down_far, y_up, y_down, own_up, own_down, own_turn, turned),
+            (held, up, down, x_up_far, x_down_far),
         )
         keeps.append(keep)
         takes.append(swap(give))

time: 119 us -> 108 us (0.908)
  waiting for transfers between devices: 60.2 us -> 47.4 us
  starting transfers between devices: 38.2 us -> 42.5 us
  Pallas kernels: 16 us -> 14.2 us
    ppermute x4 -> x6, waiting for transfers between devices: 21.2 us -> 5.16 us  [along_y(): return lax.ppermute(value, 'rx', [(i, (i + hop) % 4) for i in range(4)])]
    ppermute x7, waiting for transfers between devices: 17.6 us -> 25.8 us  [along_x(): return lax.ppermute(value, 'ry', pairs)]
    ppermute x7, waiting for transfers between devices: 17.5 us -> 12.4 us  [along_z(): lax.ppermute(value, 'shot', [(i, (i + hop) % planes) for i in range(plane...]
    ppermute x4 -> x6, starting transfers between devices: 6.38 us -> 8.24 us  [along_y(): return lax.ppermute(value, 'rx', [(i, (i + hop) % 4) for i in range(4)])]
    pallas_call x1 -> x3, Pallas kernels: 2.67 us -> 0.97 us  [the longest x1 0.68 us: sort_blocks(): pl.pallas_call(sort_kernel, out_shape=[eight, two, two, two, two], in_spe...]
    ppermute x2, starting transfers between devices: 6.74 us -> 8.12 us  [swap(): return lax.ppermute(value, 'ry', [(i, i ^ 1) for i in range(8)])]
  transfers between devices with their start and end apart: 20 -> 22, of which waited for: 11 -> 14; matrix products, arithmetic and copies ran while one was open for 0% -> 0% of each run, Pallas kernels for 0% -> 0%
where the time goes in v2:
time: 108 us
  waiting for transfers between devices  47.4 us (44%)
  starting transfers between devices  42.5 us (39%)
  Pallas kernels  14.2 us (13%)
  other arithmetic  3.29 us (3%)
    ppermute x7, waiting for transfers between devices, along_x(): return lax.ppermute(value, 'ry', pairs)  25.8 us
    ppermute x7, starting transfers between devices, along_z(): lax.ppermute(value, 'shot', [(i, (i + hop) % planes) for i in range(plane...  16.4 us
    ppermute x7, waiting for transfers between devices, along_z(): lax.ppermute(value, 'shot', [(i, (i + hop) % planes) for i in range(plane...  12.4 us
    ppermute x7, starting transfers between devices, along_x(): return lax.ppermute(value, 'ry', pairs)  9.71 us
    pallas_call x1, Pallas kernels, front(): pl.pallas_call(functools.partial(front_kernel, chunks=chunks, planes=plan...  8.72 us
    ppermute x6, starting transfers between devices, along_y(): return lax.ppermute(value, 'rx', [(i, (i + hop) % 4) for i in range(4)])  8.24 us
    ppermute x2, starting transfers between devices, swap(): return lax.ppermute(value, 'ry', [(i, i ^ 1) for i in range(8)])  8.12 us
    ppermute x6, waiting for transfers between devices, along_y(): return lax.ppermute(value, 'rx', [(i, (i + hop) % 4) for i in range(4)])  5.16 us
  transfers between devices with their start and end apart: 22, of which 14 were waited for; matrix products, arithmetic and copies ran while one was open for 0% of the time, Pallas kernels for 0%

profile of v2, /device:TPU:1, one launch (start us, length us, event | category | flops | bytes accessed | tf_op | source)
XLA Modules:
  0.0 107.5 jit_solution(12402484832102219737)
XLA Ops:
  0.0 0.6 pad_add_fusion.place_ref
  0.6 8.7 %front.1 = (bf16[8,8,32,128]{3,2,1,0:T(8,128)(2,1)}, bf16[8,8,32,128]{3,2,1,0:T(8,128)(2,1)}) custom-call(s32[4]{0:T(128)} %pad_add_fusion.place_ref, bf16[1,64]{1,0:T(2,128)(2,1)} %bitcast.38, s32[1,64]{1,0:T(1,128)} %bitcast.39, bf16[128,32,1024]{2,1,0:T(8,128)(2,1)} %traces_ref.1), custom_call_target="tpu_custom_call" | custom-call | flops 2147483648 | bytes 8388608 | tf_op jit(solution)/shard_map/front/pallas_call | solution.py:109
  9.3 3.2 %collective-permute-start = (bf16[8,8,32,128]{3,2,1,0:T(8,128)(2,1)}, bf16[8,8,32,128]{3,2,1,0:T(8,128)(2,1)S(1)}, u32[]{:S(2)}, u32[]{:S(2)}) collective-permute-start(bf16[8,8,32,128]{3,2,1,0:T(8,128)(2,1)} %get-tuple-element.22), channel_id=1, source_target_pairs={{0,1},{1,0},{2,3},{3,2},{4,5},{5,4},{6,7},{7,6},{8,9},{9,8},{10,11... | collective-permute-start | bytes 1572872 | tf_op jit(solution)/shard_map/ppermute | solution.py:351
  12.6 1.7 %collective-permute-done = bf16[8,8,32,128]{3,2,1,0:T(8,128)(2,1)S(1)} collective-permute-done((bf16[8,8,32,128]{3,2,1,0:T(8,128)(2,1)}, bf16[8,8,32,128]{3,2,1,0:T(8,128)(2,1)S(1)}, u32[]{:S(2)}, u32[]{:S(2)}) %collective-permute-start) | collective-permute-done | bytes 524320 | tf_op jit(solution)/shard_map/ppermute | solution.py:351
  14.3 1.1 %broadcast_select_fusion.1 = (bf16[8,8,32,128]{3,2,1,0:T(8,128)(2,1)S(1)}, bf16[8,8,32,128]{3,2,1,0:T(8,128)(2,1)S(1)}) fusion(bf16[8,8,32,128]{3,2,1,0:T(8,128)(2,1)} %get-tuple-element.21, bf16[8,8,32,128]{3,2,1,0:T(8,128)(2,1)S(1)} %collective-permute-done, pred[]{:T(512)S(6)} %eq.4), kind=kLoop, calls=%fused_computation.2 | loop fusion | flops 524288 | bytes 2097153 | tf_op jit(solution)/shard_map/jit(_where)/select_n | solution.py:357
  15.4 0.1 slice_bitcast_fusion
  15.5 2.7 %collective-permute-start.1 = (bf16[8,64,128]{2,1,0:T(8,128)(2,1)S(1)}, bf16[8,64,128]{2,1,0:T(8,128)(2,1)S(1)}, u32[]{:S(2)}, u32[]{:S(2)}) collective-permute-start(bf16[8,64,128]{2,1,0:T(8,128)(2,1)S(1)} %pad_maximum_fusion), channel_id=1, source_target_pairs={{0,96},{32,128},{64,160},{96,192},{128,224},{160,0},{192,32},{224,... | collective-permute-start | bytes 393224 | tf_op jit(solution)/shard_map/ppermute | solution.py:348
  18.2 2.2 %collective-permute-start.2 = (bf16[8,64,128]{2,1,0:T(8,128)(2,1)S(1)}, bf16[8,64,128]{2,1,0:T(8,128)(2,1)S(1)}, u32[]{:S(2)}, u32[]{:S(2)}) collective-permute-start(bf16[8,64,128]{2,1,0:T(8,128)(2,1)S(1)} %pad_maximum_fusion.1), channel_id=1, source_target_pairs={{0,160},{32,192},{64,224},{96,0},{128,32},{160,64},{192,96},{224,1... | collective-permute-start | bytes 393224 | tf_op jit(solution)/shard_map/ppermute | solution.py:348
  20.5 5.0 %collective-permute-start.3 = (bf16[8,64,128]{2,1,0:T(8,128)(2,1)S(1)}, bf16[8,64,128]{2,1,0:T(8,128)(2,1)S(1)}, u32[]{:S(2)}, u32[]{:S(2)}) collective-permute-start(bf16[8,64,128]{2,1,0:T(8,128)(2,1)S(1)} %pad_maximum_fusion.2), channel_id=1, source_target_pairs={{0,128},{32,160},{64,192},{96,224},{128,0},{160,32},{192,64},{224,... | collective-permute-start | bytes 393224 | tf_op jit(solution)/shard_map/ppermute | solution.py:348
  25.5 1.3 %collective-permute-start.4 = (bf16[8,64,128]{2,1,0:T(8,128)(2,1)S(1)}, bf16[8,64,128]{2,1,0:T(8,128)(2,1)S(1)}, u32[]{:S(2)}, u32[]{:S(2)}) collective-permute-start(bf16[8,64,128]{2,1,0:T(8,128)(2,1)S(1)} %pad_maximum_fusion.3), channel_id=1, source_target_pairs={{0,64},{32,96},{64,128},{96,160},{128,192},{160,224},{192,0},{224,... | collective-permute-start | bytes 393224 | tf_op jit(solution)/shard_map/ppermute | solution.py:348
  26.7 2.5 %collective-permute-start.5 = (bf16[8,64,128]{2,1,0:T(8,128)(2,1)S(1)}, bf16[8,64,128]{2,1,0:T(8,128)(2,1)S(1)}, u32[]{:S(2)}, u32[]{:S(2)}) collective-permute-start(bf16[8,64,128]{2,1,0:T(8,128)(2,1)S(1)} %pad_maximum_fusion.4), channel_id=1, source_target_pairs={{0,192},{32,224},{64,0},{96,32},{128,64},{160,96},{192,128},{224,1... | collective-permute-start | bytes 393224 | tf_op jit(solution)/shard_map/ppermute | solution.py:348
  29.2 0.0 collective-permute-done.1.refs_0_
  29.2 0.8 collective-permute-start.6
  30.1 0.0 collective-permute-done.2.refs_1_
  30.1 2.0 %collective-permute-start.7 = (bf16[8,64,128]{2,1,0:T(8,128)(2,1)S(1)}, bf16[8,64,128]{2,1,0:T(8,128)(2,1)S(1)}, u32[]{:S(2)}, u32[]{:S(2)}) collective-permute-start(bf16[8,64,128]{2,1,0:T(8,128)(2,1)S(1)} %pad_maximum_fusion.6), channel_id=1, source_target_pairs={{0,224},{32,0},{64,32},{96,64},{128,96},{160,128},{192,160},{224,1... | collective-permute-start | bytes 393224 | tf_op jit(solution)/shard_map/ppermute | solution.py:348
  32.1 2.7 %collective-permute-done.3.refs_2_ = bf16[8,64,128]{2,1,0:T(8,128)(2,1)S(1)} collective-permute-done((bf16[8,64,128]{2,1,0:T(8,128)(2,1)S(1)}, bf16[8,64,128]{2,1,0:T(8,128)(2,1)S(1)}, u32[]{:S(2)}, u32[]{:S(2)}) %collective-permute-start.3) | collective-permute-done | bytes 131104 | tf_op jit(solution)/shard_map/ppermute | solution.py:348
  34.8 5.6 %collective-permute-done.4.refs_3_ = bf16[8,64,128]{2,1,0:T(8,128)(2,1)S(1)} collective-permute-done((bf16[8,64,128]{2,1,0:T(8,128)(2,1)S(1)}, bf16[8,64,128]{2,1,0:T(8,128)(2,1)S(1)}, u32[]{:S(2)}, u32[]{:S(2)}) %collective-permute-start.4) | collective-permute-done | bytes 131104 | tf_op jit(solution)/shard_map/ppermute | solution.py:348
  40.4 1.9 %collective-permute-done.5.refs_4_ = bf16[8,64,128]{2,1,0:T(8,128)(2,1)S(1)} collective-permute-done((bf16[8,64,128]{2,1,0:T(8,128)(2,1)S(1)}, bf16[8,64,128]{2,1,0:T(8,128)(2,1)S(1)}, u32[]{:S(2)}, u32[]{:S(2)}) %collective-permute-start.5) | collective-permute-done | bytes 131104 | tf_op jit(solution)/shard_map/ppermute | solution.py:348
  42.3 0.3 collective-permute-done.6.refs_5_
  42.7 1.8 %collective-permute-done.7.refs_6_ = bf16[8,64,128]{2,1,0:T(8,128)(2,1)S(1)} collective-permute-done((bf16[8,64,128]{2,1,0:T(8,128)(2,1)S(1)}, bf16[8,64,128]{2,1,0:T(8,128)(2,1)S(1)}, u32[]{:S(2)}, u32[]{:S(2)}) %collective-permute-start.7) | collective-permute-done | bytes 131104 | tf_op jit(solution)/shard_map/ppermute | solution.py:348
  44.4 0.7 sort.1
  45.1 1.3 %collective-permute-start.8 = (bf16[2,8,64,128]{3,2,1,0:T(8,128)(2,1)S(1)}, bf16[2,8,64,128]{3,2,1,0:T(8,128)(2,1)S(1)}, u32[]{:S(2)}, u32[]{:S(2)}) collective-permute-start(bf16[2,8,64,128]{3,2,1,0:T(8,128)(2,1)S(1)} %get-tuple-element.24), channel_id=1, source_target_pairs={{0,2},{1,3},{2,4},{3,5},{4,6},{5,7},{6,0},{7,1},{8,10},{9,11},{10,... | collective-permute-start | bytes 786440 | tf_op jit(solution)/shard_map/ppermute | solution.py:342
  46.4 1.5 %collective-permute-start.9 = (bf16[2,8,64,128]{3,2,1,0:T(8,128)(2,1)S(1)}, bf16[2,8,64,128]{3,2,1,0:T(8,128)(2,1)S(1)}, u32[]{:S(2)}, u32[]{:S(2)}) collective-permute-start(bf16[2,8,64,128]{3,2,1,0:T(8,128)(2,1)S(1)} %get-tuple-element.25), channel_id=1, source_target_pairs={{0,6},{1,7},{2,0},{3,1},{4,2},{5,3},{6,4},{7,5},{8,14},{9,15},{10,... | collective-permute-start | bytes 786440 | tf_op jit(solution)/shard_map/ppermute | solution.py:342
  47.9 1.5 %collective-permute-start.10 = (bf16[2,8,64,128]{3,2,1,0:T(8,128)(2,1)S(1)}, bf16[2,8,64,128]{3,2,1,0:T(8,128)(2,1)S(1)}, u32[]{:S(2)}, u32[]{:S(2)}) collective-permute-start(bf16[2,8,64,128]{3,2,1,0:T(8,128)(2,1)S(1)} %get-tuple-element.26), channel_id=1, source_target_pairs={{0,4},{1,5},{2,6},{3,7},{4,0},{5,1},{6,2},{7,3},{8,12},{9,13},{10,... | collective-permute-start | bytes 786440 | tf_op jit(solution)/shard_map/ppermute | solution.py:342
  49.4 2.7 %collective-permute-start.12 = (bf16[2,8,64,128]{3,2,1,0:T(8,128)(2,1)S(1)}, bf16[2,8,64,128]{3,2,1,0:T(8,128)(2,1)S(1)}, u32[]{:S(2)}, u32[]{:S(2)}) collective-permute-start(bf16[2,8,64,128]{3,2,1,0:T(8,128)(2,1)S(1)} %get-tuple-element.27.refs_6_), channel_id=1, source_target_pairs={{0,24},{8,0},{16,8},{24,16},{1,25},{9,1},{17,9},{25,17},{2,26},{10... | collective-permute-start | bytes 786440 | tf_op jit(solution)/shard_map/ppermute | solution.py:345
  52.1 0.0 collective-permute-start.11
  52.1 1.2 %collective-permute-done.8.up_turn = bf16[2,8,64,128]{3,2,1,0:T(8,128)(2,1)S(1)} collective-permute-done((bf16[2,8,64,128]{3,2,1,0:T(8,128)(2,1)S(1)}, bf16[2,8,64,128]{3,2,1,0:T(8,128)(2,1)S(1)}, u32[]{:S(2)}, u32[]{:S(2)}) %collective-permute-start.8) | collective-permute-done | bytes 262176 | tf_op jit(solution)/shard_map/ppermute | solution.py:342
  53.3 0.0 collective-permute-done.9.down_turn
  53.3 6.6 %collective-permute-done.10.far_turn = bf16[2,8,64,128]{3,2,1,0:T(8,128)(2,1)S(1)} collective-permute-done((bf16[2,8,64,128]{3,2,1,0:T(8,128)(2,1)S(1)}, bf16[2,8,64,128]{3,2,1,0:T(8,128)(2,1)S(1)}, u32[]{:S(2)}, u32[]{:S(2)}) %collective-permute-start.10) | collective-permute-done | bytes 262176 | tf_op jit(solution)/shard_map/ppermute | solution.py:342
  59.9 0.2 second.1
  60.1 0.6 collective-permute-start.15
  60.7 2.1 %collective-permute-start.16 = (bf16[6,8,64,128]{3,2,1,0:T(8,128)(2,1)S(1)}, bf16[6,8,64,128]{3,2,1,0:T(8,128)(2,1)S(1)}, u32[]{:S(2)}, u32[]{:S(2)}) collective-permute-start(bf16[6,8,64,128]{3,2,1,0:T(8,128)(2,1)S(1)} %get-tuple-element.30), channel_id=1, source_target_pairs={{0,6},{1,7},{2,0},{3,1},{4,2},{5,3},{6,4},{7,5},{8,14},{9,15},{10,... | collective-permute-start | bytes 2359304 | tf_op jit(solution)/shard_map/ppermute | solution.py:342
  62.8 2.7 %collective-permute-start.14 = (bf16[3,2,8,64,128]{4,3,2,1,0:T(8,128)(2,1)S(1)}, bf16[3,2,8,64,128]{4,3,2,1,0:T(8,128)(2,1)S(1)}, u32[]{:S(2)}, u32[]{:S(2)}) collective-permute-start(bf16[3,2,8,64,128]{4,3,2,1,0:T(8,128)(2,1)S(1)} %get-tuple-element.28.refs_7_), channel_id=1, source_target_pairs={{0,24},{8,0},{16,8},{24,16},{1,25},{9,1},{17,9},{25,17},{2,26},{10... | collective-permute-start | bytes 2359304 | tf_op jit(solution)/shard_map/ppermute | solution.py:345
  65.6 0.0 collective-permute-start.13
  65.6 12.6 %collective-permute-done.15.x_up.refs_9_ = bf16[6,8,64,128]{3,2,1,0:T(8,128)(2,1)S(1)} collective-permute-done((bf16[6,8,64,128]{3,2,1,0:T(8,128)(2,1)S(1)}, bf16[6,8,64,128]{3,2,1,0:T(8,128)(2,1)S(1)}, u32[]{:S(2)}, u32[]{:S(2)}) %collective-permute-start.15) | collective-permute-done | bytes 786464 | tf_op jit(solution)/shard_map/ppermute | solution.py:342
  78.2 0.0 collective-permute-done.16.x_down.refs_10_
  78.2 1.8 %collective-permute-done.14.y_down.refs_3_ = bf16[3,2,8,64,128]{4,3,2,1,0:T(8,128)(2,1)S(1)} collective-permute-done((bf16[3,2,8,64,128]{4,3,2,1,0:T(8,128)(2,1)S(1)}, bf16[3,2,8,64,128]{4,3,2,1,0:T(8,128)(2,1)S(1)}, u32[]{:S(2)}, u32[]{:S(2)}) %collective-permute-start.14) | collective-permute-done | bytes 786464 | tf_op jit(solution)/shard_map/ppermute | solution.py:345
  80.0 3.1 %collective-permute-done.13.y_up.refs_2_ = bf16[3,2,8,64,128]{4,3,2,1,0:T(8,128)(2,1)S(1)} collective-permute-done((bf16[3,2,8,64,128]{4,3,2,1,0:T(8,128)(2,1)S(1)}, bf16[3,2,8,64,128]{4,3,2,1,0:T(8,128)(2,1)S(1)}, u32[]{:S(2)}, u32[]{:S(2)}) %collective-permute-start.13) | collective-permute-done | bytes 786464 | tf_op jit(solution)/shard_map/ppermute | solution.py:345
  83.2 0.1 third.1
  83.3 0.1 collective-permute-start.17
  83.4 2.7 %collective-permute-start.18 = (bf16[2,2,8,64,128]{4,3,2,1,0:T(8,128)(2,1)S(1)}, bf16[2,2,8,64,128]{4,3,2,1,0:T(8,128)(2,1)S(1)}, u32[]{:S(2)}, u32[]{:S(2)}) collective-permute-start(bf16[2,2,8,64,128]{4,3,2,1,0:T(8,128)(2,1)S(1)} %get-tuple-element.32), channel_id=1, source_target_pairs={{0,24},{8,0},{16,8},{24,16},{1,25},{9,1},{17,9},{25,17},{2,26},{10... | collective-permute-start | bytes 1572872 | tf_op jit(solution)/shard_map/ppermute | solution.py:345
  86.0 2.7 %collective-permute-start.20 = (bf16[3,8,64,128]{3,2,1,0:T(8,128)(2,1)S(1)}, bf16[3,8,64,128]{3,2,1,0:T(8,128)(2,1)S(1)}, u32[]{:S(2)}, u32[]{:S(2)}) collective-permute-start(bf16[3,8,64,128]{3,2,1,0:T(8,128)(2,1)S(1)} %get-tuple-element.34), channel_id=1, source_target_pairs={{0,6},{1,7},{2,0},{3,1},{4,2},{5,3},{6,4},{7,5},{8,14},{9,15},{10,... | collective-permute-start | bytes 1179656 | tf_op jit(solution)/shard_map/ppermute | solution.py:342
  88.7 5.5 %collective-permute-done.19.refs_11_ = bf16[3,8,64,128]{3,2,1,0:T(8,128)(2,1)S(1)} collective-permute-done((bf16[3,8,64,128]{3,2,1,0:T(8,128)(2,1)S(1)}, bf16[3,8,64,128]{3,2,1,0:T(8,128)(2,1)S(1)}, u32[]{:S(2)}, u32[]{:S(2)}) %collective-permute-start.19) | collective-permute-done | bytes 393248 | tf_op jit(solution)/shard_map/ppermute | solution.py:342
  94.2 0.2 collective-permute-done.17.refs_0_
  94.4 4.5 %product.1 = (f32[4,2,128,256]{3,2,1,0:T(8,128)S(1)}, f32[4,2,128,256]{3,2,1,0:T(8,128)S(1)}) custom-call(s32[4]{0:T(128)S(1)} %copy-done, bf16[2,2,8,64,128]{4,3,2,1,0:T(8,128)(2,1)S(1)} %collective-permute-done.17.refs_0_, bf16[2,2,8,64,128]{4,3,2,1,0:T(8,128)(2,1)S(1)} %collective-permute-done.18.refs_1_, ...), custom_call_target="tpu_custom_call" | custom-call | flops 2147483648 | bytes 25165824 | tf_op jit(solution)/shard_map/product/pallas_call | solution.py:311
  98.9 4.9 %collective-permute-start.21 = (f32[4,2,128,256]{3,2,1,0:T(8,128)S(1)}, f32[4,2,128,256]{3,2,1,0:T(8,128)S(1)}, u32[]{:S(2)}, u32[]{:S(2)}) collective-permute-start(f32[4,2,128,256]{3,2,1,0:T(8,128)S(1)} %get-tuple-element.36), channel_id=1, source_target_pairs={{0,1},{1,0},{2,3},{3,2},{4,5},{5,4},{6,7},{7,6},{8,9},{9,8},{10,11... | collective-permute-start | bytes 3145736 | tf_op jit(solution)/shard_map/ppermute | solution.py:351
  103.7 2.3 %collective-permute-done.21 = f32[4,2,128,256]{3,2,1,0:T(8,128)S(1)} collective-permute-done((f32[4,2,128,256]{3,2,1,0:T(8,128)S(1)}, f32[4,2,128,256]{3,2,1,0:T(8,128)S(1)}, u32[]{:S(2)}, u32[]{:S(2)}) %collective-permute-start.21) | collective-permute-done | bytes 1048608 | tf_op jit(solution)/shard_map/ppermute | solution.py:351
  106.0 1.5 %maximum_select_fusion = f32[8,2,128,256]{3,2,1,0:T(8,128)} fusion(f32[4,2,128,256]{3,2,1,0:T(8,128)S(1)} %collective-permute-done.21, f32[4,2,128,256]{3,2,1,0:T(8,128)S(1)} %get-tuple-element.35, pred[]{:T(512)S(6)} %eq.4), kind=kLoop, calls=%fused_computation | loop fusion | flops 1572864 | bytes 4194305 | tf_op jit(solution)/shard_map/jit(_where)/select_n | solution.py:387
  (15 shorter events, 0.1 us)
Async XLA Ops:
  9.3 5.0 %collective-permute-start = (bf16[8,8,32,128]{3,2,1,0:T(8,128)(2,1)}, bf16[8,8,32,128]{3,2,1,0:T(8,128)(2,1)S(1)}, u32[]{:S(2)}, u32[]{:S(2)}) collective-permute-start(bf16[8,8,32,128]{3,2,1,0:T(8,128)(2,1)} %get-tuple-element.22), channel_id=1, source_target_pairs={{0,1},{1,0},{2,3},{3,2},{4,5},{5,4},{6,7},{7,6},{8,9},{9,8},{10,11... | collective-permute-start | bytes 1572872 | tf_op jit(solution)/shard_map/ppermute | solution.py:351
  15.4 29.0 %copy-start = (s32[4]{0:T(128)S(1)}, s32[4]{0:T(128)}, u32[]{:S(2)}) copy-start(s32[4]{0:T(128)} %pad_add_fusion.place_ref) | copy-start | bytes 52
  15.5 13.7 %collective-permute-start.1 = (bf16[8,64,128]{2,1,0:T(8,128)(2,1)S(1)}, bf16[8,64,128]{2,1,0:T(8,128)(2,1)S(1)}, u32[]{:S(2)}, u32[]{:S(2)}) collective-permute-start(bf16[8,64,128]{2,1,0:T(8,128)(2,1)S(1)} %pad_maximum_fusion), channel_id=1, source_target_pairs={{0,96},{32,128},{64,160},{96,192},{128,224},{160,0},{192,32},{224,... | collective-permute-start | bytes 393224 | tf_op jit(solution)/shard_map/ppermute | solution.py:348
  18.2 11.8 %collective-permute-start.2 = (bf16[8,64,128]{2,1,0:T(8,128)(2,1)S(1)}, bf16[8,64,128]{2,1,0:T(8,128)(2,1)S(1)}, u32[]{:S(2)}, u32[]{:S(2)}) collective-permute-start(bf16[8,64,128]{2,1,0:T(8,128)(2,1)S(1)} %pad_maximum_fusion.1), channel_id=1, source_target_pairs={{0,160},{32,192},{64,224},{96,0},{128,32},{160,64},{192,96},{224,1... | collective-permute-start | bytes 393224 | tf_op jit(solution)/shard_map/ppermute | solution.py:348
  20.5 14.4 %collective-permute-start.3 = (bf16[8,64,128]{2,1,0:T(8,128)(2,1)S(1)}, bf16[8,64,128]{2,1,0:T(8,128)(2,1)S(1)}, u32[]{:S(2)}, u32[]{:S(2)}) collective-permute-start(bf16[8,64,128]{2,1,0:T(8,128)(2,1)S(1)} %pad_maximum_fusion.2), channel_id=1, source_target_pairs={{0,128},{32,160},{64,192},{96,224},{128,0},{160,32},{192,64},{224,... | collective-permute-start | bytes 393224 | tf_op jit(solution)/shard_map/ppermute | solution.py:348
  25.5 15.0 %collective-permute-start.4 = (bf16[8,64,128]{2,1,0:T(8,128)(2,1)S(1)}, bf16[8,64,128]{2,1,0:T(8,128)(2,1)S(1)}, u32[]{:S(2)}, u32[]{:S(2)}) collective-permute-start(bf16[8,64,128]{2,1,0:T(8,128)(2,1)S(1)} %pad_maximum_fusion.3), channel_id=1, source_target_pairs={{0,64},{32,96},{64,128},{96,160},{128,192},{160,224},{192,0},{224,... | collective-permute-start | bytes 393224 | tf_op jit(solution)/shard_map/ppermute | solution.py:348
  26.7 15.6 %collective-permute-start.5 = (bf16[8,64,128]{2,1,0:T(8,128)(2,1)S(1)}, bf16[8,64,128]{2,1,0:T(8,128)(2,1)S(1)}, u32[]{:S(2)}, u32[]{:S(2)}) collective-permute-start(bf16[8,64,128]{2,1,0:T(8,128)(2,1)S(1)} %pad_maximum_fusion.4), channel_id=1, source_target_pairs={{0,192},{32,224},{64,0},{96,32},{128,64},{160,96},{192,128},{224,1... | collective-permute-start | bytes 393224 | tf_op jit(solution)/shard_map/ppermute | solution.py:348
  29.2 13.4 %collective-permute-start.6 = (bf16[8,64,128]{2,1,0:T(8,128)(2,1)S(1)}, bf16[8,64,128]{2,1,0:T(8,128)(2,1)S(1)}, u32[]{:S(2)}, u32[]{:S(2)}) collective-permute-start(bf16[8,64,128]{2,1,0:T(8,128)(2,1)S(1)} %pad_maximum_fusion.5), channel_id=1, source_target_pairs={{0,32},{32,64},{64,96},{96,128},{128,160},{160,192},{192,224},{224... | collective-permute-start | bytes 393224 | tf_op jit(solution)/shard_map/ppermute | solution.py:348
  30.1 14.4 %collective-permute-start.7 = (bf16[8,64,128]{2,1,0:T(8,128)(2,1)S(1)}, bf16[8,64,128]{2,1,0:T(8,128)(2,1)S(1)}, u32[]{:S(2)}, u32[]{:S(2)}) collective-permute-start(bf16[8,64,128]{2,1,0:T(8,128)(2,1)S(1)} %pad_maximum_fusion.6), channel_id=1, source_target_pairs={{0,224},{32,0},{64,32},{96,64},{128,96},{160,128},{192,160},{224,1... | collective-permute-start | bytes 393224 | tf_op jit(solution)/shard_map/ppermute | solution.py:348
  45.1 8.2 %collective-permute-start.8 = (bf16[2,8,64,128]{3,2,1,0:T(8,128)(2,1)S(1)}, bf16[2,8,64,128]{3,2,1,0:T(8,128)(2,1)S(1)}, u32[]{:S(2)}, u32[]{:S(2)}) collective-permute-start(bf16[2,8,64,128]{3,2,1,0:T(8,128)(2,1)S(1)} %get-tuple-element.24), channel_id=1, source_target_pairs={{0,2},{1,3},{2,4},{3,5},{4,6},{5,7},{6,0},{7,1},{8,10},{9,11},{10,... | collective-permute-start | bytes 786440 | tf_op jit(solution)/shard_map/ppermute | solution.py:342
  46.4 6.9 %collective-permute-start.9 = (bf16[2,8,64,128]{3,2,1,0:T(8,128)(2,1)S(1)}, bf16[2,8,64,128]{3,2,1,0:T(8,128)(2,1)S(1)}, u32[]{:S(2)}, u32[]{:S(2)}) collective-permute-start(bf16[2,8,64,128]{3,2,1,0:T(8,128)(2,1)S(1)} %get-tuple-element.25), channel_id=1, source_target_pairs={{0,6},{1,7},{2,0},{3,1},{4,2},{5,3},{6,4},{7,5},{8,14},{9,15},{10,... | collective-permute-start | bytes 786440 | tf_op jit(solution)/shard_map/ppermute | solution.py:342
  47.9 12.0 %collective-permute-start.10 = (bf16[2,8,64,128]{3,2,1,0:T(8,128)(2,1)S(1)}, bf16[2,8,64,128]{3,2,1,0:T(8,128)(2,1)S(1)}, u32[]{:S(2)}, u32[]{:S(2)}) collective-permute-start(bf16[2,8,64,128]{3,2,1,0:T(8,128)(2,1)S(1)} %get-tuple-element.26), channel_id=1, source_target_pairs={{0,4},{1,5},{2,6},{3,7},{4,0},{5,1},{6,2},{7,3},{8,12},{9,13},{10,... | collective-permute-start | bytes 786440 | tf_op jit(solution)/shard_map/ppermute | solution.py:342
  49.4 10.5 %collective-permute-start.12 = (bf16[2,8,64,128]{3,2,1,0:T(8,128)(2,1)S(1)}, bf16[2,8,64,128]{3,2,1,0:T(8,128)(2,1)S(1)}, u32[]{:S(2)}, u32[]{:S(2)}) collective-permute-start(bf16[2,8,64,128]{3,2,1,0:T(8,128)(2,1)S(1)} %get-tuple-element.27.refs_6_), channel_id=1, source_target_pairs={{0,24},{8,0},{16,8},{24,16},{1,25},{9,1},{17,9},{25,17},{2,26},{10... | collective-permute-start | bytes 786440 | tf_op jit(solution)/shard_map/ppermute | solution.py:345
  52.1 7.8 %collective-permute-start.11 = (bf16[2,8,64,128]{3,2,1,0:T(8,128)(2,1)S(1)}, bf16[2,8,64,128]{3,2,1,0:T(8,128)(2,1)S(1)}, u32[]{:S(2)}, u32[]{:S(2)}) collective-permute-start(bf16[2,8,64,128]{3,2,1,0:T(8,128)(2,1)S(1)} %get-tuple-element.27.refs_6_), channel_id=1, source_target_pairs={{0,8},{8,16},{16,24},{24,0},{1,9},{9,17},{17,25},{25,1},{2,10},{10... | collective-permute-start | bytes 786440 | tf_op jit(solution)/shard_map/ppermute | solution.py:345
  60.1 18.2 %collective-permute-start.15 = (bf16[6,8,64,128]{3,2,1,0:T(8,128)(2,1)S(1)}, bf16[6,8,64,128]{3,2,1,0:T(8,128)(2,1)S(1)}, u32[]{:S(2)}, u32[]{:S(2)}) collective-permute-start(bf16[6,8,64,128]{3,2,1,0:T(8,128)(2,1)S(1)} %get-tuple-element.29), channel_id=1, source_target_pairs={{0,2},{1,3},{2,4},{3,5},{4,6},{5,7},{6,0},{7,1},{8,10},{9,11},{10,... | collective-permute-start | bytes 2359304 | tf_op jit(solution)/shard_map/ppermute | solution.py:342
  60.7 17.5 %collective-permute-start.16 = (bf16[6,8,64,128]{3,2,1,0:T(8,128)(2,1)S(1)}, bf16[6,8,64,128]{3,2,1,0:T(8,128)(2,1)S(1)}, u32[]{:S(2)}, u32[]{:S(2)}) collective-permute-start(bf16[6,8,64,128]{3,2,1,0:T(8,128)(2,1)S(1)} %get-tuple-element.30), channel_id=1, source_target_pairs={{0,6},{1,7},{2,0},{3,1},{4,2},{5,3},{6,4},{7,5},{8,14},{9,15},{10,... | collective-permute-start | bytes 2359304 | tf_op jit(solution)/shard_map/ppermute | solution.py:342
  62.8 17.2 %collective-permute-start.14 = (bf16[3,2,8,64,128]{4,3,2,1,0:T(8,128)(2,1)S(1)}, bf16[3,2,8,64,128]{4,3,2,1,0:T(8,128)(2,1)S(1)}, u32[]{:S(2)}, u32[]{:S(2)}) collective-permute-start(bf16[3,2,8,64,128]{4,3,2,1,0:T(8,128)(2,1)S(1)} %get-tuple-element.28.refs_7_), channel_id=1, source_target_pairs={{0,24},{8,0},{16,8},{24,16},{1,25},{9,1},{17,9},{25,17},{2,26},{10... | collective-permute-start | bytes 2359304 | tf_op jit(solution)/shard_map/ppermute | solution.py:345
  65.6 17.6 %collective-permute-start.13 = (bf16[3,2,8,64,128]{4,3,2,1,0:T(8,128)(2,1)S(1)}, bf16[3,2,8,64,128]{4,3,2,1,0:T(8,128)(2,1)S(1)}, u32[]{:S(2)}, u32[]{:S(2)}) collective-permute-start(bf16[3,2,8,64,128]{4,3,2,1,0:T(8,128)(2,1)S(1)} %get-tuple-element.28.refs_7_), channel_id=1, source_target_pairs={{0,8},{8,16},{16,24},{24,0},{1,9},{9,17},{17,25},{25,1},{2,10},{10... | collective-permute-start | bytes 2359304 | tf_op jit(solution)/shard_map/ppermute | solution.py:345
  83.3 11.1 %collective-permute-start.17 = (bf16[2,2,8,64,128]{4,3,2,1,0:T(8,128)(2,1)S(1)}, bf16[2,2,8,64,128]{4,3,2,1,0:T(8,128)(2,1)S(1)}, u32[]{:S(2)}, u32[]{:S(2)}) collective-permute-start(bf16[2,2,8,64,128]{4,3,2,1,0:T(8,128)(2,1)S(1)} %get-tuple-element.31), channel_id=1, source_target_pairs={{0,8},{8,16},{16,24},{24,0},{1,9},{9,17},{17,25},{25,1},{2,10},{10... | collective-permute-start | bytes 1572872 | tf_op jit(solution)/shard_map/ppermute | solution.py:345
  83.4 11.0 %collective-permute-start.18 = (bf16[2,2,8,64,128]{4,3,2,1,0:T(8,128)(2,1)S(1)}, bf16[2,2,8,64,128]{4,3,2,1,0:T(8,128)(2,1)S(1)}, u32[]{:S(2)}, u32[]{:S(2)}) collective-permute-start(bf16[2,2,8,64,128]{4,3,2,1,0:T(8,128)(2,1)S(1)} %get-tuple-element.32), channel_id=1, source_target_pairs={{0,24},{8,0},{16,8},{24,16},{1,25},{9,1},{17,9},{25,17},{2,26},{10... | collective-permute-start | bytes 1572872 | tf_op jit(solution)/shard_map/ppermute | solution.py:345
  86.0 8.1 %collective-permute-start.19 = (bf16[3,8,64,128]{3,2,1,0:T(8,128)(2,1)S(1)}, bf16[3,8,64,128]{3,2,1,0:T(8,128)(2,1)S(1)}, u32[]{:S(2)}, u32[]{:S(2)}) collective-permute-start(bf16[3,8,64,128]{3,2,1,0:T(8,128)(2,1)S(1)} %get-tuple-element.33), channel_id=1, source_target_pairs={{0,2},{1,3},{2,4},{3,5},{4,6},{5,7},{6,0},{7,1},{8,10},{9,11},{10,... | collective-permute-start | bytes 1179656 | tf_op jit(solution)/shard_map/ppermute | solution.py:342
  86.0 8.1 %collective-permute-start.20 = (bf16[3,8,64,128]{3,2,1,0:T(8,128)(2,1)S(1)}, bf16[3,8,64,128]{3,2,1,0:T(8,128)(2,1)S(1)}, u32[]{:S(2)}, u32[]{:S(2)}) collective-permute-start(bf16[3,8,64,128]{3,2,1,0:T(8,128)(2,1)S(1)} %get-tuple-element.34), channel_id=1, source_target_pairs={{0,6},{1,7},{2,0},{3,1},{4,2},{5,3},{6,4},{7,5},{8,14},{9,15},{10,... | collective-permute-start | bytes 1179656 | tf_op jit(solution)/shard_map/ppermute | solution.py:342
  98.9 7.2 %collective-permute-start.21 = (f32[4,2,128,256]{3,2,1,0:T(8,128)S(1)}, f32[4,2,128,256]{3,2,1,0:T(8,128)S(1)}, u32[]{:S(2)}, u32[]{:S(2)}) collective-permute-start(f32[4,2,128,256]{3,2,1,0:T(8,128)S(1)} %get-tuple-element.36), channel_id=1, source_target_pairs={{0,1},{1,0},{2,3},{3,2},{4,5},{5,4},{6,7},{7,6},{8,9},{9,8},{10,11... | collective-permute-start | bytes 3145736 | tf_op jit(solution)/shard_map/ppermute | solution.py:351

commit v3 on v2

v3 whole, which is shorter than its diff:
```python
import functools
import math

import jax
import jax.numpy as jnp
from jax import lax
from jax.experimental import pallas as pl
from jax.experimental.pallas import tpu as pltpu
from jax.sharding import PartitionSpec as P

ZORDER = (7, 1, 6, 2, 3, 5, 4, 0)


def filter_table(taps_ref, bands_ref, weights_ref, table_ref):
    samples = weights_ref.shape[0]
    taps = taps_ref.shape[1]
    bands = bands_ref[...]
    count = bands.shape[1]
    both = jnp.concatenate([bands, bands], 1)
    first = lax.broadcasted_iota(jnp.int32, (1, 2 * count), 1) < count
    step = 32
    index = lax.broadcasted_iota(jnp.int32, (step, 2 * count), 0)

    def angle_of(times):
        phase = lax.rem(times * both, samples)
        return (2.0 * math.pi / samples) * phase.astype(jnp.float32)

    coarse = angle_of(index * step)
    fine = angle_of(index)
    coarse_cos, coarse_sin = jnp.cos(coarse), jnp.sin(coarse)
    scale = 1.0 / math.sqrt(samples)
    fine_cos, fine_sin = jnp.cos(fine) * scale, jnp.sin(fine) * scale
    first_part = jnp.where(first, coarse_cos, -coarse_sin)
    second_part = jnp.where(first, coarse_sin, coarse_cos)
    for block in range(samples // step):
        rows = (
            first_part[block : block + 1] * fine_cos - second_part[block : block + 1] * fine_sin
        )
        table_ref[block * step : (block + 1) * step, :] = rows.astype(jnp.bfloat16)
    table_ref[samples:, :] = jnp.zeros((table_ref.shape[0] - samples, 2 * count), jnp.bfloat16)

    block = 128
    padded = jnp.concatenate(
        [taps_ref[...].astype(jnp.float32), jnp.zeros((1, 2 * block - taps), jnp.float32)], 1
    )
    band_matrix = pltpu.roll(
        jnp.broadcast_to(padded, (block, 2 * block)), 0, 1, stride=1, stride_axis=0
    ).astype(jnp.bfloat16)
    for at in range(samples // block):
        filtered = jnp.dot(
            band_matrix,
            table_ref[at * block : (at + 2) * block, :],
            preferred_element_type=jnp.float32,
        )
        high = filtered.astype(jnp.bfloat16)
        low = (filtered - high.astype(jnp.float32)).astype(jnp.bfloat16)
        weights_ref[at * block : (at + 1) * block, : 2 * count] = high
        weights_ref[at * block : (at + 1) * block, 2 * count :] = low


def front_kernel(taps_ref, bands_ref, traces_ref, *rest, planes, block, parts, pitch):
    mine, others = rest[:2]
    weights_ref, table_ref, traces, picked, turned, sems = rest[2:]
    shots, receivers, samples = traces_ref.shape
    count = bands_ref.shape[1]
    lanes = 2 * count
    size = shots // parts
    blocks = receivers // block

    def load(at, part):
        rows = pl.ds(part * size, size)
        return pltpu.make_async_copy(
            traces_ref.at[rows, pl.ds(at * block, block), :],
            traces.at[at, rows],
            sems.at[at, part],
        )

    for at in range(blocks):
        for part in range(parts):
            load(at, part).start()
    filter_table(taps_ref, bands_ref, weights_ref, table_ref)

    group = 256 // block

    def pick(at, part):
        load(at, part).wait()
        for first in range(part * size, (part + 1) * size, group):
            rows = traces[at, first : first + group].reshape(group * block, samples)
            both = jnp.dot(rows, weights_ref[...], preferred_element_type=jnp.float32)
            picked[at, first * block : (first + group) * block, :] = (
                both[:, :lanes] + both[:, lanes:]
            )

    def turn(at, receiver):
        turned[at, receiver * pitch : receiver * pitch + lanes, :] = picked[
            at, pl.ds(receiver, shots, stride=block), :
        ].T

    plane, core, _, _ = place_of()
    owned = count // planes
    half = owned // 2

    def write(at, hop):
        for other, out in enumerate((mine, others)):
            base = lax.rem(plane + hop, planes) * owned + (core ^ other) * half
            for part in range(2):
                for band in range(half):
                    rows = turned[
                        at, pl.ds(base + (part * count + band), block, stride=pitch), :
                    ]
                    out[hop, part * half + band, at * block : (at + 1) * block, :] = rows.astype(
                        jnp.bfloat16
                    )

    for at in range(blocks + 1):
        for part in range(parts):
            if at < blocks:
                pick(at, part)
            if at > 0 and part < parts // 2:
                step = 2 * block // parts
                for receiver in range(part * step, (part + 1) * step):
                    turn(at - 1, receiver)
            elif at > 0:
                step = 2 * planes // parts
                for hop in range((part - parts // 2) * step, (part - parts // 2 + 1) * step):
                    write(at - 1, hop)


def front(taps, bands, traces, planes):
    shots, receivers, samples = traces.shape
    count = bands.shape[0]
    block, parts = 16, 2
    pitch = 2 * count + 4
    blocks = receivers // block
    out = jax.ShapeDtypeStruct((planes, count // planes, receivers, shots), jnp.bfloat16)
    vmem = pl.BlockSpec(memory_space=pltpu.VMEM)
    return pl.pallas_call(
        functools.partial(front_kernel, planes=planes, block=block, parts=parts, pitch=pitch),
        out_shape=[out] * 2,
        grid=(1,),
        in_specs=[
            pl.BlockSpec((1, taps.shape[0]), lambda i: (0, 0)),
            pl.BlockSpec((1, count), lambda i: (0, 0)),
            pl.BlockSpec(memory_space=pltpu.HBM),
        ],
        out_specs=[vmem] * 2,
        scratch_shapes=[
            pltpu.VMEM((samples, 4 * count), jnp.bfloat16),
            pltpu.VMEM((samples + 128, 2 * count), jnp.bfloat16),
            pltpu.VMEM((blocks, shots, block, samples), jnp.bfloat16),
            pltpu.VMEM((blocks, shots * block, 2 * count), jnp.float32),
            pltpu.VMEM((blocks, block * pitch, shots), jnp.float32),
            pltpu.SemaphoreType.DMA((blocks, parts)),
        ],
        compiler_params=pltpu.CompilerParams(vmem_limit_bytes=52 * 1024 * 1024),
        cost_estimate=pl.CostEstimate(
            flops=4 * shots * receivers * samples * count * 2,
            bytes_accessed=shots * receivers * samples * 2,
            transcendentals=0,
        ),
        name="front",
    )(taps.reshape(1, -1), bands.reshape(1, -1), traces)


UP = ((6, 2), (0, 2), (4, 2))
DOWN = ((1, 3), (0, 1), (4, 2))


def place_of():
    row = lax.axis_index("ry")
    return lax.axis_index("shot"), lax.rem(row, 2), row // 2, lax.axis_index("rx")


def sort_kernel(*refs):
    pieces = refs[:8]
    held = refs[8]
    turns = refs[9:]
    plane, core, chip, _ = place_of()
    first = plane - 2 * chip + 8
    width = held.shape[2] // 2
    for hop, piece in zip(ZORDER, pieces):
        block = lax.rem(first - hop + 8, 8)
        for part in range(2):
            start = pl.multiple_of((core ^ part) * width, width)
            held[block, :, pl.ds(start, width), :] = piece[:, part * width : (part + 1) * width]
    for pair, turn in enumerate(turns):
        turn[...] = held[2 * pair : 2 * pair + 2]


def sort_blocks(pieces):
    shape = pieces[0].shape
    two = jax.ShapeDtypeStruct((2,) + shape, jnp.bfloat16)
    eight = jax.ShapeDtypeStruct((8,) + shape, jnp.bfloat16)
    vmem = pl.BlockSpec(memory_space=pltpu.VMEM)
    return pl.pallas_call(
        sort_kernel,
        out_shape=[eight, two, two, two, two],
        in_specs=[vmem] * 8,
        out_specs=[vmem] * 5,
        compiler_params=pltpu.CompilerParams(vmem_limit_bytes=16 * 1024 * 1024),
        cost_estimate=pl.CostEstimate(flops=0, bytes_accessed=1 << 20, transcendentals=0),
        name="sort",
    )(*[pieces[hop] for hop in ZORDER])


def second_kernel(held, after_up, after_down, up_turn, down_turn, far_turn, up, down, turned):
    del after_up, after_down
    for target, order in ((up, UP), (down, DOWN)):
        at = 0
        for first, size in order:
            target[at : at + size] = held[first : first + size]
            at += size
    for at, turn in enumerate((up_turn, down_turn, far_turn)):
        turned[at] = turn[...]


def second_step(held, turns, after):
    block = held.shape[1:]
    six = jax.ShapeDtypeStruct((6,) + block, jnp.bfloat16)
    turned = jax.ShapeDtypeStruct((3, 2) + block, jnp.bfloat16)
    vmem = pl.BlockSpec(memory_space=pltpu.VMEM)
    hbm = pl.BlockSpec(memory_space=pl.ANY)
    return pl.pallas_call(
        second_kernel,
        out_shape=[six, six, turned],
        in_specs=[vmem] + [hbm] * 2 + [vmem] * 3,
        out_specs=[vmem] * 3,
        compiler_params=pltpu.CompilerParams(vmem_limit_bytes=16 * 1024 * 1024),
        cost_estimate=pl.CostEstimate(flops=0, bytes_accessed=1 << 20, transcendentals=0),
        name="second",
    )(held, *after, *turns)


def third_kernel(y_up, y_down, own_down, x_up, x_down, y_up_far, y_down_far, x_up_far, x_down_far):
    y_up_far[...] = y_up[:2]
    y_down_far[0] = own_down[...]
    y_down_far[1] = y_down[2]
    x_up_far[...] = x_up[:3]
    x_down_far[...] = x_down[:3]


def third_step(y_up, y_down, own_down, x_up, x_down):
    block = x_up.shape[1:]
    two = jax.ShapeDtypeStruct((2, 2) + block, jnp.bfloat16)
    three = jax.ShapeDtypeStruct((3,) + block, jnp.bfloat16)
    vmem = pl.BlockSpec(memory_space=pltpu.VMEM)
    return pl.pallas_call(
        third_kernel,
        out_shape=[two, two, three, three],
        in_specs=[vmem] * 5,
        out_specs=[vmem] * 4,
        compiler_params=pltpu.CompilerParams(vmem_limit_bytes=16 * 1024 * 1024),
        cost_estimate=pl.CostEstimate(flops=0, bytes_accessed=1 << 20, transcendentals=0),
        name="third",
    )(y_up, y_down, own_down, x_up, x_down)


LEFTS = (
    (3, (0,)),
    (1, (0,)),
    (3, (1, 2, 3)),
    (1, (1, 2, 3)),
    (0, (0,)),
    (0, (1, 2, 3)),
)
LAST_LEFTS = ((2, (1, 2)), (2, (0, 3)))


def panel_copies(right, left, sems, rights, lefts):
    _, _, chip, column = place_of()
    width = right.shape[2] // 4
    chips = [lax.rem(chip + hop, 4) for hop in (0, 3, 1, 2)]
    copies = []

    def copy(source, target):
        copies.append(pltpu.make_async_copy(source, target, sems.at[len(copies)]))

    for source, runs, slot in rights:
        at = 0
        for first, size in runs:
            while size and at < source.shape[0]:
                step = min(size, 2 - first % 2, source.shape[0] - at)
                block = lax.rem(2 * chips[slot] + first, 8)
                start = pl.multiple_of(chips[slot] * width, width)
                copy(
                    source.at[pl.ds(at, step)],
                    right.at[pl.ds(block, step), :, pl.ds(start, width), :],
                )
                at, first, size = at + step, first + step, size - step
    for source, (hop, slots) in lefts:
        for at, slot in enumerate(slots):
            start = lax.rem(column + hop, 4) * 4 * width + chips[slot] * width
            copy(
                source.at[at] if len(slots) > 1 else source,
                left.at[:, :, pl.ds(pl.multiple_of(start, width), width), :],
            )
    for one in copies:
        one.start()
    for one in copies:
        one.wait()


def stage_kernel(*refs):
    lefts = refs[: len(LEFTS)]
    held, up, down = refs[len(LEFTS) : len(LEFTS) + 3]
    right, left, sems = refs[len(LEFTS) + 3 :]
    turned = lefts[-1]
    rights = [(held, ((0, 8),), 0), (up, UP, 1), (down, DOWN, 2)]
    for slot, first in ((1, 2), (2, 6), (3, 4)):
        rights.append((turned.at[slot - 1], ((first, 2),), slot))
    panel_copies(right, left, sems, rights, list(zip(lefts, LEFTS)))


def stage(lefts, rights):
    blocks, parts, width, shots = rights[0].shape
    anywhere = pl.BlockSpec(memory_space=pl.ANY)
    vmem = pl.BlockSpec(memory_space=pltpu.VMEM)
    return pl.pallas_call(
        stage_kernel,
        out_shape=[
            jax.ShapeDtypeStruct((blocks, parts, 4 * width, shots), jnp.bfloat16),
            jax.ShapeDtypeStruct((2, parts, 16 * width, shots), jnp.bfloat16),
        ],
        in_specs=[anywhere] * (len(lefts) + len(rights)),
        out_specs=[vmem] * 2,
        scratch_shapes=[pltpu.SemaphoreType.DMA((64,))],
        compiler_params=pltpu.CompilerParams(vmem_limit_bytes=16 * 1024 * 1024),
        cost_estimate=pl.CostEstimate(flops=0, bytes_accessed=8 << 20, transcendentals=0),
        name="stage",
    )(*lefts, *rights)


def multiply(right, left, keep, give, out, out_sem, bands):
    _, core, _, _ = place_of()
    half_bands = right.shape[1] // 2
    factor = -1.0 / math.sqrt(left.shape[2])
    stores = []
    for at, band in enumerate(bands):
        rows = jnp.concatenate(
            [
                jnp.concatenate(
                    [right[z, part * half_bands + band] for z in range(right.shape[0])], 1
                )
                for part in range(2)
            ],
            0,
        )
        real, imag = (
            jnp.dot(
                rows,
                jnp.concatenate(
                    [left[s, part * half_bands + band] for s in (core, 1 - core)], 1
                ),
                preferred_element_type=jnp.float32,
            )
            for part in range(2)
        )
        half = real.shape[0] // 2
        for part, value in enumerate((real[:half] - imag[half:], imag[:half] + real[half:])):
            turned_value = (value * factor).T
            keep[at, part] = turned_value[: half // 2]
            give[at, part] = turned_value[half // 2 :]
        store = pltpu.make_async_copy(
            keep.at[at], out.at[core * half_bands + band], out_sem.at[at]
        )
        store.start()
        stores.append(store)
    for store in stores:
        store.wait()


def first_product_kernel(*refs, bands):
    y_up_far, y_down_far, x_up_far, x_down_far = refs[2:6]
    right, left, out, give, keep, sems, out_sem = refs[6:]
    panel_copies(
        right,
        left,
        sems,
        [(x_up_far, UP, 3), (x_down_far, DOWN, 3)],
        list(zip((y_up_far, y_down_far), LAST_LEFTS)),
    )
    multiply(right, left, keep, give, out, out_sem, bands)


def second_product_kernel(right, left, _, out, give, keep, out_sem, *, bands):
    multiply(right, left, keep, give, out, out_sem, bands)


def product_cost(right, left, bands):
    return pl.CostEstimate(
        flops=8 * len(bands) * right.shape[2] * 2 * left.shape[3] * left.shape[2],
        bytes_accessed=8 << 20,
        transcendentals=0,
    )


def first_product(right, left, last, bands):
    vmem = pl.BlockSpec(memory_space=pltpu.VMEM)
    block = (2, left.shape[3], right.shape[2])
    return pl.pallas_call(
        functools.partial(first_product_kernel, bands=bands),
        out_shape=[
            jax.ShapeDtypeStruct(right.shape, right.dtype),
            jax.ShapeDtypeStruct(left.shape, left.dtype),
            jax.ShapeDtypeStruct((right.shape[1],) + block, jnp.float32),
            jax.ShapeDtypeStruct((len(bands),) + block, jnp.float32),
        ],
        in_specs=[vmem] * 2 + [pl.BlockSpec(memory_space=pl.ANY)] * 4,
        out_specs=[vmem, vmem, pl.BlockSpec(memory_space=pltpu.HBM), vmem],
        scratch_shapes=[
            pltpu.VMEM((len(bands),) + block, jnp.float32),
            pltpu.SemaphoreType.DMA((16,)),
            pltpu.SemaphoreType.DMA((len(bands),)),
        ],
        input_output_aliases={0: 0, 1: 1},
        compiler_params=pltpu.CompilerParams(vmem_limit_bytes=32 * 1024 * 1024),
        cost_estimate=product_cost(right, left, bands),
        name="first_product",
    )(right, left, *last)


def second_product(right, left, whole, bands):
    vmem = pl.BlockSpec(memory_space=pltpu.VMEM)
    hbm = pl.BlockSpec(memory_space=pltpu.HBM)
    block = (2, left.shape[3], right.shape[2])
    return pl.pallas_call(
        functools.partial(second_product_kernel, bands=bands),
        out_shape=[
            jax.ShapeDtypeStruct(whole.shape, whole.dtype),
            jax.ShapeDtypeStruct((len(bands),) + block, jnp.float32),
        ],
        in_specs=[vmem, vmem, hbm],
        out_specs=[hbm, vmem],
        scratch_shapes=[
            pltpu.VMEM((len(bands),) + block, jnp.float32),
            pltpu.SemaphoreType.DMA((len(bands),)),
        ],
        input_output_aliases={2: 0},
        compiler_params=pltpu.CompilerParams(vmem_limit_bytes=32 * 1024 * 1024),
        cost_estimate=product_cost(right, left, bands),
        name="second_product",
    )(right, left, whole)


def local(traces, ghost_filter, bands):
    planes = 8
    mine, others = front(ghost_filter, bands, traces, planes)

    def along_x(value, hop):
        pairs = [(i, ((i // 2 + hop) % 4) * 2 + i % 2) for i in range(8)]
        return lax.ppermute(value, "ry", pairs)

    def along_y(value, hop):
        return lax.ppermute(value, "rx", [(i, (i + hop) % 4) for i in range(4)])

    def along_z(value, hop):
        return lax.ppermute(value, "shot", [(i, (i + hop) % planes) for i in range(planes)])

    def swap(value):
        return lax.ppermute(value, "ry", [(i, i ^ 1) for i in range(8)])

    theirs = swap(others)
    pieces = [None] * planes
    for hop in ZORDER:
        piece = jnp.concatenate([mine[hop], theirs[hop]], 1)
        pieces[hop] = along_z(piece, hop) if hop else piece
    held, own_turn, up_turn, far_turn, down_turn = sort_blocks(pieces)
    own_up, own_down = along_y(own_turn, 1), along_y(own_turn, -1)
    turns = along_x(up_turn, 1), along_x(down_turn, -1), along_x(far_turn, 2)
    up, down, turned = second_step(held, turns, (own_up, own_down))
    y_up, y_down = along_y(turned, 1), along_y(turned, -1)
    up, down = along_x(up, 1), along_x(down, -1)
    y_up_far, y_down_far, x_up_far, x_down_far = third_step(y_up, y_down, own_down, up, down)
    y_up_far, y_down_far = along_y(y_up_far, 1), along_y(y_down_far, -1)
    x_up_far, x_down_far = along_x(x_up_far, 1), along_x(x_down_far, -1)
    right, left = stage((own_up, own_down, y_up, y_down, own_turn, turned), (held, up, down))
    half = right.shape[1] // 4
    right, left, whole, first_give = first_product(
        right, left, (y_up_far, y_down_far, x_up_far, x_down_far), tuple(range(half))
    )
    first_take = swap(first_give)
    whole, second_give = second_product(right, left, whole, tuple(range(half, 2 * half)))
    second_take = swap(second_give)
    start = (1 - lax.rem(lax.axis_index("ry"), 2)) * 2 * half
    whole = lax.dynamic_update_slice(whole, first_take, (start, 0, 0, 0))
    return lax.dynamic_update_slice(whole, second_take, (start + half, 0, 0, 0))


def solution(mesh):
    placed = (P("shot", ("rx", "ry"), None), P(), P())
    return jax.shard_map(
        local, mesh=mesh, in_specs=placed, out_specs=P("shot", None, "ry", "rx"), check_vma=False
    )
```

time: 108 us -> 102 us (0.944)
  waiting for transfers between devices: 47.4 us -> 44 us
  other arithmetic: 3.29 us -> 0.08 us
  local copies, waits for them, and re-layouts: 0.08 us -> 3.05 us
  Pallas kernels: 14.2 us -> 11.3 us
    ppermute x7, waiting for transfers between devices: 25.8 us -> 15.2 us  [along_x(): return lax.ppermute(value, 'ry', pairs)]
    ppermute x6, waiting for transfers between devices: 5.16 us -> 13.9 us  [along_y(): return lax.ppermute(value, 'rx', [(i, (i + hop) % 4) for i in range(4)])]
    select_n x2 -> x0, other arithmetic: 2.62 us -> none  [the longest x1 1.51 us: local(): jnp.where(core == 0, jnp.concatenate(keeps + takes), jnp.concatenate(take...]
    pallas_call x2 -> x4, Pallas kernels: 13.2 us -> 10.9 us  [the longest x1 4.97 us: front(): pl.pallas_call(functools.partial(front_kernel, planes=planes, block=block...]
    dynamic_update_slice x0 -> x2, local copies, waits for them, and re-layouts: none -> 1.67 us  [the longest x1 0.84 us: local(): whole = lax.dynamic_update_slice(whole, first_take, (start, 0, 0, 0))]
    ppermute x2 -> x3, waiting for transfers between devices: 4.03 us -> 2.54 us  [swap(): return lax.ppermute(value, 'ry', [(i, i ^ 1) for i in range(8)])]
    unnamed x2 -> x4, local copies, waits for them, and re-layouts: 0.01 us -> 1.31 us
    ppermute x2 -> x3, starting transfers between devices: 8.12 us -> 8.65 us  [swap(): return lax.ppermute(value, 'ry', [(i, i ^ 1) for i in range(8)])]
  transfers between devices with their start and end apart: 22 -> 23, of which waited for: 14 -> 14; matrix products, arithmetic and copies ran while one was open for 0% -> 1% of each run, Pallas kernels for 0% -> 3%
where the time goes in v3:
time: 102 us
  waiting for transfers between devices  44 us (43%)
  starting transfers between devices  43 us (42%)
  Pallas kernels  11.3 us (11%)
  local copies, waits for them, and re-layouts  3.05 us (3%)
    ppermute x7, starting transfers between devices, along_z(): lax.ppermute(value, 'shot', [(i, (i + hop) % planes) for i in range(plane...  16.4 us
    ppermute x7, waiting for transfers between devices, along_x(): return lax.ppermute(value, 'ry', pairs)  15.2 us
    ppermute x6, waiting for transfers between devices, along_y(): return lax.ppermute(value, 'rx', [(i, (i + hop) % 4) for i in range(4)])  13.9 us
    ppermute x7, waiting for transfers between devices, along_z(): lax.ppermute(value, 'shot', [(i, (i + hop) % planes) for i in range(plane...  12.3 us
    ppermute x7, starting transfers between devices, along_x(): return lax.ppermute(value, 'ry', pairs)  9.56 us
    ppermute x3, starting transfers between devices, swap(): return lax.ppermute(value, 'ry', [(i, i ^ 1) for i in range(8)])  8.65 us
    ppermute x6, starting transfers between devices, along_y(): return lax.ppermute(value, 'rx', [(i, (i + hop) % 4) for i in range(4)])  8.39 us
    pallas_call x1, Pallas kernels, front(): pl.pallas_call(functools.partial(front_kernel, planes=planes, block=block...  4.97 us
  transfers between devices with their start and end apart: 23, of which 14 were waited for; matrix products, arithmetic and copies ran while one was open for 1% of the time, Pallas kernels for 3%

profile of v3, /device:TPU:1, one launch (start us, length us, event | category | flops | bytes accessed | tf_op | source)
XLA Modules:
  0.0 101.7 jit_solution(5176340405399165309)
XLA Ops:
  0.0 0.7 copy-done
  0.7 0.7 copy-done.1
  1.3 5.0 %front.1 = (bf16[8,8,32,128]{3,2,1,0:T(8,128)(2,1)S(1)}, bf16[8,8,32,128]{3,2,1,0:T(8,128)(2,1)S(1)}) custom-call(bf16[1,64]{1,0:T(2,128)(2,1)S(1)} %bitcast.34, s32[1,64]{1,0:T(1,128)S(1)} %bitcast.35, bf16[128,32,1024]{2,1,0:T(8,128)(2,1)} %traces_ref.1), custom_call_target="tpu_custom_call" | custom-call | flops 2147483648 | bytes 8388608 | tf_op jit(solution)/shard_map/front/pallas_call | solution.py:137
  6.3 3.3 %collective-permute-start = (bf16[8,8,32,128]{3,2,1,0:T(8,128)(2,1)S(1)}, bf16[8,8,32,128]{3,2,1,0:T(8,128)(2,1)S(1)}, u32[]{:S(2)}, u32[]{:S(2)}) collective-permute-start(bf16[8,8,32,128]{3,2,1,0:T(8,128)(2,1)S(1)} %get-tuple-element.28), channel_id=1, source_target_pairs={{0,1},{1,0},{2,3},{3,2},{4,5},{5,4},{6,7},{7,6},{8,9},{9,8},{10,11... | collective-permute-start | bytes 1572872 | tf_op jit(solution)/shard_map/ppermute | solution.py:460
  9.7 1.5 %collective-permute-done = bf16[8,8,32,128]{3,2,1,0:T(8,128)(2,1)S(1)} collective-permute-done((bf16[8,8,32,128]{3,2,1,0:T(8,128)(2,1)S(1)}, bf16[8,8,32,128]{3,2,1,0:T(8,128)(2,1)S(1)}, u32[]{:S(2)}, u32[]{:S(2)}) %collective-permute-start) | collective-permute-done | bytes 524320 | tf_op jit(solution)/shard_map/ppermute | solution.py:460
  11.2 2.7 %collective-permute-start.5 = (bf16[8,64,128]{2,1,0:T(8,128)(2,1)S(1)}, bf16[8,64,128]{2,1,0:T(8,128)(2,1)S(1)}, u32[]{:S(2)}, u32[]{:S(2)}) collective-permute-start(bf16[8,64,128]{2,1,0:T(8,128)(2,1)S(1)} %pad_maximum_fusion.4), channel_id=1, source_target_pairs={{0,96},{32,128},{64,160},{96,192},{128,224},{160,0},{192,32},{224,... | collective-permute-start | bytes 393224 | tf_op jit(solution)/shard_map/ppermute | solution.py:457
  13.9 2.2 %collective-permute-start.6 = (bf16[8,64,128]{2,1,0:T(8,128)(2,1)S(1)}, bf16[8,64,128]{2,1,0:T(8,128)(2,1)S(1)}, u32[]{:S(2)}, u32[]{:S(2)}) collective-permute-start(bf16[8,64,128]{2,1,0:T(8,128)(2,1)S(1)} %pad_maximum_fusion.5), channel_id=1, source_target_pairs={{0,160},{32,192},{64,224},{96,0},{128,32},{160,64},{192,96},{224,1... | collective-permute-start | bytes 393224 | tf_op jit(solution)/shard_map/ppermute | solution.py:457
  16.1 5.0 %collective-permute-start.7 = (bf16[8,64,128]{2,1,0:T(8,128)(2,1)S(1)}, bf16[8,64,128]{2,1,0:T(8,128)(2,1)S(1)}, u32[]{:S(2)}, u32[]{:S(2)}) collective-permute-start(bf16[8,64,128]{2,1,0:T(8,128)(2,1)S(1)} %pad_maximum_fusion.6), channel_id=1, source_target_pairs={{0,128},{32,160},{64,192},{96,224},{128,0},{160,32},{192,64},{224,... | collective-permute-start | bytes 393224 | tf_op jit(solution)/shard_map/ppermute | solution.py:457
  21.1 1.3 %collective-permute-start.4 = (bf16[8,64,128]{2,1,0:T(8,128)(2,1)S(1)}, bf16[8,64,128]{2,1,0:T(8,128)(2,1)S(1)}, u32[]{:S(2)}, u32[]{:S(2)}) collective-permute-start(bf16[8,64,128]{2,1,0:T(8,128)(2,1)S(1)} %pad_maximum_fusion.3), channel_id=1, source_target_pairs={{0,64},{32,96},{64,128},{96,160},{128,192},{160,224},{192,0},{224,... | collective-permute-start | bytes 393224 | tf_op jit(solution)/shard_map/ppermute | solution.py:457
  22.4 2.5 %collective-permute-start.3 = (bf16[8,64,128]{2,1,0:T(8,128)(2,1)S(1)}, bf16[8,64,128]{2,1,0:T(8,128)(2,1)S(1)}, u32[]{:S(2)}, u32[]{:S(2)}) collective-permute-start(bf16[8,64,128]{2,1,0:T(8,128)(2,1)S(1)} %pad_maximum_fusion.2), channel_id=1, source_target_pairs={{0,192},{32,224},{64,0},{96,32},{128,64},{160,96},{192,128},{224,1... | collective-permute-start | bytes 393224 | tf_op jit(solution)/shard_map/ppermute | solution.py:457
  24.9 0.0 collective-permute-done.5.refs_4_
  24.9 0.8 collective-permute-start.2
  25.7 2.0 %collective-permute-start.1 = (bf16[8,64,128]{2,1,0:T(8,128)(2,1)S(1)}, bf16[8,64,128]{2,1,0:T(8,128)(2,1)S(1)}, u32[]{:S(2)}, u32[]{:S(2)}) collective-permute-start(bf16[8,64,128]{2,1,0:T(8,128)(2,1)S(1)} %pad_maximum_fusion), channel_id=1, source_target_pairs={{0,224},{32,0},{64,32},{96,64},{128,96},{160,128},{192,160},{224,1... | collective-permute-start | bytes 393224 | tf_op jit(solution)/shard_map/ppermute | solution.py:457
  27.8 2.7 %collective-permute-done.7.refs_6_ = bf16[8,64,128]{2,1,0:T(8,128)(2,1)S(1)} collective-permute-done((bf16[8,64,128]{2,1,0:T(8,128)(2,1)S(1)}, bf16[8,64,128]{2,1,0:T(8,128)(2,1)S(1)}, u32[]{:S(2)}, u32[]{:S(2)}) %collective-permute-start.7) | collective-permute-done | bytes 131104 | tf_op jit(solution)/shard_map/ppermute | solution.py:457
  30.5 5.6 %collective-permute-done.4.refs_3_ = bf16[8,64,128]{2,1,0:T(8,128)(2,1)S(1)} collective-permute-done((bf16[8,64,128]{2,1,0:T(8,128)(2,1)S(1)}, bf16[8,64,128]{2,1,0:T(8,128)(2,1)S(1)}, u32[]{:S(2)}, u32[]{:S(2)}) %collective-permute-start.4) | collective-permute-done | bytes 131104 | tf_op jit(solution)/shard_map/ppermute | solution.py:457
  36.1 1.9 %collective-permute-done.3.refs_2_ = bf16[8,64,128]{2,1,0:T(8,128)(2,1)S(1)} collective-permute-done((bf16[8,64,128]{2,1,0:T(8,128)(2,1)S(1)}, bf16[8,64,128]{2,1,0:T(8,128)(2,1)S(1)}, u32[]{:S(2)}, u32[]{:S(2)}) %collective-permute-start.3) | collective-permute-done | bytes 131104 | tf_op jit(solution)/shard_map/ppermute | solution.py:457
  38.0 0.4 collective-permute-done.2.refs_1_
  38.4 1.7 %collective-permute-done.1.refs_0_ = bf16[8,64,128]{2,1,0:T(8,128)(2,1)S(1)} collective-permute-done((bf16[8,64,128]{2,1,0:T(8,128)(2,1)S(1)}, bf16[8,64,128]{2,1,0:T(8,128)(2,1)S(1)}, u32[]{:S(2)}, u32[]{:S(2)}) %collective-permute-start.1) | collective-permute-done | bytes 131104 | tf_op jit(solution)/shard_map/ppermute | solution.py:457
  40.1 0.2 sort.1
  40.3 1.4 %collective-permute-start.8 = (bf16[2,8,64,128]{3,2,1,0:T(8,128)(2,1)S(1)}, bf16[2,8,64,128]{3,2,1,0:T(8,128)(2,1)S(1)}, u32[]{:S(2)}, u32[]{:S(2)}) collective-permute-start(bf16[2,8,64,128]{3,2,1,0:T(8,128)(2,1)S(1)} %get-tuple-element.29.refs_4_), channel_id=1, source_target_pairs={{0,8},{8,16},{16,24},{24,0},{1,9},{9,17},{17,25},{25,1},{2,10},{10... | collective-permute-start | bytes 786440 | tf_op jit(solution)/shard_map/ppermute | solution.py:454
  41.6 1.5 %collective-permute-start.9 = (bf16[2,8,64,128]{3,2,1,0:T(8,128)(2,1)S(1)}, bf16[2,8,64,128]{3,2,1,0:T(8,128)(2,1)S(1)}, u32[]{:S(2)}, u32[]{:S(2)}) collective-permute-start(bf16[2,8,64,128]{3,2,1,0:T(8,128)(2,1)S(1)} %get-tuple-element.29.refs_4_), channel_id=1, source_target_pairs={{0,24},{8,0},{16,8},{24,16},{1,25},{9,1},{17,9},{25,17},{2,26},{10... | collective-permute-start | bytes 786440 | tf_op jit(solution)/shard_map/ppermute | solution.py:454
  43.2 1.2 %collective-permute-start.10 = (bf16[2,8,64,128]{3,2,1,0:T(8,128)(2,1)S(1)}, bf16[2,8,64,128]{3,2,1,0:T(8,128)(2,1)S(1)}, u32[]{:S(2)}, u32[]{:S(2)}) collective-permute-start(bf16[2,8,64,128]{3,2,1,0:T(8,128)(2,1)S(1)} %get-tuple-element.31), channel_id=1, source_target_pairs={{0,2},{1,3},{2,4},{3,5},{4,6},{5,7},{6,0},{7,1},{8,10},{9,11},{10,... | collective-permute-start | bytes 786440 | tf_op jit(solution)/shard_map/ppermute | solution.py:451
  44.4 1.5 %collective-permute-start.11 = (bf16[2,8,64,128]{3,2,1,0:T(8,128)(2,1)S(1)}, bf16[2,8,64,128]{3,2,1,0:T(8,128)(2,1)S(1)}, u32[]{:S(2)}, u32[]{:S(2)}) collective-permute-start(bf16[2,8,64,128]{3,2,1,0:T(8,128)(2,1)S(1)} %get-tuple-element.32), channel_id=1, source_target_pairs={{0,6},{1,7},{2,0},{3,1},{4,2},{5,3},{6,4},{7,5},{8,14},{9,15},{10,... | collective-permute-start | bytes 786440 | tf_op jit(solution)/shard_map/ppermute | solution.py:451
  45.8 1.5 %collective-permute-start.12 = (bf16[2,8,64,128]{3,2,1,0:T(8,128)(2,1)S(1)}, bf16[2,8,64,128]{3,2,1,0:T(8,128)(2,1)S(1)}, u32[]{:S(2)}, u32[]{:S(2)}) collective-permute-start(bf16[2,8,64,128]{3,2,1,0:T(8,128)(2,1)S(1)} %get-tuple-element.33), channel_id=1, source_target_pairs={{0,4},{1,5},{2,6},{3,7},{4,0},{5,1},{6,2},{7,3},{8,12},{9,13},{10,... | collective-permute-start | bytes 786440 | tf_op jit(solution)/shard_map/ppermute | solution.py:451
  47.4 1.2 %collective-permute-done.8.after_up.refs_0_ = bf16[2,8,64,128]{3,2,1,0:T(8,128)(2,1)S(1)} collective-permute-done((bf16[2,8,64,128]{3,2,1,0:T(8,128)(2,1)S(1)}, bf16[2,8,64,128]{3,2,1,0:T(8,128)(2,1)S(1)}, u32[]{:S(2)}, u32[]{:S(2)}) %collective-permute-start.8) | collective-permute-done | bytes 262176 | tf_op jit(solution)/shard_map/ppermute | solution.py:454
  48.6 2.3 %collective-permute-done.10.up_turn = bf16[2,8,64,128]{3,2,1,0:T(8,128)(2,1)S(1)} collective-permute-done((bf16[2,8,64,128]{3,2,1,0:T(8,128)(2,1)S(1)}, bf16[2,8,64,128]{3,2,1,0:T(8,128)(2,1)S(1)}, u32[]{:S(2)}, u32[]{:S(2)}) %collective-permute-start.10) | collective-permute-done | bytes 262176 | tf_op jit(solution)/shard_map/ppermute | solution.py:451
  50.8 6.6 %collective-permute-done.12.far_turn = bf16[2,8,64,128]{3,2,1,0:T(8,128)(2,1)S(1)} collective-permute-done((bf16[2,8,64,128]{3,2,1,0:T(8,128)(2,1)S(1)}, bf16[2,8,64,128]{3,2,1,0:T(8,128)(2,1)S(1)}, u32[]{:S(2)}, u32[]{:S(2)}) %collective-permute-start.12) | collective-permute-done | bytes 262176 | tf_op jit(solution)/shard_map/ppermute | solution.py:451
  57.4 0.2 second.1
  57.6 0.1 collective-permute-start.13
  57.7 2.7 %collective-permute-start.14 = (bf16[3,2,8,64,128]{4,3,2,1,0:T(8,128)(2,1)S(1)}, bf16[3,2,8,64,128]{4,3,2,1,0:T(8,128)(2,1)S(1)}, u32[]{:S(2)}, u32[]{:S(2)}) collective-permute-start(bf16[3,2,8,64,128]{4,3,2,1,0:T(8,128)(2,1)S(1)} %get-tuple-element.34.refs_5_), channel_id=1, source_target_pairs={{0,24},{8,0},{16,8},{24,16},{1,25},{9,1},{17,9},{25,17},{2,26},{10... | collective-permute-start | bytes 2359304 | tf_op jit(solution)/shard_map/ppermute | solution.py:454
  60.4 0.6 collective-permute-start.15
  61.0 2.1 %collective-permute-start.16 = (bf16[6,8,64,128]{3,2,1,0:T(8,128)(2,1)S(1)}, bf16[6,8,64,128]{3,2,1,0:T(8,128)(2,1)S(1)}, u32[]{:S(2)}, u32[]{:S(2)}) collective-permute-start(bf16[6,8,64,128]{3,2,1,0:T(8,128)(2,1)S(1)} %get-tuple-element.36), channel_id=1, source_target_pairs={{0,6},{1,7},{2,0},{3,1},{4,2},{5,3},{6,4},{7,5},{8,14},{9,15},{10,... | collective-permute-start | bytes 2359304 | tf_op jit(solution)/shard_map/ppermute | solution.py:451
  63.0 12.6 %collective-permute-done.13.refs_2_.y_up = bf16[3,2,8,64,128]{4,3,2,1,0:T(8,128)(2,1)S(1)} collective-permute-done((bf16[3,2,8,64,128]{4,3,2,1,0:T(8,128)(2,1)S(1)}, bf16[3,2,8,64,128]{4,3,2,1,0:T(8,128)(2,1)S(1)}, u32[]{:S(2)}, u32[]{:S(2)}) %collective-permute-start.13) | collective-permute-done | bytes 786464 | tf_op jit(solution)/shard_map/ppermute | solution.py:454
  75.7 2.1 %collective-permute-done.15.refs_7_.x_up = bf16[6,8,64,128]{3,2,1,0:T(8,128)(2,1)S(1)} collective-permute-done((bf16[6,8,64,128]{3,2,1,0:T(8,128)(2,1)S(1)}, bf16[6,8,64,128]{3,2,1,0:T(8,128)(2,1)S(1)}, u32[]{:S(2)}, u32[]{:S(2)}) %collective-permute-start.15) | collective-permute-done | bytes 786464 | tf_op jit(solution)/shard_map/ppermute | solution.py:451
  77.8 0.1 third.1
  77.9 0.1 collective-permute-start.17
  78.0 2.7 %collective-permute-start.18 = (bf16[2,2,8,64,128]{4,3,2,1,0:T(8,128)(2,1)S(1)}, bf16[2,2,8,64,128]{4,3,2,1,0:T(8,128)(2,1)S(1)}, u32[]{:S(2)}, u32[]{:S(2)}) collective-permute-start(bf16[2,2,8,64,128]{4,3,2,1,0:T(8,128)(2,1)S(1)} %get-tuple-element.40), channel_id=1, source_target_pairs={{0,24},{8,0},{16,8},{24,16},{1,25},{9,1},{17,9},{25,17},{2,26},{10... | collective-permute-start | bytes 1572872 | tf_op jit(solution)/shard_map/ppermute | solution.py:454
  80.7 2.7 %collective-permute-start.20 = (bf16[3,8,64,128]{3,2,1,0:T(8,128)(2,1)S(1)}, bf16[3,8,64,128]{3,2,1,0:T(8,128)(2,1)S(1)}, u32[]{:S(2)}, u32[]{:S(2)}) collective-permute-start(bf16[3,8,64,128]{3,2,1,0:T(8,128)(2,1)S(1)} %get-tuple-element.42), channel_id=1, source_target_pairs={{0,6},{1,7},{2,0},{3,1},{4,2},{5,3},{6,4},{7,5},{8,14},{9,15},{10,... | collective-permute-start | bytes 1179656 | tf_op jit(solution)/shard_map/ppermute | solution.py:451
  83.4 1.2 %stage.1 = (bf16[8,8,256,128]{3,2,1,0:T(8,128)(2,1)S(1)}, bf16[2,8,1024,128]{3,2,1,0:T(8,128)(2,1)S(1)}) custom-call(bf16[2,8,64,128]{3,2,1,0:T(8,128)(2,1)S(1)} %collective-permute-done.8.after_up.refs_0_, bf16[2,8,64,128]{3,2,1,0:T(8,128)(2,1)S(1)} %collective-permute-done.9.after_down.refs_1_.own_down, ...), custom_call_target="tpu_custom_call" | custom-call | bytes 8388608 | tf_op jit(solution)/shard_map/stage/pallas_call | solution.py:318
  84.6 4.3 %collective-permute-done.19.refs_4_ = bf16[3,8,64,128]{3,2,1,0:T(8,128)(2,1)S(1)} collective-permute-done((bf16[3,8,64,128]{3,2,1,0:T(8,128)(2,1)S(1)}, bf16[3,8,64,128]{3,2,1,0:T(8,128)(2,1)S(1)}, u32[]{:S(2)}, u32[]{:S(2)}) %collective-permute-start.19) | collective-permute-done | bytes 393248 | tf_op jit(solution)/shard_map/ppermute | solution.py:451
  88.8 0.1 collective-permute-done.17.refs_2_
  88.9 2.5 %first_product.1 = (bf16[8,8,256,128]{3,2,1,0:T(8,128)(2,1)S(1)}, bf16[2,8,1024,128]{3,2,1,0:T(8,128)(2,1)S(1)}, f32[8,2,128,256]{3,2,1,0:T(8,128)}, f32[2,2,128,256]{3,2,1,0:T(8,128)S(1)}) custom-call(bf16[8,8,256,128]{3,2,1,0:T(8,128)(2,1)S(1)} %get-tuple-element.37.refs_0_, ...), custom_call_target="tpu_custom_call", output_to_operand_aliasing={{0}: (0, {}), {1}: (1, {})} | custom-call | flops 1073741824 | bytes 8388608 | tf_op jit(solution)/shard_map/first_product/pallas_call | solution.py:400
  91.4 5.2 %collective-permute-start.21 = (f32[2,2,128,256]{3,2,1,0:T(8,128)S(1)}, f32[2,2,128,256]{3,2,1,0:T(8,128)S(1)}, u32[]{:S(2)}, u32[]{:S(2)}) collective-permute-start(f32[2,2,128,256]{3,2,1,0:T(8,128)S(1)} %get-tuple-element.47), channel_id=1, source_target_pairs={{0,1},{1,0},{2,3},{3,2},{4,5},{5,4},{6,7},{7,6},{8,9},{9,8},{10,11... | collective-permute-start | bytes 1572872 | tf_op jit(solution)/shard_map/ppermute | solution.py:460
  96.6 2.2 %second_product.1 = (f32[8,2,128,256]{3,2,1,0:T(8,128)}, f32[2,2,128,256]{3,2,1,0:T(8,128)S(1)}) custom-call(bf16[8,8,256,128]{3,2,1,0:T(8,128)(2,1)S(1)} %get-tuple-element.43.right, bf16[2,8,1024,128]{3,2,1,0:T(8,128)(2,1)S(1)} %get-tuple-element.44.left, f32[8,2,128,256]{3,2,1,0:T(8,128)} %get-tuple-element.45._), custom_call_target="tpu_custom_call", output_to_operand_aliasing={{0}: (2, {})} | custom-call | flops 1073741824 | bytes 8388608 | tf_op jit(solution)/shard_map/second_product/pallas_call | solution.py:426
  98.8 0.1 collective-permute-start.22
  98.9 0.8 constant_dynamic-update-slice_fusion.1
  99.8 1.0 %collective-permute-done.22 = f32[2,2,128,256]{3,2,1,0:T(8,128)S(1)} collective-permute-done((f32[2,2,128,256]{3,2,1,0:T(8,128)S(1)}, f32[2,2,128,256]{3,2,1,0:T(8,128)S(1)}, u32[]{:S(2)}, u32[]{:S(2)}) %collective-permute-start.22) | collective-permute-done | bytes 524320 | tf_op jit(solution)/shard_map/ppermute | solution.py:460
  100.8 0.8 constant_dynamic-update-slice_fusion
  (21 shorter events, 0.2 us)
Async XLA Ops:
  0.0 0.7 copy-start
  0.7 0.7 copy-start.1
  6.3 4.9 %collective-permute-start = (bf16[8,8,32,128]{3,2,1,0:T(8,128)(2,1)S(1)}, bf16[8,8,32,128]{3,2,1,0:T(8,128)(2,1)S(1)}, u32[]{:S(2)}, u32[]{:S(2)}) collective-permute-start(bf16[8,8,32,128]{3,2,1,0:T(8,128)(2,1)S(1)} %get-tuple-element.28), channel_id=1, source_target_pairs={{0,1},{1,0},{2,3},{3,2},{4,5},{5,4},{6,7},{7,6},{8,9},{9,8},{10,11... | collective-permute-start | bytes 1572872 | tf_op jit(solution)/shard_map/ppermute | solution.py:460
  11.2 13.7 %collective-permute-start.5 = (bf16[8,64,128]{2,1,0:T(8,128)(2,1)S(1)}, bf16[8,64,128]{2,1,0:T(8,128)(2,1)S(1)}, u32[]{:S(2)}, u32[]{:S(2)}) collective-permute-start(bf16[8,64,128]{2,1,0:T(8,128)(2,1)S(1)} %pad_maximum_fusion.4), channel_id=1, source_target_pairs={{0,96},{32,128},{64,160},{96,192},{128,224},{160,0},{192,32},{224,... | collective-permute-start | bytes 393224 | tf_op jit(solution)/shard_map/ppermute | solution.py:457
  13.9 11.8 %collective-permute-start.6 = (bf16[8,64,128]{2,1,0:T(8,128)(2,1)S(1)}, bf16[8,64,128]{2,1,0:T(8,128)(2,1)S(1)}, u32[]{:S(2)}, u32[]{:S(2)}) collective-permute-start(bf16[8,64,128]{2,1,0:T(8,128)(2,1)S(1)} %pad_maximum_fusion.5), channel_id=1, source_target_pairs={{0,160},{32,192},{64,224},{96,0},{128,32},{160,64},{192,96},{224,1... | collective-permute-start | bytes 393224 | tf_op jit(solution)/shard_map/ppermute | solution.py:457
  16.1 14.3 %collective-permute-start.7 = (bf16[8,64,128]{2,1,0:T(8,128)(2,1)S(1)}, bf16[8,64,128]{2,1,0:T(8,128)(2,1)S(1)}, u32[]{:S(2)}, u32[]{:S(2)}) collective-permute-start(bf16[8,64,128]{2,1,0:T(8,128)(2,1)S(1)} %pad_maximum_fusion.6), channel_id=1, source_target_pairs={{0,128},{32,160},{64,192},{96,224},{128,0},{160,32},{192,64},{224,... | collective-permute-start | bytes 393224 | tf_op jit(solution)/shard_map/ppermute | solution.py:457
  21.1 15.0 %collective-permute-start.4 = (bf16[8,64,128]{2,1,0:T(8,128)(2,1)S(1)}, bf16[8,64,128]{2,1,0:T(8,128)(2,1)S(1)}, u32[]{:S(2)}, u32[]{:S(2)}) collective-permute-start(bf16[8,64,128]{2,1,0:T(8,128)(2,1)S(1)} %pad_maximum_fusion.3), channel_id=1, source_target_pairs={{0,64},{32,96},{64,128},{96,160},{128,192},{160,224},{192,0},{224,... | collective-permute-start | bytes 393224 | tf_op jit(solution)/shard_map/ppermute | solution.py:457
  22.4 15.5 %collective-permute-start.3 = (bf16[8,64,128]{2,1,0:T(8,128)(2,1)S(1)}, bf16[8,64,128]{2,1,0:T(8,128)(2,1)S(1)}, u32[]{:S(2)}, u32[]{:S(2)}) collective-permute-start(bf16[8,64,128]{2,1,0:T(8,128)(2,1)S(1)} %pad_maximum_fusion.2), channel_id=1, source_target_pairs={{0,192},{32,224},{64,0},{96,32},{128,64},{160,96},{192,128},{224,1... | collective-permute-start | bytes 393224 | tf_op jit(solution)/shard_map/ppermute | solution.py:457
  24.9 13.4 %collective-permute-start.2 = (bf16[8,64,128]{2,1,0:T(8,128)(2,1)S(1)}, bf16[8,64,128]{2,1,0:T(8,128)(2,1)S(1)}, u32[]{:S(2)}, u32[]{:S(2)}) collective-permute-start(bf16[8,64,128]{2,1,0:T(8,128)(2,1)S(1)} %pad_maximum_fusion.1), channel_id=1, source_target_pairs={{0,32},{32,64},{64,96},{96,128},{128,160},{160,192},{192,224},{224... | collective-permute-start | bytes 393224 | tf_op jit(solution)/shard_map/ppermute | solution.py:457
  25.7 14.3 %collective-permute-start.1 = (bf16[8,64,128]{2,1,0:T(8,128)(2,1)S(1)}, bf16[8,64,128]{2,1,0:T(8,128)(2,1)S(1)}, u32[]{:S(2)}, u32[]{:S(2)}) collective-permute-start(bf16[8,64,128]{2,1,0:T(8,128)(2,1)S(1)} %pad_maximum_fusion), channel_id=1, source_target_pairs={{0,224},{32,0},{64,32},{96,64},{128,96},{160,128},{192,160},{224,1... | collective-permute-start | bytes 393224 | tf_op jit(solution)/shard_map/ppermute | solution.py:457
  40.3 8.3 %collective-permute-start.8 = (bf16[2,8,64,128]{3,2,1,0:T(8,128)(2,1)S(1)}, bf16[2,8,64,128]{3,2,1,0:T(8,128)(2,1)S(1)}, u32[]{:S(2)}, u32[]{:S(2)}) collective-permute-start(bf16[2,8,64,128]{3,2,1,0:T(8,128)(2,1)S(1)} %get-tuple-element.29.refs_4_), channel_id=1, source_target_pairs={{0,8},{8,16},{16,24},{24,0},{1,9},{9,17},{17,25},{25,1},{2,10},{10... | collective-permute-start | bytes 786440 | tf_op jit(solution)/shard_map/ppermute | solution.py:454
  41.6 6.9 %collective-permute-start.9 = (bf16[2,8,64,128]{3,2,1,0:T(8,128)(2,1)S(1)}, bf16[2,8,64,128]{3,2,1,0:T(8,128)(2,1)S(1)}, u32[]{:S(2)}, u32[]{:S(2)}) collective-permute-start(bf16[2,8,64,128]{3,2,1,0:T(8,128)(2,1)S(1)} %get-tuple-element.29.refs_4_), channel_id=1, source_target_pairs={{0,24},{8,0},{16,8},{24,16},{1,25},{9,1},{17,9},{25,17},{2,26},{10... | collective-permute-start | bytes 786440 | tf_op jit(solution)/shard_map/ppermute | solution.py:454
  43.2 7.7 %collective-permute-start.10 = (bf16[2,8,64,128]{3,2,1,0:T(8,128)(2,1)S(1)}, bf16[2,8,64,128]{3,2,1,0:T(8,128)(2,1)S(1)}, u32[]{:S(2)}, u32[]{:S(2)}) collective-permute-start(bf16[2,8,64,128]{3,2,1,0:T(8,128)(2,1)S(1)} %get-tuple-element.31), channel_id=1, source_target_pairs={{0,2},{1,3},{2,4},{3,5},{4,6},{5,7},{6,0},{7,1},{8,10},{9,11},{10,... | collective-permute-start | bytes 786440 | tf_op jit(solution)/shard_map/ppermute | solution.py:451
  44.4 6.5 %collective-permute-start.11 = (bf16[2,8,64,128]{3,2,1,0:T(8,128)(2,1)S(1)}, bf16[2,8,64,128]{3,2,1,0:T(8,128)(2,1)S(1)}, u32[]{:S(2)}, u32[]{:S(2)}) collective-permute-start(bf16[2,8,64,128]{3,2,1,0:T(8,128)(2,1)S(1)} %get-tuple-element.32), channel_id=1, source_target_pairs={{0,6},{1,7},{2,0},{3,1},{4,2},{5,3},{6,4},{7,5},{8,14},{9,15},{10,... | collective-permute-start | bytes 786440 | tf_op jit(solution)/shard_map/ppermute | solution.py:451
  45.8 11.6 %collective-permute-start.12 = (bf16[2,8,64,128]{3,2,1,0:T(8,128)(2,1)S(1)}, bf16[2,8,64,128]{3,2,1,0:T(8,128)(2,1)S(1)}, u32[]{:S(2)}, u32[]{:S(2)}) collective-permute-start(bf16[2,8,64,128]{3,2,1,0:T(8,128)(2,1)S(1)} %get-tuple-element.33), channel_id=1, source_target_pairs={{0,4},{1,5},{2,6},{3,7},{4,0},{5,1},{6,2},{7,3},{8,12},{9,13},{10,... | collective-permute-start | bytes 786440 | tf_op jit(solution)/shard_map/ppermute | solution.py:451
  57.6 18.1 %collective-permute-start.13 = (bf16[3,2,8,64,128]{4,3,2,1,0:T(8,128)(2,1)S(1)}, bf16[3,2,8,64,128]{4,3,2,1,0:T(8,128)(2,1)S(1)}, u32[]{:S(2)}, u32[]{:S(2)}) collective-permute-start(bf16[3,2,8,64,128]{4,3,2,1,0:T(8,128)(2,1)S(1)} %get-tuple-element.34.refs_5_), channel_id=1, source_target_pairs={{0,8},{8,16},{16,24},{24,0},{1,9},{9,17},{17,25},{25,1},{2,10},{10... | collective-permute-start | bytes 2359304 | tf_op jit(solution)/shard_map/ppermute | solution.py:454
  57.7 18.0 %collective-permute-start.14 = (bf16[3,2,8,64,128]{4,3,2,1,0:T(8,128)(2,1)S(1)}, bf16[3,2,8,64,128]{4,3,2,1,0:T(8,128)(2,1)S(1)}, u32[]{:S(2)}, u32[]{:S(2)}) collective-permute-start(bf16[3,2,8,64,128]{4,3,2,1,0:T(8,128)(2,1)S(1)} %get-tuple-element.34.refs_5_), channel_id=1, source_target_pairs={{0,24},{8,0},{16,8},{24,16},{1,25},{9,1},{17,9},{25,17},{2,26},{10... | collective-permute-start | bytes 2359304 | tf_op jit(solution)/shard_map/ppermute | solution.py:454
  60.4 17.4 %collective-permute-start.15 = (bf16[6,8,64,128]{3,2,1,0:T(8,128)(2,1)S(1)}, bf16[6,8,64,128]{3,2,1,0:T(8,128)(2,1)S(1)}, u32[]{:S(2)}, u32[]{:S(2)}) collective-permute-start(bf16[6,8,64,128]{3,2,1,0:T(8,128)(2,1)S(1)} %get-tuple-element.35), channel_id=1, source_target_pairs={{0,2},{1,3},{2,4},{3,5},{4,6},{5,7},{6,0},{7,1},{8,10},{9,11},{10,... | collective-permute-start | bytes 2359304 | tf_op jit(solution)/shard_map/ppermute | solution.py:451
  61.0 16.9 %collective-permute-start.16 = (bf16[6,8,64,128]{3,2,1,0:T(8,128)(2,1)S(1)}, bf16[6,8,64,128]{3,2,1,0:T(8,128)(2,1)S(1)}, u32[]{:S(2)}, u32[]{:S(2)}) collective-permute-start(bf16[6,8,64,128]{3,2,1,0:T(8,128)(2,1)S(1)} %get-tuple-element.36), channel_id=1, source_target_pairs={{0,6},{1,7},{2,0},{3,1},{4,2},{5,3},{6,4},{7,5},{8,14},{9,15},{10,... | collective-permute-start | bytes 2359304 | tf_op jit(solution)/shard_map/ppermute | solution.py:451
  77.9 11.0 %collective-permute-start.17 = (bf16[2,2,8,64,128]{4,3,2,1,0:T(8,128)(2,1)S(1)}, bf16[2,2,8,64,128]{4,3,2,1,0:T(8,128)(2,1)S(1)}, u32[]{:S(2)}, u32[]{:S(2)}) collective-permute-start(bf16[2,2,8,64,128]{4,3,2,1,0:T(8,128)(2,1)S(1)} %get-tuple-element.39), channel_id=1, source_target_pairs={{0,8},{8,16},{16,24},{24,0},{1,9},{9,17},{17,25},{25,1},{2,10},{10... | collective-permute-start | bytes 1572872 | tf_op jit(solution)/shard_map/ppermute | solution.py:454
  78.0 10.9 %collective-permute-start.18 = (bf16[2,2,8,64,128]{4,3,2,1,0:T(8,128)(2,1)S(1)}, bf16[2,2,8,64,128]{4,3,2,1,0:T(8,128)(2,1)S(1)}, u32[]{:S(2)}, u32[]{:S(2)}) collective-permute-start(bf16[2,2,8,64,128]{4,3,2,1,0:T(8,128)(2,1)S(1)} %get-tuple-element.40), channel_id=1, source_target_pairs={{0,24},{8,0},{16,8},{24,16},{1,25},{9,1},{17,9},{25,17},{2,26},{10... | collective-permute-start | bytes 1572872 | tf_op jit(solution)/shard_map/ppermute | solution.py:454
  80.7 8.1 %collective-permute-start.19 = (bf16[3,8,64,128]{3,2,1,0:T(8,128)(2,1)S(1)}, bf16[3,8,64,128]{3,2,1,0:T(8,128)(2,1)S(1)}, u32[]{:S(2)}, u32[]{:S(2)}) collective-permute-start(bf16[3,8,64,128]{3,2,1,0:T(8,128)(2,1)S(1)} %get-tuple-element.41), channel_id=1, source_target_pairs={{0,2},{1,3},{2,4},{3,5},{4,6},{5,7},{6,0},{7,1},{8,10},{9,11},{10,... | collective-permute-start | bytes 1179656 | tf_op jit(solution)/shard_map/ppermute | solution.py:451
  80.7 8.1 %collective-permute-start.20 = (bf16[3,8,64,128]{3,2,1,0:T(8,128)(2,1)S(1)}, bf16[3,8,64,128]{3,2,1,0:T(8,128)(2,1)S(1)}, u32[]{:S(2)}, u32[]{:S(2)}) collective-permute-start(bf16[3,8,64,128]{3,2,1,0:T(8,128)(2,1)S(1)} %get-tuple-element.42), channel_id=1, source_target_pairs={{0,6},{1,7},{2,0},{3,1},{4,2},{5,3},{6,4},{7,5},{8,14},{9,15},{10,... | collective-permute-start | bytes 1179656 | tf_op jit(solution)/shard_map/ppermute | solution.py:451
  91.4 7.5 %collective-permute-start.21 = (f32[2,2,128,256]{3,2,1,0:T(8,128)S(1)}, f32[2,2,128,256]{3,2,1,0:T(8,128)S(1)}, u32[]{:S(2)}, u32[]{:S(2)}) collective-permute-start(f32[2,2,128,256]{3,2,1,0:T(8,128)S(1)} %get-tuple-element.47), channel_id=1, source_target_pairs={{0,1},{1,0},{2,3},{3,2},{4,5},{5,4},{6,7},{7,6},{8,9},{9,8},{10,11... | collective-permute-start | bytes 1572872 | tf_op jit(solution)/shard_map/ppermute | solution.py:460
  98.8 2.0 %collective-permute-start.22 = (f32[2,2,128,256]{3,2,1,0:T(8,128)S(1)}, f32[2,2,128,256]{3,2,1,0:T(8,128)S(1)}, u32[]{:S(2)}, u32[]{:S(2)}) collective-permute-start(f32[2,2,128,256]{3,2,1,0:T(8,128)S(1)} %get-tuple-element.48), channel_id=1, source_target_pairs={{0,1},{1,0},{2,3},{3,2},{4,5},{5,4},{6,7},{7,6},{8,9},{9,8},{10,11... | collective-permute-start | bytes 1572872 | tf_op jit(solution)/shard_map/ppermute | solution.py:460

commit v4 on v3

--- a/solution.py
+++ b/solution.py
@@ -11,13 +11,12 @@
 ZORDER = (7, 1, 6, 2, 3, 5, 4, 0)
 
 
-def filter_table(taps_ref, bands_ref, weights_ref, table_ref):
+def filter_table(small_ref, weights_ref, table_ref):
     samples = weights_ref.shape[0]
-    taps = taps_ref.shape[1]
-    bands = bands_ref[...]
-    count = bands.shape[1]
-    both = jnp.concatenate([bands, bands], 1)
+    small = small_ref[...]
+    count = small.shape[1] // 2
     first = lax.broadcasted_iota(jnp.int32, (1, 2 * count), 1) < count
+    both = jnp.where(first, pltpu.roll(small, count, 1), small).astype(jnp.int32)
     step = 32
     index = lax.broadcasted_iota(jnp.int32, (step, 2 * count), 0)
 
@@ -41,7 +40,7 @@
 
     block = 128
     padded = jnp.concatenate(
-        [taps_ref[...].astype(jnp.float32), jnp.zeros((1, 2 * block - taps), jnp.float32)], 1
+        [jnp.where(first, small, 0.0), jnp.zeros((1, 2 * block - 2 * count), jnp.float32)], 1
     )
     band_matrix = pltpu.roll(
         jnp.broadcast_to(padded, (block, 2 * block)), 0, 1, stride=1, stride_axis=0
@@ -58,11 +57,11 @@
         weights_ref[at * block : (at + 1) * block, 2 * count :] = low
 
 
-def front_kernel(taps_ref, bands_ref, traces_ref, *rest, planes, block, parts, pitch):
+def front_kernel(small_ref, traces_ref, *rest, planes, block, parts, pitch):
     mine, others = rest[:2]
     weights_ref, table_ref, traces, picked, turned, sems = rest[2:]
     shots, receivers, samples = traces_ref.shape
-    count = bands_ref.shape[1]
+    count = small_ref.shape[1] // 2
     lanes = 2 * count
     size = shots // parts
     blocks = receivers // block
@@ -78,7 +77,7 @@
     for at in range(blocks):
         for part in range(parts):
             load(at, part).start()
-    filter_table(taps_ref, bands_ref, weights_ref, table_ref)
+    filter_table(small_ref, weights_ref, table_ref)
 
     group = 256 // block
 
@@ -137,10 +136,8 @@
     return pl.pallas_call(
         functools.partial(front_kernel, planes=planes, block=block, parts=parts, pitch=pitch),
         out_shape=[out] * 2,
-        grid=(1,),
         in_specs=[
-            pl.BlockSpec((1, taps.shape[0]), lambda i: (0, 0)),
-            pl.BlockSpec((1, count), lambda i: (0, 0)),
+            vmem,
             pl.BlockSpec(memory_space=pltpu.HBM),
         ],
         out_specs=[vmem] * 2,
@@ -159,7 +156,7 @@
             transcendentals=0,
         ),
         name="front",
-    )(taps.reshape(1, -1), bands.reshape(1, -1), traces)
+    )(jnp.concatenate([taps.astype(jnp.float32), bands.astype(jnp.float32)]).reshape(1, -1), traces)
 
 
 UP = ((6, 2), (0, 2), (4, 2))
@@ -203,8 +200,7 @@
     )(*[pieces[hop] for hop in ZORDER])
 
 
-def second_kernel(held, after_up, after_down, up_turn, down_turn, far_turn, up, down, turned):
-    del after_up, after_down
+def second_kernel(held, own_up, own_down, down_turn, up_turn, far_turn, up, down, turned, owns):
     for target, order in ((up, UP), (down, DOWN)):
         at = 0
         for first, size in order:
@@ -212,34 +208,36 @@
             at += size
     for at, turn in enumerate((up_turn, down_turn, far_turn)):
         turned[at] = turn[...]
-
-
-def second_step(held, turns, after):
+    for at, own in enumerate((own_up, own_down)):
+        owns[at] = own[...]
+
+
+def second_step(held, turns, owns):
     block = held.shape[1:]
     six = jax.ShapeDtypeStruct((6,) + block, jnp.bfloat16)
     turned = jax.ShapeDtypeStruct((3, 2) + block, jnp.bfloat16)
-    vmem = pl.BlockSpec(memory_space=pltpu.VMEM)
-    hbm = pl.BlockSpec(memory_space=pl.ANY)
+    both = jax.ShapeDtypeStruct((2, 2) + block, jnp.bfloat16)
+    vmem = pl.BlockSpec(memory_space=pltpu.VMEM)
     return pl.pallas_call(
         second_kernel,
-        out_shape=[six, six, turned],
-        in_specs=[vmem] + [hbm] * 2 + [vmem] * 3,
-        out_specs=[vmem] * 3,
+        out_shape=[six, six, turned, both],
+        in_specs=[vmem] * 6,
+        out_specs=[vmem] * 4,
         compiler_params=pltpu.CompilerParams(vmem_limit_bytes=16 * 1024 * 1024),
         cost_estimate=pl.CostEstimate(flops=0, bytes_accessed=1 << 20, transcendentals=0),
         name="second",
-    )(held, *after, *turns)
-
-
-def third_kernel(y_up, y_down, own_down, x_up, x_down, y_up_far, y_down_far, x_up_far, x_down_far):
+    )(held, owns[0], owns[1], turns[1], turns[0], turns[2])
+
+
+def third_kernel(y_up, y_down, x_up, owns, x_down, y_up_far, y_down_far, x_up_far, x_down_far):
     y_up_far[...] = y_up[:2]
-    y_down_far[0] = own_down[...]
+    y_down_far[0] = owns[1]
     y_down_far[1] = y_down[2]
     x_up_far[...] = x_up[:3]
     x_down_far[...] = x_down[:3]
 
 
-def third_step(y_up, y_down, own_down, x_up, x_down):
+def third_step(y_up, y_down, owns, x_up, x_down):
     block = x_up.shape[1:]
     two = jax.ShapeDtypeStruct((2, 2) + block, jnp.bfloat16)
     three = jax.ShapeDtypeStruct((3,) + block, jnp.bfloat16)
@@ -252,12 +250,10 @@
         compiler_params=pltpu.CompilerParams(vmem_limit_bytes=16 * 1024 * 1024),
         cost_estimate=pl.CostEstimate(flops=0, bytes_accessed=1 << 20, transcendentals=0),
         name="third",
-    )(y_up, y_down, own_down, x_up, x_down)
+    )(y_up, y_down, x_up, owns, x_down)
 
 
 LEFTS = (
-    (3, (0,)),
-    (1, (0,)),
     (3, (1, 2, 3)),
     (1, (1, 2, 3)),
     (0, (0,)),
@@ -303,12 +299,13 @@
 def stage_kernel(*refs):
     lefts = refs[: len(LEFTS)]
     held, up, down = refs[len(LEFTS) : len(LEFTS) + 3]
-    right, left, sems = refs[len(LEFTS) + 3 :]
-    turned = lefts[-1]
+    right, left, sems = refs[len(LEFTS) + 4 :]
+    turned, owns = lefts[-1], refs[len(LEFTS) + 3]
+    lefts = list(zip(lefts, LEFTS)) + [(owns.at[0], (3, (0,))), (owns.at[1], (1, (0,)))]
     rights = [(held, ((0, 8),), 0), (up, UP, 1), (down, DOWN, 2)]
     for slot, first in ((1, 2), (2, 6), (3, 4)):
         rights.append((turned.at[slot - 1], ((first, 2),), slot))
-    panel_copies(right, left, sems, rights, list(zip(lefts, LEFTS)))
+    panel_copies(right, left, sems, rights, lefts)
 
 
 def stage(lefts, rights):
@@ -330,11 +327,10 @@
     )(*lefts, *rights)
 
 
-def multiply(right, left, keep, give, out, out_sem, bands):
+def multiply(right, left, keep, give, bands):
     _, core, _, _ = place_of()
     half_bands = right.shape[1] // 2
     factor = -1.0 / math.sqrt(left.shape[2])
-    stores = []
     for at, band in enumerate(bands):
         rows = jnp.concatenate(
             [
@@ -360,18 +356,11 @@
             turned_value = (value * factor).T
             keep[at, part] = turned_value[: half // 2]
             give[at, part] = turned_value[half // 2 :]
-        store = pltpu.make_async_copy(
-            keep.at[at], out.at[core * half_bands + band], out_sem.at[at]
-        )
-        store.start()
-        stores.append(store)
-    for store in stores:
-        store.wait()
 
 
 def first_product_kernel(*refs, bands):
     y_up_far, y_down_far, x_up_far, x_down_far = refs[2:6]
-    right, left, out, give, keep, sems, out_sem = refs[6:]
+    right, left, keep, give, sems = refs[6:]
     panel_copies(
         right,
         left,
@@ -379,11 +368,11 @@
         [(x_up_far, UP, 3), (x_down_far, DOWN, 3)],
         list(zip((y_up_far, y_down_far), LAST_LEFTS)),
     )
-    multiply(right, left, keep, give, out, out_sem, bands)
-
-
-def second_product_kernel(right, left, _, out, give, keep, out_sem, *, bands):
-    multiply(right, left, keep, give, out, out_sem, bands)
+    multiply(right, left, keep, give, bands)
+
+
+def second_product_kernel(right, left, keep, give, *, bands):
+    multiply(right, left, keep, give, bands)
 
 
 def product_cost(right, left, bands):
@@ -402,16 +391,12 @@
         out_shape=[
             jax.ShapeDtypeStruct(right.shape, right.dtype),
             jax.ShapeDtypeStruct(left.shape, left.dtype),
-            jax.ShapeDtypeStruct((right.shape[1],) + block, jnp.float32),
+            jax.ShapeDtypeStruct((len(bands),) + block, jnp.float32),
             jax.ShapeDtypeStruct((len(bands),) + block, jnp.float32),
         ],
         in_specs=[vmem] * 2 + [pl.BlockSpec(memory_space=pl.ANY)] * 4,
-        out_specs=[vmem, vmem, pl.BlockSpec(memory_space=pltpu.HBM), vmem],
-        scratch_shapes=[
-            pltpu.VMEM((len(bands),) + block, jnp.float32),
-            pltpu.SemaphoreType.DMA((16,)),
-            pltpu.SemaphoreType.DMA((len(bands),)),
-        ],
+        out_specs=[vmem] * 4,
+        scratch_shapes=[pltpu.SemaphoreType.DMA((16,))],
         input_output_aliases={0: 0, 1: 1},
         compiler_params=pltpu.CompilerParams(vmem_limit_bytes=32 * 1024 * 1024),
         cost_estimate=product_cost(right, left, bands),
@@ -419,27 +404,18 @@
     )(right, left, *last)
 
 
-def second_product(right, left, whole, bands):
-    vmem = pl.BlockSpec(memory_space=pltpu.VMEM)
-    hbm = pl.BlockSpec(memory_space=pltpu.HBM)
-    block = (2, left.shape[3], right.shape[2])
+def second_product(right, left, bands):
+    vmem = pl.BlockSpec(memory_space=pltpu.VMEM)
+    out = jax.ShapeDtypeStruct((len(bands), 2, left.shape[3], right.shape[2]), jnp.float32)
     return pl.pallas_call(
         functools.partial(second_product_kernel, bands=bands),
-        out_shape=[
-            jax.ShapeDtypeStruct(whole.shape, whole.dtype),
-            jax.ShapeDtypeStruct((len(bands),) + block, jnp.float32),
-        ],
-        in_specs=[vmem, vmem, hbm],
-        out_specs=[hbm, vmem],
-        scratch_shapes=[
-            pltpu.VMEM((len(bands),) + block, jnp.float32),
-            pltpu.SemaphoreType.DMA((len(bands),)),
-        ],
-        input_output_aliases={2: 0},
-        compiler_params=pltpu.CompilerParams(vmem_limit_bytes=32 * 1024 * 1024),
+        out_shape=[out] * 2,
+        in_specs=[vmem] * 2,
+        out_specs=[vmem] * 2,
+        compiler_params=pltpu.CompilerParams(vmem_limit_bytes=16 * 1024 * 1024),
         cost_estimate=product_cost(right, left, bands),
         name="second_product",
-    )(right, left, whole)
+    )(right, left)
 
 
 def local(traces, ghost_filter, bands):
@@ -467,23 +443,25 @@
     held, own_turn, up_turn, far_turn, down_turn = sort_blocks(pieces)
     own_up, own_down = along_y(own_turn, 1), along_y(own_turn, -1)
     turns = along_x(up_turn, 1), along_x(down_turn, -1), along_x(far_turn, 2)
-    up, down, turned = second_step(held, turns, (own_up, own_down))
+    up, down, turned, owns = second_step(held, turns, (own_up, own_down))
     y_up, y_down = along_y(turned, 1), along_y(turned, -1)
     up, down = along_x(up, 1), along_x(down, -1)
-    y_up_far, y_down_far, x_up_far, x_down_far = third_step(y_up, y_down, own_down, up, down)
+    y_up_far, y_down_far, x_up_far, x_down_far = third_step(y_up, y_down, owns, up, down)
     y_up_far, y_down_far = along_y(y_up_far, 1), along_y(y_down_far, -1)
     x_up_far, x_down_far = along_x(x_up_far, 1), along_x(x_down_far, -1)
-    right, left = stage((own_up, own_down, y_up, y_down, own_turn, turned), (held, up, down))
+    right, left = stage((y_up, y_down, own_turn, turned), (held, up, down, owns))
     half = right.shape[1] // 4
-    right, left, whole, first_give = first_product(
+    right, left, first_keep, first_give = first_product(
         right, left, (y_up_far, y_down_far, x_up_far, x_down_far), tuple(range(half))
     )
     first_take = swap(first_give)
-    whole, second_give = second_product(right, left, whole, tuple(range(half, 2 * half)))
-    second_take = swap(second_give)
-    start = (1 - lax.rem(lax.axis_index("ry"), 2)) * 2 * half
-    whole = lax.dynamic_update_slice(whole, first_take, (start, 0, 0, 0))
-    return lax.dynamic_update_slice(whole, second_take, (start + half, 0, 0, 0))
+    second_keep, second_give = second_product(right, left, tuple(range(half, 2 * half)))
+    keep = [first_keep, second_keep]
+    take = [first_take, swap(second_give)]
+    core = lax.rem(lax.axis_index("ry"), 2)
+    low = [jnp.where(core == 0, k, t) for k, t in zip(keep, take)]
+    high = [jnp.where(core == 0, t, k) for k, t in zip(keep, take)]
+    return jnp.concatenate(low + high)
 
 
 def solution(mesh):

time: 102 us -> 99.2 us (0.973)
  other arithmetic: 0.08 us -> 3.11 us
  local copies, waits for them, and re-layouts: 3.05 us -> 0.07 us
  waiting for transfers between devices: 44 us -> 42.1 us
  Pallas kernels: 11.3 us -> 9.9 us
    ppermute x6, waiting for transfers between devices: 13.9 us -> 11.8 us  [along_y(): return lax.ppermute(value, 'rx', [(i, (i + hop) % 4) for i in range(4)])]
    dynamic_update_slice x2 -> x0, local copies, waits for them, and re-layouts: 1.67 us -> none  [the longest x1 0.84 us: local(): whole = lax.dynamic_update_slice(whole, first_take, (start, 0, 0, 0))]
    concatenate x0 -> x1, other arithmetic: none -> 1.48 us  [local(): return jnp.concatenate(low + high)]
    convert_element_type x0 -> x2, other arithmetic: none -> 1.31 us  [the longest x1 0.66 us: front(): taps.astype(jnp.float32)]
    unnamed x4 -> x0, local copies, waits for them, and re-layouts: 1.31 us -> none
  transfers between devices with their start and end apart: 23 -> 23, of which waited for: 14 -> 13; matrix products, arithmetic and copies ran while one was open for 1% -> 0% of each run, Pallas kernels for 3% -> 3%
where the time goes in v4:
time: 99.2 us; the launch traced here: 99.1 us
  starting transfers between devices  43.7 us (44%)
  waiting for transfers between devices  42.1 us (42%)
  Pallas kernels  9.9 us (10%)
  other arithmetic  3.11 us (3%)
    ppermute x7, starting transfers between devices, along_z(): lax.ppermute(value, 'shot', [(i, (i + hop) % planes) for i in range(plane...  16.4 us
    ppermute x7, waiting for transfers between devices, along_x(): return lax.ppermute(value, 'ry', pairs)  14.6 us
    ppermute x7, waiting for transfers between devices, along_z(): lax.ppermute(value, 'shot', [(i, (i + hop) % planes) for i in range(plane...  12.3 us
    ppermute x6, waiting for transfers between devices, along_y(): return lax.ppermute(value, 'rx', [(i, (i + hop) % 4) for i in range(4)])  11.8 us
    ppermute x7, starting transfers between devices, along_x(): return lax.ppermute(value, 'ry', pairs)  9.66 us
    ppermute x3, starting transfers between devices, swap(): return lax.ppermute(value, 'ry', [(i, i ^ 1) for i in range(8)])  9.32 us
    ppermute x6, starting transfers between devices, along_y(): return lax.ppermute(value, 'rx', [(i, (i + hop) % 4) for i in range(4)])  8.34 us
    pallas_call x1, Pallas kernels, front(): pl.pallas_call(functools.partial(front_kernel, planes=planes, block=block...  4.97 us
  transfers between devices with their start and end apart: 23, of which 13 were waited for; matrix products, arithmetic and copies ran while one was open for 0% of the time, Pallas kernels for 3%

profile of v4, /device:TPU:1, one launch (start us, length us, event | category | flops | bytes accessed | tf_op | source)
XLA Modules:
  0.0 99.1 jit_solution(10703299300728172239)
XLA Ops:
  0.0 0.7 convert_element_type.6
  0.7 0.7 convert_element_type.7
  1.3 0.1 maximum_bitcast_fusion.small_ref
  1.4 5.0 %front.1 = (bf16[8,8,32,128]{3,2,1,0:T(8,128)(2,1)S(1)}, bf16[8,8,32,128]{3,2,1,0:T(8,128)(2,1)S(1)}) custom-call(f32[1,128]{1,0:T(1,128)S(1)} %maximum_bitcast_fusion.small_ref, bf16[128,32,1024]{2,1,0:T(8,128)(2,1)} %traces_ref.1), custom_call_target="tpu_custom_call" | custom-call | flops 2147483648 | bytes 8388608 | tf_op jit(solution)/shard_map/front/pallas_call | solution.py:136
  6.4 3.3 %collective-permute-start = (bf16[8,8,32,128]{3,2,1,0:T(8,128)(2,1)S(1)}, bf16[8,8,32,128]{3,2,1,0:T(8,128)(2,1)S(1)}, u32[]{:S(2)}, u32[]{:S(2)}) collective-permute-start(bf16[8,8,32,128]{3,2,1,0:T(8,128)(2,1)S(1)} %get-tuple-element.29), channel_id=1, source_target_pairs={{0,1},{1,0},{2,3},{3,2},{4,5},{5,4},{6,7},{7,6},{8,9},{9,8},{10,11... | collective-permute-start | bytes 1572872 | tf_op jit(solution)/shard_map/ppermute | solution.py:436
  9.7 1.5 %collective-permute-done = bf16[8,8,32,128]{3,2,1,0:T(8,128)(2,1)S(1)} collective-permute-done((bf16[8,8,32,128]{3,2,1,0:T(8,128)(2,1)S(1)}, bf16[8,8,32,128]{3,2,1,0:T(8,128)(2,1)S(1)}, u32[]{:S(2)}, u32[]{:S(2)}) %collective-permute-start) | collective-permute-done | bytes 524320 | tf_op jit(solution)/shard_map/ppermute | solution.py:436
  11.3 2.7 %collective-permute-start.5 = (bf16[8,64,128]{2,1,0:T(8,128)(2,1)S(1)}, bf16[8,64,128]{2,1,0:T(8,128)(2,1)S(1)}, u32[]{:S(2)}, u32[]{:S(2)}) collective-permute-start(bf16[8,64,128]{2,1,0:T(8,128)(2,1)S(1)} %pad_maximum_fusion.5), channel_id=1, source_target_pairs={{0,96},{32,128},{64,160},{96,192},{128,224},{160,0},{192,32},{224,... | collective-permute-start | bytes 393224 | tf_op jit(solution)/shard_map/ppermute | solution.py:433
  14.0 2.2 %collective-permute-start.6 = (bf16[8,64,128]{2,1,0:T(8,128)(2,1)S(1)}, bf16[8,64,128]{2,1,0:T(8,128)(2,1)S(1)}, u32[]{:S(2)}, u32[]{:S(2)}) collective-permute-start(bf16[8,64,128]{2,1,0:T(8,128)(2,1)S(1)} %pad_maximum_fusion.6), channel_id=1, source_target_pairs={{0,160},{32,192},{64,224},{96,0},{128,32},{160,64},{192,96},{224,1... | collective-permute-start | bytes 393224 | tf_op jit(solution)/shard_map/ppermute | solution.py:433
  16.2 5.0 %collective-permute-start.7 = (bf16[8,64,128]{2,1,0:T(8,128)(2,1)S(1)}, bf16[8,64,128]{2,1,0:T(8,128)(2,1)S(1)}, u32[]{:S(2)}, u32[]{:S(2)}) collective-permute-start(bf16[8,64,128]{2,1,0:T(8,128)(2,1)S(1)} %pad_maximum_fusion.7), channel_id=1, source_target_pairs={{0,128},{32,160},{64,192},{96,224},{128,0},{160,32},{192,64},{224,... | collective-permute-start | bytes 393224 | tf_op jit(solution)/shard_map/ppermute | solution.py:433
  21.2 1.3 %collective-permute-start.4 = (bf16[8,64,128]{2,1,0:T(8,128)(2,1)S(1)}, bf16[8,64,128]{2,1,0:T(8,128)(2,1)S(1)}, u32[]{:S(2)}, u32[]{:S(2)}) collective-permute-start(bf16[8,64,128]{2,1,0:T(8,128)(2,1)S(1)} %pad_maximum_fusion.4), channel_id=1, source_target_pairs={{0,64},{32,96},{64,128},{96,160},{128,192},{160,224},{192,0},{224,... | collective-permute-start | bytes 393224 | tf_op jit(solution)/shard_map/ppermute | solution.py:433
  22.5 2.5 %collective-permute-start.3 = (bf16[8,64,128]{2,1,0:T(8,128)(2,1)S(1)}, bf16[8,64,128]{2,1,0:T(8,128)(2,1)S(1)}, u32[]{:S(2)}, u32[]{:S(2)}) collective-permute-start(bf16[8,64,128]{2,1,0:T(8,128)(2,1)S(1)} %pad_maximum_fusion.3), channel_id=1, source_target_pairs={{0,192},{32,224},{64,0},{96,32},{128,64},{160,96},{192,128},{224,1... | collective-permute-start | bytes 393224 | tf_op jit(solution)/shard_map/ppermute | solution.py:433
  25.0 0.0 collective-permute-done.5.refs_4_
  25.0 0.8 collective-permute-start.2
  25.8 2.0 %collective-permute-start.1 = (bf16[8,64,128]{2,1,0:T(8,128)(2,1)S(1)}, bf16[8,64,128]{2,1,0:T(8,128)(2,1)S(1)}, u32[]{:S(2)}, u32[]{:S(2)}) collective-permute-start(bf16[8,64,128]{2,1,0:T(8,128)(2,1)S(1)} %pad_maximum_fusion.1), channel_id=1, source_target_pairs={{0,224},{32,0},{64,32},{96,64},{128,96},{160,128},{192,160},{224,1... | collective-permute-start | bytes 393224 | tf_op jit(solution)/shard_map/ppermute | solution.py:433
  27.8 2.7 %collective-permute-done.7.refs_6_ = bf16[8,64,128]{2,1,0:T(8,128)(2,1)S(1)} collective-permute-done((bf16[8,64,128]{2,1,0:T(8,128)(2,1)S(1)}, bf16[8,64,128]{2,1,0:T(8,128)(2,1)S(1)}, u32[]{:S(2)}, u32[]{:S(2)}) %collective-permute-start.7) | collective-permute-done | bytes 131104 | tf_op jit(solution)/shard_map/ppermute | solution.py:433
  30.5 5.6 %collective-permute-done.4.refs_3_ = bf16[8,64,128]{2,1,0:T(8,128)(2,1)S(1)} collective-permute-done((bf16[8,64,128]{2,1,0:T(8,128)(2,1)S(1)}, bf16[8,64,128]{2,1,0:T(8,128)(2,1)S(1)}, u32[]{:S(2)}, u32[]{:S(2)}) %collective-permute-start.4) | collective-permute-done | bytes 131104 | tf_op jit(solution)/shard_map/ppermute | solution.py:433
  36.2 1.9 %collective-permute-done.3.refs_2_ = bf16[8,64,128]{2,1,0:T(8,128)(2,1)S(1)} collective-permute-done((bf16[8,64,128]{2,1,0:T(8,128)(2,1)S(1)}, bf16[8,64,128]{2,1,0:T(8,128)(2,1)S(1)}, u32[]{:S(2)}, u32[]{:S(2)}) %collective-permute-start.3) | collective-permute-done | bytes 131104 | tf_op jit(solution)/shard_map/ppermute | solution.py:433
  38.0 0.4 collective-permute-done.2.refs_1_
  38.4 1.7 %collective-permute-done.1.refs_0_ = bf16[8,64,128]{2,1,0:T(8,128)(2,1)S(1)} collective-permute-done((bf16[8,64,128]{2,1,0:T(8,128)(2,1)S(1)}, bf16[8,64,128]{2,1,0:T(8,128)(2,1)S(1)}, u32[]{:S(2)}, u32[]{:S(2)}) %collective-permute-start.1) | collective-permute-done | bytes 131104 | tf_op jit(solution)/shard_map/ppermute | solution.py:433
  40.2 0.2 sort.1
  40.3 2.6 %collective-permute-start.10 = (bf16[2,8,64,128]{3,2,1,0:T(8,128)(2,1)S(1)}, bf16[2,8,64,128]{3,2,1,0:T(8,128)(2,1)S(1)}, u32[]{:S(2)}, u32[]{:S(2)}) collective-permute-start(bf16[2,8,64,128]{3,2,1,0:T(8,128)(2,1)S(1)} %get-tuple-element.32), channel_id=1, source_target_pairs={{0,6},{1,7},{2,0},{3,1},{4,2},{5,3},{6,4},{7,5},{8,14},{9,15},{10,... | collective-permute-start | bytes 786440 | tf_op jit(solution)/shard_map/ppermute | solution.py:427
  42.9 1.7 %collective-permute-start.12 = (bf16[2,8,64,128]{3,2,1,0:T(8,128)(2,1)S(1)}, bf16[2,8,64,128]{3,2,1,0:T(8,128)(2,1)S(1)}, u32[]{:S(2)}, u32[]{:S(2)}) collective-permute-start(bf16[2,8,64,128]{3,2,1,0:T(8,128)(2,1)S(1)} %get-tuple-element.34), channel_id=1, source_target_pairs={{0,4},{1,5},{2,6},{3,7},{4,0},{5,1},{6,2},{7,3},{8,12},{9,13},{10,... | collective-permute-start | bytes 786440 | tf_op jit(solution)/shard_map/ppermute | solution.py:427
  44.6 1.3 %collective-permute-start.8 = (bf16[2,8,64,128]{3,2,1,0:T(8,128)(2,1)S(1)}, bf16[2,8,64,128]{3,2,1,0:T(8,128)(2,1)S(1)}, u32[]{:S(2)}, u32[]{:S(2)}) collective-permute-start(bf16[2,8,64,128]{3,2,1,0:T(8,128)(2,1)S(1)} %get-tuple-element.31.refs_2_), channel_id=1, source_target_pairs={{0,8},{8,16},{16,24},{24,0},{1,9},{9,17},{17,25},{25,1},{2,10},{10... | collective-permute-start | bytes 786440 | tf_op jit(solution)/shard_map/ppermute | solution.py:430
  45.9 1.4 %collective-permute-start.9 = (bf16[2,8,64,128]{3,2,1,0:T(8,128)(2,1)S(1)}, bf16[2,8,64,128]{3,2,1,0:T(8,128)(2,1)S(1)}, u32[]{:S(2)}, u32[]{:S(2)}) collective-permute-start(bf16[2,8,64,128]{3,2,1,0:T(8,128)(2,1)S(1)} %get-tuple-element.31.refs_2_), channel_id=1, source_target_pairs={{0,24},{8,0},{16,8},{24,16},{1,25},{9,1},{17,9},{25,17},{2,26},{10... | collective-permute-start | bytes 786440 | tf_op jit(solution)/shard_map/ppermute | solution.py:430
  47.4 0.9 collective-permute-done.10.down_turn
  48.2 3.4 %collective-permute-done.11.up_turn = bf16[2,8,64,128]{3,2,1,0:T(8,128)(2,1)S(1)} collective-permute-done((bf16[2,8,64,128]{3,2,1,0:T(8,128)(2,1)S(1)}, bf16[2,8,64,128]{3,2,1,0:T(8,128)(2,1)S(1)}, u32[]{:S(2)}, u32[]{:S(2)}) %collective-permute-start.11) | collective-permute-done | bytes 262176 | tf_op jit(solution)/shard_map/ppermute | solution.py:427
  51.6 3.8 %collective-permute-done.12.far_turn = bf16[2,8,64,128]{3,2,1,0:T(8,128)(2,1)S(1)} collective-permute-done((bf16[2,8,64,128]{3,2,1,0:T(8,128)(2,1)S(1)}, bf16[2,8,64,128]{3,2,1,0:T(8,128)(2,1)S(1)}, u32[]{:S(2)}, u32[]{:S(2)}) %collective-permute-start.12) | collective-permute-done | bytes 262176 | tf_op jit(solution)/shard_map/ppermute | solution.py:427
  55.5 0.2 second.1
  55.7 1.4 %collective-permute-start.13 = (bf16[3,2,8,64,128]{4,3,2,1,0:T(8,128)(2,1)S(1)}, bf16[3,2,8,64,128]{4,3,2,1,0:T(8,128)(2,1)S(1)}, u32[]{:S(2)}, u32[]{:S(2)}) collective-permute-start(bf16[3,2,8,64,128]{4,3,2,1,0:T(8,128)(2,1)S(1)} %get-tuple-element.35.refs_3_), channel_id=1, source_target_pairs={{0,8},{8,16},{16,24},{24,0},{1,9},{9,17},{17,25},{25,1},{2,10},{10... | collective-permute-start | bytes 2359304 | tf_op jit(solution)/shard_map/ppermute | solution.py:430
  57.0 1.5 %collective-permute-start.14 = (bf16[3,2,8,64,128]{4,3,2,1,0:T(8,128)(2,1)S(1)}, bf16[3,2,8,64,128]{4,3,2,1,0:T(8,128)(2,1)S(1)}, u32[]{:S(2)}, u32[]{:S(2)}) collective-permute-start(bf16[3,2,8,64,128]{4,3,2,1,0:T(8,128)(2,1)S(1)} %get-tuple-element.35.refs_3_), channel_id=1, source_target_pairs={{0,24},{8,0},{16,8},{24,16},{1,25},{9,1},{17,9},{25,17},{2,26},{10... | collective-permute-start | bytes 2359304 | tf_op jit(solution)/shard_map/ppermute | solution.py:430
  58.5 2.7 %collective-permute-start.16 = (bf16[6,8,64,128]{3,2,1,0:T(8,128)(2,1)S(1)}, bf16[6,8,64,128]{3,2,1,0:T(8,128)(2,1)S(1)}, u32[]{:S(2)}, u32[]{:S(2)}) collective-permute-start(bf16[6,8,64,128]{3,2,1,0:T(8,128)(2,1)S(1)} %get-tuple-element.37), channel_id=1, source_target_pairs={{0,6},{1,7},{2,0},{3,1},{4,2},{5,3},{6,4},{7,5},{8,14},{9,15},{10,... | collective-permute-start | bytes 2359304 | tf_op jit(solution)/shard_map/ppermute | solution.py:427
  61.2 11.8 %collective-permute-done.13.refs_0_.y_up = bf16[3,2,8,64,128]{4,3,2,1,0:T(8,128)(2,1)S(1)} collective-permute-done((bf16[3,2,8,64,128]{4,3,2,1,0:T(8,128)(2,1)S(1)}, bf16[3,2,8,64,128]{4,3,2,1,0:T(8,128)(2,1)S(1)}, u32[]{:S(2)}, u32[]{:S(2)}) %collective-permute-start.13) | collective-permute-done | bytes 786464 | tf_op jit(solution)/shard_map/ppermute | solution.py:430
  73.0 2.3 %collective-permute-done.15.refs_5_.x_up = bf16[6,8,64,128]{3,2,1,0:T(8,128)(2,1)S(1)} collective-permute-done((bf16[6,8,64,128]{3,2,1,0:T(8,128)(2,1)S(1)}, bf16[6,8,64,128]{3,2,1,0:T(8,128)(2,1)S(1)}, u32[]{:S(2)}, u32[]{:S(2)}) %collective-permute-start.15) | collective-permute-done | bytes 786464 | tf_op jit(solution)/shard_map/ppermute | solution.py:427
  75.3 0.1 third.1
  75.5 0.1 collective-permute-start.17
  75.5 2.7 %collective-permute-start.18 = (bf16[2,2,8,64,128]{4,3,2,1,0:T(8,128)(2,1)S(1)}, bf16[2,2,8,64,128]{4,3,2,1,0:T(8,128)(2,1)S(1)}, u32[]{:S(2)}, u32[]{:S(2)}) collective-permute-start(bf16[2,2,8,64,128]{4,3,2,1,0:T(8,128)(2,1)S(1)} %get-tuple-element.42), channel_id=1, source_target_pairs={{0,24},{8,0},{16,8},{24,16},{1,25},{9,1},{17,9},{25,17},{2,26},{10... | collective-permute-start | bytes 1572872 | tf_op jit(solution)/shard_map/ppermute | solution.py:430
  78.2 0.9 collective-permute-start.19
  79.1 1.8 %collective-permute-start.20 = (bf16[3,8,64,128]{3,2,1,0:T(8,128)(2,1)S(1)}, bf16[3,8,64,128]{3,2,1,0:T(8,128)(2,1)S(1)}, u32[]{:S(2)}, u32[]{:S(2)}) collective-permute-start(bf16[3,8,64,128]{3,2,1,0:T(8,128)(2,1)S(1)} %get-tuple-element.44), channel_id=1, source_target_pairs={{0,6},{1,7},{2,0},{3,1},{4,2},{5,3},{6,4},{7,5},{8,14},{9,15},{10,... | collective-permute-start | bytes 1179656 | tf_op jit(solution)/shard_map/ppermute | solution.py:427
  80.9 1.2 %stage.1 = (bf16[8,8,256,128]{3,2,1,0:T(8,128)(2,1)S(1)}, bf16[2,8,1024,128]{3,2,1,0:T(8,128)(2,1)S(1)}) custom-call(bf16[3,2,8,64,128]{4,3,2,1,0:T(8,128)(2,1)S(1)} %collective-permute-done.13.refs_0_.y_up, bf16[3,2,8,64,128]{4,3,2,1,0:T(8,128)(2,1)S(1)} %collective-permute-done.14.refs_1_.y_down, bf16[2,8,64,128]{3,2,1,0:T(8,128)(2,1)S(1)} %get-tuple-element.31.refs_2_, ...), custom_call_target="tpu_custom_call" | custom-call | bytes 8388608 | tf_op jit(solution)/shard_map/stage/pallas_call | solution.py:315
  82.1 4.3 %collective-permute-done.19.refs_4_ = bf16[3,8,64,128]{3,2,1,0:T(8,128)(2,1)S(1)} collective-permute-done((bf16[3,8,64,128]{3,2,1,0:T(8,128)(2,1)S(1)}, bf16[3,8,64,128]{3,2,1,0:T(8,128)(2,1)S(1)}, u32[]{:S(2)}, u32[]{:S(2)}) %collective-permute-start.19) | collective-permute-done | bytes 393248 | tf_op jit(solution)/shard_map/ppermute | solution.py:427
  86.4 1.8 %first_product.1 = (bf16[8,8,256,128]{3,2,1,0:T(8,128)(2,1)S(1)}, bf16[2,8,1024,128]{3,2,1,0:T(8,128)(2,1)S(1)}, f32[2,2,128,256]{3,2,1,0:T(8,128)S(1)}, f32[2,2,128,256]{3,2,1,0:T(8,128)S(1)}) custom-call(bf16[8,8,256,128]{3,2,1,0:T(8,128)(2,1)S(1)} %get-tuple-element.39.refs_0_, ...), custom_call_target="tpu_custom_call", output_to_operand_aliasing={{0}: (0, {}), {1}: (1, {})} | custom-call | flops 1073741824 | bytes 8388608 | tf_op jit(solution)/shard_map/first_product/pallas_call | solution.py:389
  88.2 5.9 %collective-permute-start.21 = (f32[2,2,128,256]{3,2,1,0:T(8,128)S(1)}, f32[2,2,128,256]{3,2,1,0:T(8,128)S(1)}, u32[]{:S(2)}, u32[]{:S(2)}) collective-permute-start(f32[2,2,128,256]{3,2,1,0:T(8,128)S(1)} %get-tuple-element.46), channel_id=1, source_target_pairs={{0,1},{1,0},{2,3},{3,2},{4,5},{5,4},{6,7},{7,6},{8,9},{9,8},{10,11... | collective-permute-start | bytes 1572872 | tf_op jit(solution)/shard_map/ppermute | solution.py:436
  94.0 1.5 %second_product.1 = (f32[2,2,128,256]{3,2,1,0:T(8,128)S(1)}, f32[2,2,128,256]{3,2,1,0:T(8,128)S(1)}) custom-call(bf16[8,8,256,128]{3,2,1,0:T(8,128)(2,1)S(1)} %get-tuple-element.47.right, bf16[2,8,1024,128]{3,2,1,0:T(8,128)(2,1)S(1)} %get-tuple-element.48.left), custom_call_target="tpu_custom_call" | custom-call | flops 1073741824 | bytes 8388608 | tf_op jit(solution)/shard_map/second_product/pallas_call | solution.py:410
  95.5 0.1 collective-permute-start.22
  95.6 0.1 broadcast_select_fusion.3
  95.7 1.8 %collective-permute-done.22 = f32[2,2,128,256]{3,2,1,0:T(8,128)S(1)} collective-permute-done((f32[2,2,128,256]{3,2,1,0:T(8,128)S(1)}, f32[2,2,128,256]{3,2,1,0:T(8,128)S(1)}, u32[]{:S(2)}, u32[]{:S(2)}) %collective-permute-start.22) | collective-permute-done | bytes 524320 | tf_op jit(solution)/shard_map/ppermute | solution.py:436
  97.5 0.1 broadcast_select_fusion.2
  97.6 1.5 %pad_maximum_fusion = f32[8,2,128,256]{3,2,1,0:T(8,128)} fusion(f32[2,2,128,256]{3,2,1,0:T(8,128)S(1)} %get-tuple-element.54, f32[2,2,128,256]{3,2,1,0:T(8,128)S(1)} %get-tuple-element.52, f32[2,2,128,256]{3,2,1,0:T(8,128)S(1)} %get-tuple-element.53, f32[2,2,128,256]{3,2,1,0:T(8,128)S(1)} %get-tuple-element.51), kind=kLoop, calls=%fused_computation | loop fusion | flops 1572864 | bytes 4194304 | tf_op jit(solution)/shard_map/concatenate | solution.py:464
  (21 shorter events, 0.2 us)
Async XLA Ops:
  6.4 4.9 %collective-permute-start = (bf16[8,8,32,128]{3,2,1,0:T(8,128)(2,1)S(1)}, bf16[8,8,32,128]{3,2,1,0:T(8,128)(2,1)S(1)}, u32[]{:S(2)}, u32[]{:S(2)}) collective-permute-start(bf16[8,8,32,128]{3,2,1,0:T(8,128)(2,1)S(1)} %get-tuple-element.29), channel_id=1, source_target_pairs={{0,1},{1,0},{2,3},{3,2},{4,5},{5,4},{6,7},{7,6},{8,9},{9,8},{10,11... | collective-permute-start | bytes 1572872 | tf_op jit(solution)/shard_map/ppermute | solution.py:436
  11.3 13.7 %collective-permute-start.5 = (bf16[8,64,128]{2,1,0:T(8,128)(2,1)S(1)}, bf16[8,64,128]{2,1,0:T(8,128)(2,1)S(1)}, u32[]{:S(2)}, u32[]{:S(2)}) collective-permute-start(bf16[8,64,128]{2,1,0:T(8,128)(2,1)S(1)} %pad_maximum_fusion.5), channel_id=1, source_target_pairs={{0,96},{32,128},{64,160},{96,192},{128,224},{160,0},{192,32},{224,... | collective-permute-start | bytes 393224 | tf_op jit(solution)/shard_map/ppermute | solution.py:433
  14.0 11.8 %collective-permute-start.6 = (bf16[8,64,128]{2,1,0:T(8,128)(2,1)S(1)}, bf16[8,64,128]{2,1,0:T(8,128)(2,1)S(1)}, u32[]{:S(2)}, u32[]{:S(2)}) collective-permute-start(bf16[8,64,128]{2,1,0:T(8,128)(2,1)S(1)} %pad_maximum_fusion.6), channel_id=1, source_target_pairs={{0,160},{32,192},{64,224},{96,0},{128,32},{160,64},{192,96},{224,1... | collective-permute-start | bytes 393224 | tf_op jit(solution)/shard_map/ppermute | solution.py:433
  16.2 14.3 %collective-permute-start.7 = (bf16[8,64,128]{2,1,0:T(8,128)(2,1)S(1)}, bf16[8,64,128]{2,1,0:T(8,128)(2,1)S(1)}, u32[]{:S(2)}, u32[]{:S(2)}) collective-permute-start(bf16[8,64,128]{2,1,0:T(8,128)(2,1)S(1)} %pad_maximum_fusion.7), channel_id=1, source_target_pairs={{0,128},{32,160},{64,192},{96,224},{128,0},{160,32},{192,64},{224,... | collective-permute-start | bytes 393224 | tf_op jit(solution)/shard_map/ppermute | solution.py:433
  21.2 15.0 %collective-permute-start.4 = (bf16[8,64,128]{2,1,0:T(8,128)(2,1)S(1)}, bf16[8,64,128]{2,1,0:T(8,128)(2,1)S(1)}, u32[]{:S(2)}, u32[]{:S(2)}) collective-permute-start(bf16[8,64,128]{2,1,0:T(8,128)(2,1)S(1)} %pad_maximum_fusion.4), channel_id=1, source_target_pairs={{0,64},{32,96},{64,128},{96,160},{128,192},{160,224},{192,0},{224,... | collective-permute-start | bytes 393224 | tf_op jit(solution)/shard_map/ppermute | solution.py:433
  22.5 15.5 %collective-permute-start.3 = (bf16[8,64,128]{2,1,0:T(8,128)(2,1)S(1)}, bf16[8,64,128]{2,1,0:T(8,128)(2,1)S(1)}, u32[]{:S(2)}, u32[]{:S(2)}) collective-permute-start(bf16[8,64,128]{2,1,0:T(8,128)(2,1)S(1)} %pad_maximum_fusion.3), channel_id=1, source_target_pairs={{0,192},{32,224},{64,0},{96,32},{128,64},{160,96},{192,128},{224,1... | collective-permute-start | bytes 393224 | tf_op jit(solution)/shard_map/ppermute | solution.py:433
  25.0 13.4 %collective-permute-start.2 = (bf16[8,64,128]{2,1,0:T(8,128)(2,1)S(1)}, bf16[8,64,128]{2,1,0:T(8,128)(2,1)S(1)}, u32[]{:S(2)}, u32[]{:S(2)}) collective-permute-start(bf16[8,64,128]{2,1,0:T(8,128)(2,1)S(1)} %pad_maximum_fusion.2), channel_id=1, source_target_pairs={{0,32},{32,64},{64,96},{96,128},{128,160},{160,192},{192,224},{224... | collective-permute-start | bytes 393224 | tf_op jit(solution)/shard_map/ppermute | solution.py:433
  25.8 14.3 %collective-permute-start.1 = (bf16[8,64,128]{2,1,0:T(8,128)(2,1)S(1)}, bf16[8,64,128]{2,1,0:T(8,128)(2,1)S(1)}, u32[]{:S(2)}, u32[]{:S(2)}) collective-permute-start(bf16[8,64,128]{2,1,0:T(8,128)(2,1)S(1)} %pad_maximum_fusion.1), channel_id=1, source_target_pairs={{0,224},{32,0},{64,32},{96,64},{128,96},{160,128},{192,160},{224,1... | collective-permute-start | bytes 393224 | tf_op jit(solution)/shard_map/ppermute | solution.py:433
  40.3 7.9 %collective-permute-start.10 = (bf16[2,8,64,128]{3,2,1,0:T(8,128)(2,1)S(1)}, bf16[2,8,64,128]{3,2,1,0:T(8,128)(2,1)S(1)}, u32[]{:S(2)}, u32[]{:S(2)}) collective-permute-start(bf16[2,8,64,128]{3,2,1,0:T(8,128)(2,1)S(1)} %get-tuple-element.32), channel_id=1, source_target_pairs={{0,6},{1,7},{2,0},{3,1},{4,2},{5,3},{6,4},{7,5},{8,14},{9,15},{10,... | collective-permute-start | bytes 786440 | tf_op jit(solution)/shard_map/ppermute | solution.py:427
  42.9 8.7 %collective-permute-start.11 = (bf16[2,8,64,128]{3,2,1,0:T(8,128)(2,1)S(1)}, bf16[2,8,64,128]{3,2,1,0:T(8,128)(2,1)S(1)}, u32[]{:S(2)}, u32[]{:S(2)}) collective-permute-start(bf16[2,8,64,128]{3,2,1,0:T(8,128)(2,1)S(1)} %get-tuple-element.33), channel_id=1, source_target_pairs={{0,2},{1,3},{2,4},{3,5},{4,6},{5,7},{6,0},{7,1},{8,10},{9,11},{10,... | collective-permute-start | bytes 786440 | tf_op jit(solution)/shard_map/ppermute | solution.py:427
  42.9 12.6 %collective-permute-start.12 = (bf16[2,8,64,128]{3,2,1,0:T(8,128)(2,1)S(1)}, bf16[2,8,64,128]{3,2,1,0:T(8,128)(2,1)S(1)}, u32[]{:S(2)}, u32[]{:S(2)}) collective-permute-start(bf16[2,8,64,128]{3,2,1,0:T(8,128)(2,1)S(1)} %get-tuple-element.34), channel_id=1, source_target_pairs={{0,4},{1,5},{2,6},{3,7},{4,0},{5,1},{6,2},{7,3},{8,12},{9,13},{10,... | collective-permute-start | bytes 786440 | tf_op jit(solution)/shard_map/ppermute | solution.py:427
  44.6 10.8 %collective-permute-start.8 = (bf16[2,8,64,128]{3,2,1,0:T(8,128)(2,1)S(1)}, bf16[2,8,64,128]{3,2,1,0:T(8,128)(2,1)S(1)}, u32[]{:S(2)}, u32[]{:S(2)}) collective-permute-start(bf16[2,8,64,128]{3,2,1,0:T(8,128)(2,1)S(1)} %get-tuple-element.31.refs_2_), channel_id=1, source_target_pairs={{0,8},{8,16},{16,24},{24,0},{1,9},{9,17},{17,25},{25,1},{2,10},{10... | collective-permute-start | bytes 786440 | tf_op jit(solution)/shard_map/ppermute | solution.py:430
  45.9 9.5 %collective-permute-start.9 = (bf16[2,8,64,128]{3,2,1,0:T(8,128)(2,1)S(1)}, bf16[2,8,64,128]{3,2,1,0:T(8,128)(2,1)S(1)}, u32[]{:S(2)}, u32[]{:S(2)}) collective-permute-start(bf16[2,8,64,128]{3,2,1,0:T(8,128)(2,1)S(1)} %get-tuple-element.31.refs_2_), channel_id=1, source_target_pairs={{0,24},{8,0},{16,8},{24,16},{1,25},{9,1},{17,9},{25,17},{2,26},{10... | collective-permute-start | bytes 786440 | tf_op jit(solution)/shard_map/ppermute | solution.py:430
  55.7 17.4 %collective-permute-start.13 = (bf16[3,2,8,64,128]{4,3,2,1,0:T(8,128)(2,1)S(1)}, bf16[3,2,8,64,128]{4,3,2,1,0:T(8,128)(2,1)S(1)}, u32[]{:S(2)}, u32[]{:S(2)}) collective-permute-start(bf16[3,2,8,64,128]{4,3,2,1,0:T(8,128)(2,1)S(1)} %get-tuple-element.35.refs_3_), channel_id=1, source_target_pairs={{0,8},{8,16},{16,24},{24,0},{1,9},{9,17},{17,25},{25,1},{2,10},{10... | collective-permute-start | bytes 2359304 | tf_op jit(solution)/shard_map/ppermute | solution.py:430
  57.0 16.0 %collective-permute-start.14 = (bf16[3,2,8,64,128]{4,3,2,1,0:T(8,128)(2,1)S(1)}, bf16[3,2,8,64,128]{4,3,2,1,0:T(8,128)(2,1)S(1)}, u32[]{:S(2)}, u32[]{:S(2)}) collective-permute-start(bf16[3,2,8,64,128]{4,3,2,1,0:T(8,128)(2,1)S(1)} %get-tuple-element.35.refs_3_), channel_id=1, source_target_pairs={{0,24},{8,0},{16,8},{24,16},{1,25},{9,1},{17,9},{25,17},{2,26},{10... | collective-permute-start | bytes 2359304 | tf_op jit(solution)/shard_map/ppermute | solution.py:430
  58.5 16.8 %collective-permute-start.15 = (bf16[6,8,64,128]{3,2,1,0:T(8,128)(2,1)S(1)}, bf16[6,8,64,128]{3,2,1,0:T(8,128)(2,1)S(1)}, u32[]{:S(2)}, u32[]{:S(2)}) collective-permute-start(bf16[6,8,64,128]{3,2,1,0:T(8,128)(2,1)S(1)} %get-tuple-element.36), channel_id=1, source_target_pairs={{0,2},{1,3},{2,4},{3,5},{4,6},{5,7},{6,0},{7,1},{8,10},{9,11},{10,... | collective-permute-start | bytes 2359304 | tf_op jit(solution)/shard_map/ppermute | solution.py:427
  58.5 16.8 %collective-permute-start.16 = (bf16[6,8,64,128]{3,2,1,0:T(8,128)(2,1)S(1)}, bf16[6,8,64,128]{3,2,1,0:T(8,128)(2,1)S(1)}, u32[]{:S(2)}, u32[]{:S(2)}) collective-permute-start(bf16[6,8,64,128]{3,2,1,0:T(8,128)(2,1)S(1)} %get-tuple-element.37), channel_id=1, source_target_pairs={{0,6},{1,7},{2,0},{3,1},{4,2},{5,3},{6,4},{7,5},{8,14},{9,15},{10,... | collective-permute-start | bytes 2359304 | tf_op jit(solution)/shard_map/ppermute | solution.py:427
  75.5 10.9 %collective-permute-start.17 = (bf16[2,2,8,64,128]{4,3,2,1,0:T(8,128)(2,1)S(1)}, bf16[2,2,8,64,128]{4,3,2,1,0:T(8,128)(2,1)S(1)}, u32[]{:S(2)}, u32[]{:S(2)}) collective-permute-start(bf16[2,2,8,64,128]{4,3,2,1,0:T(8,128)(2,1)S(1)} %get-tuple-element.41), channel_id=1, source_target_pairs={{0,8},{8,16},{16,24},{24,0},{1,9},{9,17},{17,25},{25,1},{2,10},{10... | collective-permute-start | bytes 1572872 | tf_op jit(solution)/shard_map/ppermute | solution.py:430
  75.5 10.8 %collective-permute-start.18 = (bf16[2,2,8,64,128]{4,3,2,1,0:T(8,128)(2,1)S(1)}, bf16[2,2,8,64,128]{4,3,2,1,0:T(8,128)(2,1)S(1)}, u32[]{:S(2)}, u32[]{:S(2)}) collective-permute-start(bf16[2,2,8,64,128]{4,3,2,1,0:T(8,128)(2,1)S(1)} %get-tuple-element.42), channel_id=1, source_target_pairs={{0,24},{8,0},{16,8},{24,16},{1,25},{9,1},{17,9},{25,17},{2,26},{10... | collective-permute-start | bytes 1572872 | tf_op jit(solution)/shard_map/ppermute | solution.py:430
  78.2 8.1 %collective-permute-start.19 = (bf16[3,8,64,128]{3,2,1,0:T(8,128)(2,1)S(1)}, bf16[3,8,64,128]{3,2,1,0:T(8,128)(2,1)S(1)}, u32[]{:S(2)}, u32[]{:S(2)}) collective-permute-start(bf16[3,8,64,128]{3,2,1,0:T(8,128)(2,1)S(1)} %get-tuple-element.43), channel_id=1, source_target_pairs={{0,2},{1,3},{2,4},{3,5},{4,6},{5,7},{6,0},{7,1},{8,10},{9,11},{10,... | collective-permute-start | bytes 1179656 | tf_op jit(solution)/shard_map/ppermute | solution.py:427
  79.1 7.2 %collective-permute-start.20 = (bf16[3,8,64,128]{3,2,1,0:T(8,128)(2,1)S(1)}, bf16[3,8,64,128]{3,2,1,0:T(8,128)(2,1)S(1)}, u32[]{:S(2)}, u32[]{:S(2)}) collective-permute-start(bf16[3,8,64,128]{3,2,1,0:T(8,128)(2,1)S(1)} %get-tuple-element.44), channel_id=1, source_target_pairs={{0,6},{1,7},{2,0},{3,1},{4,2},{5,3},{6,4},{7,5},{8,14},{9,15},{10,... | collective-permute-start | bytes 1179656 | tf_op jit(solution)/shard_map/ppermute | solution.py:427
  88.2 7.4 %collective-permute-start.21 = (f32[2,2,128,256]{3,2,1,0:T(8,128)S(1)}, f32[2,2,128,256]{3,2,1,0:T(8,128)S(1)}, u32[]{:S(2)}, u32[]{:S(2)}) collective-permute-start(f32[2,2,128,256]{3,2,1,0:T(8,128)S(1)} %get-tuple-element.46), channel_id=1, source_target_pairs={{0,1},{1,0},{2,3},{3,2},{4,5},{5,4},{6,7},{7,6},{8,9},{9,8},{10,11... | collective-permute-start | bytes 1572872 | tf_op jit(solution)/shard_map/ppermute | solution.py:436
  95.5 2.0 %collective-permute-start.22 = (f32[2,2,128,256]{3,2,1,0:T(8,128)S(1)}, f32[2,2,128,256]{3,2,1,0:T(8,128)S(1)}, u32[]{:S(2)}, u32[]{:S(2)}) collective-permute-start(f32[2,2,128,256]{3,2,1,0:T(8,128)S(1)} %get-tuple-element.50), channel_id=1, source_target_pairs={{0,1},{1,0},{2,3},{3,2},{4,5},{5,4},{6,7},{7,6},{8,9},{9,8},{10,11... | collective-permute-start | bytes 1572872 | tf_op jit(solution)/shard_map/ppermute | solution.py:436

commit v5 on v4

--- a/solution.py
+++ b/solution.py
@@ -145,8 +145,8 @@
             pltpu.VMEM((samples, 4 * count), jnp.bfloat16),
             pltpu.VMEM((samples + 128, 2 * count), jnp.bfloat16),
             pltpu.VMEM((blocks, shots, block, samples), jnp.bfloat16),
-            pltpu.VMEM((blocks, shots * block, 2 * count), jnp.float32),
-            pltpu.VMEM((blocks, block * pitch, shots), jnp.float32),
+            pltpu.VMEM((blocks, (shots + 1) * block, 2 * count), jnp.float32),
+            pltpu.VMEM((blocks, (block + 1) * pitch + 4, shots), jnp.float32),
             pltpu.SemaphoreType.DMA((blocks, parts)),
         ],
         compiler_params=pltpu.CompilerParams(vmem_limit_bytes=52 * 1024 * 1024),

time: 99.2 us -> 99.2 us (level)
  no operation moved by 1% of the time
where the time goes in v5:
time: 99.2 us; the launch traced here: 99.1 us
  starting transfers between devices  43.7 us (44%)
  waiting for transfers between devices  42.1 us (42%)
  Pallas kernels  9.9 us (10%)
  other arithmetic  3.11 us (3%)
    ppermute x7, starting transfers between devices, along_z(): lax.ppermute(value, 'shot', [(i, (i + hop) % planes) for i in range(plane...  16.4 us
    ppermute x7, waiting for transfers between devices, along_x(): return lax.ppermute(value, 'ry', pairs)  14.6 us
    ppermute x7, waiting for transfers between devices, along_z(): lax.ppermute(value, 'shot', [(i, (i + hop) % planes) for i in range(plane...  12.3 us
    ppermute x6, waiting for transfers between devices, along_y(): return lax.ppermute(value, 'rx', [(i, (i + hop) % 4) for i in range(4)])  11.8 us
    ppermute x7, starting transfers between devices, along_x(): return lax.ppermute(value, 'ry', pairs)  9.66 us
    ppermute x3, starting transfers between devices, swap(): return lax.ppermute(value, 'ry', [(i, i ^ 1) for i in range(8)])  9.32 us
    ppermute x6, starting transfers between devices, along_y(): return lax.ppermute(value, 'rx', [(i, (i + hop) % 4) for i in range(4)])  8.34 us
    pallas_call x1, Pallas kernels, front(): pl.pallas_call(functools.partial(front_kernel, planes=planes, block=block...  4.97 us
  transfers between devices with their start and end apart: 23, of which 13 were waited for; matrix products, arithmetic and copies ran while one was open for 0% of the time, Pallas kernels for 3%

profile of v5, /device:TPU:1, one launch (start us, length us, event | category | flops | bytes accessed | tf_op | source)
XLA Modules:
  0.0 99.1 jit_solution(11535989970427963169)
XLA Ops:
  0.0 0.7 convert_element_type.6
  0.7 0.7 convert_element_type.7
  1.3 0.1 maximum_bitcast_fusion.small_ref
  1.4 5.0 %front.1 = (bf16[8,8,32,128]{3,2,1,0:T(8,128)(2,1)S(1)}, bf16[8,8,32,128]{3,2,1,0:T(8,128)(2,1)S(1)}) custom-call(f32[1,128]{1,0:T(1,128)S(1)} %maximum_bitcast_fusion.small_ref, bf16[128,32,1024]{2,1,0:T(8,128)(2,1)} %traces_ref.1), custom_call_target="tpu_custom_call" | custom-call | flops 2147483648 | bytes 8388608 | tf_op jit(solution)/shard_map/front/pallas_call | solution.py:136
  6.4 3.3 %collective-permute-start = (bf16[8,8,32,128]{3,2,1,0:T(8,128)(2,1)S(1)}, bf16[8,8,32,128]{3,2,1,0:T(8,128)(2,1)S(1)}, u32[]{:S(2)}, u32[]{:S(2)}) collective-permute-start(bf16[8,8,32,128]{3,2,1,0:T(8,128)(2,1)S(1)} %get-tuple-element.29), channel_id=1, source_target_pairs={{0,1},{1,0},{2,3},{3,2},{4,5},{5,4},{6,7},{7,6},{8,9},{9,8},{10,11... | collective-permute-start | bytes 1572872 | tf_op jit(solution)/shard_map/ppermute | solution.py:436
  9.7 1.5 %collective-permute-done = bf16[8,8,32,128]{3,2,1,0:T(8,128)(2,1)S(1)} collective-permute-done((bf16[8,8,32,128]{3,2,1,0:T(8,128)(2,1)S(1)}, bf16[8,8,32,128]{3,2,1,0:T(8,128)(2,1)S(1)}, u32[]{:S(2)}, u32[]{:S(2)}) %collective-permute-start) | collective-permute-done | bytes 524320 | tf_op jit(solution)/shard_map/ppermute | solution.py:436
  11.3 2.7 %collective-permute-start.5 = (bf16[8,64,128]{2,1,0:T(8,128)(2,1)S(1)}, bf16[8,64,128]{2,1,0:T(8,128)(2,1)S(1)}, u32[]{:S(2)}, u32[]{:S(2)}) collective-permute-start(bf16[8,64,128]{2,1,0:T(8,128)(2,1)S(1)} %pad_maximum_fusion.5), channel_id=1, source_target_pairs={{0,96},{32,128},{64,160},{96,192},{128,224},{160,0},{192,32},{224,... | collective-permute-start | bytes 393224 | tf_op jit(solution)/shard_map/ppermute | solution.py:433
  14.0 2.2 %collective-permute-start.6 = (bf16[8,64,128]{2,1,0:T(8,128)(2,1)S(1)}, bf16[8,64,128]{2,1,0:T(8,128)(2,1)S(1)}, u32[]{:S(2)}, u32[]{:S(2)}) collective-permute-start(bf16[8,64,128]{2,1,0:T(8,128)(2,1)S(1)} %pad_maximum_fusion.6), channel_id=1, source_target_pairs={{0,160},{32,192},{64,224},{96,0},{128,32},{160,64},{192,96},{224,1... | collective-permute-start | bytes 393224 | tf_op jit(solution)/shard_map/ppermute | solution.py:433
  16.2 5.0 %collective-permute-start.7 = (bf16[8,64,128]{2,1,0:T(8,128)(2,1)S(1)}, bf16[8,64,128]{2,1,0:T(8,128)(2,1)S(1)}, u32[]{:S(2)}, u32[]{:S(2)}) collective-permute-start(bf16[8,64,128]{2,1,0:T(8,128)(2,1)S(1)} %pad_maximum_fusion.7), channel_id=1, source_target_pairs={{0,128},{32,160},{64,192},{96,224},{128,0},{160,32},{192,64},{224,... | collective-permute-start | bytes 393224 | tf_op jit(solution)/shard_map/ppermute | solution.py:433
  21.2 1.3 %collective-permute-start.4 = (bf16[8,64,128]{2,1,0:T(8,128)(2,1)S(1)}, bf16[8,64,128]{2,1,0:T(8,128)(2,1)S(1)}, u32[]{:S(2)}, u32[]{:S(2)}) collective-permute-start(bf16[8,64,128]{2,1,0:T(8,128)(2,1)S(1)} %pad_maximum_fusion.4), channel_id=1, source_target_pairs={{0,64},{32,96},{64,128},{96,160},{128,192},{160,224},{192,0},{224,... | collective-permute-start | bytes 393224 | tf_op jit(solution)/shard_map/ppermute | solution.py:433
  22.5 2.5 %collective-permute-start.3 = (bf16[8,64,128]{2,1,0:T(8,128)(2,1)S(1)}, bf16[8,64,128]{2,1,0:T(8,128)(2,1)S(1)}, u32[]{:S(2)}, u32[]{:S(2)}) collective-permute-start(bf16[8,64,128]{2,1,0:T(8,128)(2,1)S(1)} %pad_maximum_fusion.3), channel_id=1, source_target_pairs={{0,192},{32,224},{64,0},{96,32},{128,64},{160,96},{192,128},{224,1... | collective-permute-start | bytes 393224 | tf_op jit(solution)/shard_map/ppermute | solution.py:433
  25.0 0.8 collective-permute-start.2
  25.8 0.0 collective-permute-done.6.refs_5_
  25.8 2.0 %collective-permute-start.1 = (bf16[8,64,128]{2,1,0:T(8,128)(2,1)S(1)}, bf16[8,64,128]{2,1,0:T(8,128)(2,1)S(1)}, u32[]{:S(2)}, u32[]{:S(2)}) collective-permute-start(bf16[8,64,128]{2,1,0:T(8,128)(2,1)S(1)} %pad_maximum_fusion.1), channel_id=1, source_target_pairs={{0,224},{32,0},{64,32},{96,64},{128,96},{160,128},{192,160},{224,1... | collective-permute-start | bytes 393224 | tf_op jit(solution)/shard_map/ppermute | solution.py:433
  27.8 2.7 %collective-permute-done.7.refs_6_ = bf16[8,64,128]{2,1,0:T(8,128)(2,1)S(1)} collective-permute-done((bf16[8,64,128]{2,1,0:T(8,128)(2,1)S(1)}, bf16[8,64,128]{2,1,0:T(8,128)(2,1)S(1)}, u32[]{:S(2)}, u32[]{:S(2)}) %collective-permute-start.7) | collective-permute-done | bytes 131104 | tf_op jit(solution)/shard_map/ppermute | solution.py:433
  30.5 5.6 %collective-permute-done.4.refs_3_ = bf16[8,64,128]{2,1,0:T(8,128)(2,1)S(1)} collective-permute-done((bf16[8,64,128]{2,1,0:T(8,128)(2,1)S(1)}, bf16[8,64,128]{2,1,0:T(8,128)(2,1)S(1)}, u32[]{:S(2)}, u32[]{:S(2)}) %collective-permute-start.4) | collective-permute-done | bytes 131104 | tf_op jit(solution)/shard_map/ppermute | solution.py:433
  36.2 1.9 %collective-permute-done.3.refs_2_ = bf16[8,64,128]{2,1,0:T(8,128)(2,1)S(1)} collective-permute-done((bf16[8,64,128]{2,1,0:T(8,128)(2,1)S(1)}, bf16[8,64,128]{2,1,0:T(8,128)(2,1)S(1)}, u32[]{:S(2)}, u32[]{:S(2)}) %collective-permute-start.3) | collective-permute-done | bytes 131104 | tf_op jit(solution)/shard_map/ppermute | solution.py:433
  38.0 0.4 collective-permute-done.2.refs_1_
  38.4 1.7 %collective-permute-done.1.refs_0_ = bf16[8,64,128]{2,1,0:T(8,128)(2,1)S(1)} collective-permute-done((bf16[8,64,128]{2,1,0:T(8,128)(2,1)S(1)}, bf16[8,64,128]{2,1,0:T(8,128)(2,1)S(1)}, u32[]{:S(2)}, u32[]{:S(2)}) %collective-permute-start.1) | collective-permute-done | bytes 131104 | tf_op jit(solution)/shard_map/ppermute | solution.py:433
  40.2 0.2 sort.1
  40.3 2.6 %collective-permute-start.10 = (bf16[2,8,64,128]{3,2,1,0:T(8,128)(2,1)S(1)}, bf16[2,8,64,128]{3,2,1,0:T(8,128)(2,1)S(1)}, u32[]{:S(2)}, u32[]{:S(2)}) collective-permute-start(bf16[2,8,64,128]{3,2,1,0:T(8,128)(2,1)S(1)} %get-tuple-element.32), channel_id=1, source_target_pairs={{0,6},{1,7},{2,0},{3,1},{4,2},{5,3},{6,4},{7,5},{8,14},{9,15},{10,... | collective-permute-start | bytes 786440 | tf_op jit(solution)/shard_map/ppermute | solution.py:427
  42.9 1.7 %collective-permute-start.12 = (bf16[2,8,64,128]{3,2,1,0:T(8,128)(2,1)S(1)}, bf16[2,8,64,128]{3,2,1,0:T(8,128)(2,1)S(1)}, u32[]{:S(2)}, u32[]{:S(2)}) collective-permute-start(bf16[2,8,64,128]{3,2,1,0:T(8,128)(2,1)S(1)} %get-tuple-element.34), channel_id=1, source_target_pairs={{0,4},{1,5},{2,6},{3,7},{4,0},{5,1},{6,2},{7,3},{8,12},{9,13},{10,... | collective-permute-start | bytes 786440 | tf_op jit(solution)/shard_map/ppermute | solution.py:427
  44.6 1.3 %collective-permute-start.8 = (bf16[2,8,64,128]{3,2,1,0:T(8,128)(2,1)S(1)}, bf16[2,8,64,128]{3,2,1,0:T(8,128)(2,1)S(1)}, u32[]{:S(2)}, u32[]{:S(2)}) collective-permute-start(bf16[2,8,64,128]{3,2,1,0:T(8,128)(2,1)S(1)} %get-tuple-element.31.refs_2_), channel_id=1, source_target_pairs={{0,8},{8,16},{16,24},{24,0},{1,9},{9,17},{17,25},{25,1},{2,10},{10... | collective-permute-start | bytes 786440 | tf_op jit(solution)/shard_map/ppermute | solution.py:430
  45.9 1.4 %collective-permute-start.9 = (bf16[2,8,64,128]{3,2,1,0:T(8,128)(2,1)S(1)}, bf16[2,8,64,128]{3,2,1,0:T(8,128)(2,1)S(1)}, u32[]{:S(2)}, u32[]{:S(2)}) collective-permute-start(bf16[2,8,64,128]{3,2,1,0:T(8,128)(2,1)S(1)} %get-tuple-element.31.refs_2_), channel_id=1, source_target_pairs={{0,24},{8,0},{16,8},{24,16},{1,25},{9,1},{17,9},{25,17},{2,26},{10... | collective-permute-start | bytes 786440 | tf_op jit(solution)/shard_map/ppermute | solution.py:430
  47.4 0.9 collective-permute-done.10.down_turn
  48.2 3.4 %collective-permute-done.11.up_turn = bf16[2,8,64,128]{3,2,1,0:T(8,128)(2,1)S(1)} collective-permute-done((bf16[2,8,64,128]{3,2,1,0:T(8,128)(2,1)S(1)}, bf16[2,8,64,128]{3,2,1,0:T(8,128)(2,1)S(1)}, u32[]{:S(2)}, u32[]{:S(2)}) %collective-permute-start.11) | collective-permute-done | bytes 262176 | tf_op jit(solution)/shard_map/ppermute | solution.py:427
  51.6 3.8 %collective-permute-done.12.far_turn = bf16[2,8,64,128]{3,2,1,0:T(8,128)(2,1)S(1)} collective-permute-done((bf16[2,8,64,128]{3,2,1,0:T(8,128)(2,1)S(1)}, bf16[2,8,64,128]{3,2,1,0:T(8,128)(2,1)S(1)}, u32[]{:S(2)}, u32[]{:S(2)}) %collective-permute-start.12) | collective-permute-done | bytes 262176 | tf_op jit(solution)/shard_map/ppermute | solution.py:427
  55.5 0.2 second.1
  55.7 1.4 %collective-permute-start.13 = (bf16[3,2,8,64,128]{4,3,2,1,0:T(8,128)(2,1)S(1)}, bf16[3,2,8,64,128]{4,3,2,1,0:T(8,128)(2,1)S(1)}, u32[]{:S(2)}, u32[]{:S(2)}) collective-permute-start(bf16[3,2,8,64,128]{4,3,2,1,0:T(8,128)(2,1)S(1)} %get-tuple-element.35.refs_3_), channel_id=1, source_target_pairs={{0,8},{8,16},{16,24},{24,0},{1,9},{9,17},{17,25},{25,1},{2,10},{10... | collective-permute-start | bytes 2359304 | tf_op jit(solution)/shard_map/ppermute | solution.py:430
  57.0 1.5 %collective-permute-start.14 = (bf16[3,2,8,64,128]{4,3,2,1,0:T(8,128)(2,1)S(1)}, bf16[3,2,8,64,128]{4,3,2,1,0:T(8,128)(2,1)S(1)}, u32[]{:S(2)}, u32[]{:S(2)}) collective-permute-start(bf16[3,2,8,64,128]{4,3,2,1,0:T(8,128)(2,1)S(1)} %get-tuple-element.35.refs_3_), channel_id=1, source_target_pairs={{0,24},{8,0},{16,8},{24,16},{1,25},{9,1},{17,9},{25,17},{2,26},{10... | collective-permute-start | bytes 2359304 | tf_op jit(solution)/shard_map/ppermute | solution.py:430
  58.5 2.7 %collective-permute-start.16 = (bf16[6,8,64,128]{3,2,1,0:T(8,128)(2,1)S(1)}, bf16[6,8,64,128]{3,2,1,0:T(8,128)(2,1)S(1)}, u32[]{:S(2)}, u32[]{:S(2)}) collective-permute-start(bf16[6,8,64,128]{3,2,1,0:T(8,128)(2,1)S(1)} %get-tuple-element.37), channel_id=1, source_target_pairs={{0,6},{1,7},{2,0},{3,1},{4,2},{5,3},{6,4},{7,5},{8,14},{9,15},{10,... | collective-permute-start | bytes 2359304 | tf_op jit(solution)/shard_map/ppermute | solution.py:427
  61.2 11.8 %collective-permute-done.13.refs_0_.y_up = bf16[3,2,8,64,128]{4,3,2,1,0:T(8,128)(2,1)S(1)} collective-permute-done((bf16[3,2,8,64,128]{4,3,2,1,0:T(8,128)(2,1)S(1)}, bf16[3,2,8,64,128]{4,3,2,1,0:T(8,128)(2,1)S(1)}, u32[]{:S(2)}, u32[]{:S(2)}) %collective-permute-start.13) | collective-permute-done | bytes 786464 | tf_op jit(solution)/shard_map/ppermute | solution.py:430
  73.0 2.3 %collective-permute-done.15.refs_5_.x_up = bf16[6,8,64,128]{3,2,1,0:T(8,128)(2,1)S(1)} collective-permute-done((bf16[6,8,64,128]{3,2,1,0:T(8,128)(2,1)S(1)}, bf16[6,8,64,128]{3,2,1,0:T(8,128)(2,1)S(1)}, u32[]{:S(2)}, u32[]{:S(2)}) %collective-permute-start.15) | collective-permute-done | bytes 786464 | tf_op jit(solution)/shard_map/ppermute | solution.py:427
  75.3 0.1 third.1
  75.5 0.1 collective-permute-start.17
  75.5 2.7 %collective-permute-start.18 = (bf16[2,2,8,64,128]{4,3,2,1,0:T(8,128)(2,1)S(1)}, bf16[2,2,8,64,128]{4,3,2,1,0:T(8,128)(2,1)S(1)}, u32[]{:S(2)}, u32[]{:S(2)}) collective-permute-start(bf16[2,2,8,64,128]{4,3,2,1,0:T(8,128)(2,1)S(1)} %get-tuple-element.42), channel_id=1, source_target_pairs={{0,24},{8,0},{16,8},{24,16},{1,25},{9,1},{17,9},{25,17},{2,26},{10... | collective-permute-start | bytes 1572872 | tf_op jit(solution)/shard_map/ppermute | solution.py:430
  78.2 0.9 collective-permute-start.19
  79.1 1.8 %collective-permute-start.20 = (bf16[3,8,64,128]{3,2,1,0:T(8,128)(2,1)S(1)}, bf16[3,8,64,128]{3,2,1,0:T(8,128)(2,1)S(1)}, u32[]{:S(2)}, u32[]{:S(2)}) collective-permute-start(bf16[3,8,64,128]{3,2,1,0:T(8,128)(2,1)S(1)} %get-tuple-element.44), channel_id=1, source_target_pairs={{0,6},{1,7},{2,0},{3,1},{4,2},{5,3},{6,4},{7,5},{8,14},{9,15},{10,... | collective-permute-start | bytes 1179656 | tf_op jit(solution)/shard_map/ppermute | solution.py:427
  80.9 1.2 %stage.1 = (bf16[8,8,256,128]{3,2,1,0:T(8,128)(2,1)S(1)}, bf16[2,8,1024,128]{3,2,1,0:T(8,128)(2,1)S(1)}) custom-call(bf16[3,2,8,64,128]{4,3,2,1,0:T(8,128)(2,1)S(1)} %collective-permute-done.13.refs_0_.y_up, bf16[3,2,8,64,128]{4,3,2,1,0:T(8,128)(2,1)S(1)} %collective-permute-done.14.refs_1_.y_down, bf16[2,8,64,128]{3,2,1,0:T(8,128)(2,1)S(1)} %get-tuple-element.31.refs_2_, ...), custom_call_target="tpu_custom_call" | custom-call | bytes 8388608 | tf_op jit(solution)/shard_map/stage/pallas_call | solution.py:315
  82.1 4.3 %collective-permute-done.19.refs_4_ = bf16[3,8,64,128]{3,2,1,0:T(8,128)(2,1)S(1)} collective-permute-done((bf16[3,8,64,128]{3,2,1,0:T(8,128)(2,1)S(1)}, bf16[3,8,64,128]{3,2,1,0:T(8,128)(2,1)S(1)}, u32[]{:S(2)}, u32[]{:S(2)}) %collective-permute-start.19) | collective-permute-done | bytes 393248 | tf_op jit(solution)/shard_map/ppermute | solution.py:427
  86.4 1.8 %first_product.1 = (bf16[8,8,256,128]{3,2,1,0:T(8,128)(2,1)S(1)}, bf16[2,8,1024,128]{3,2,1,0:T(8,128)(2,1)S(1)}, f32[2,2,128,256]{3,2,1,0:T(8,128)S(1)}, f32[2,2,128,256]{3,2,1,0:T(8,128)S(1)}) custom-call(bf16[8,8,256,128]{3,2,1,0:T(8,128)(2,1)S(1)} %get-tuple-element.39.refs_0_, ...), custom_call_target="tpu_custom_call", output_to_operand_aliasing={{0}: (0, {}), {1}: (1, {})} | custom-call | flops 1073741824 | bytes 8388608 | tf_op jit(solution)/shard_map/first_product/pallas_call | solution.py:389
  88.2 5.9 %collective-permute-start.21 = (f32[2,2,128,256]{3,2,1,0:T(8,128)S(1)}, f32[2,2,128,256]{3,2,1,0:T(8,128)S(1)}, u32[]{:S(2)}, u32[]{:S(2)}) collective-permute-start(f32[2,2,128,256]{3,2,1,0:T(8,128)S(1)} %get-tuple-element.46), channel_id=1, source_target_pairs={{0,1},{1,0},{2,3},{3,2},{4,5},{5,4},{6,7},{7,6},{8,9},{9,8},{10,11... | collective-permute-start | bytes 1572872 | tf_op jit(solution)/shard_map/ppermute | solution.py:436
  94.0 1.5 %second_product.1 = (f32[2,2,128,256]{3,2,1,0:T(8,128)S(1)}, f32[2,2,128,256]{3,2,1,0:T(8,128)S(1)}) custom-call(bf16[8,8,256,128]{3,2,1,0:T(8,128)(2,1)S(1)} %get-tuple-element.47.right, bf16[2,8,1024,128]{3,2,1,0:T(8,128)(2,1)S(1)} %get-tuple-element.48.left), custom_call_target="tpu_custom_call" | custom-call | flops 1073741824 | bytes 8388608 | tf_op jit(solution)/shard_map/second_product/pallas_call | solution.py:410
  95.5 0.1 collective-permute-start.22
  95.6 0.1 broadcast_select_fusion.3
  95.7 1.8 %collective-permute-done.22 = f32[2,2,128,256]{3,2,1,0:T(8,128)S(1)} collective-permute-done((f32[2,2,128,256]{3,2,1,0:T(8,128)S(1)}, f32[2,2,128,256]{3,2,1,0:T(8,128)S(1)}, u32[]{:S(2)}, u32[]{:S(2)}) %collective-permute-start.22) | collective-permute-done | bytes 524320 | tf_op jit(solution)/shard_map/ppermute | solution.py:436
  97.5 0.1 broadcast_select_fusion.2
  97.6 1.5 %pad_maximum_fusion = f32[8,2,128,256]{3,2,1,0:T(8,128)} fusion(f32[2,2,128,256]{3,2,1,0:T(8,128)S(1)} %get-tuple-element.54, f32[2,2,128,256]{3,2,1,0:T(8,128)S(1)} %get-tuple-element.52, f32[2,2,128,256]{3,2,1,0:T(8,128)S(1)} %get-tuple-element.53, f32[2,2,128,256]{3,2,1,0:T(8,128)S(1)} %get-tuple-element.51), kind=kLoop, calls=%fused_computation | loop fusion | flops 1572864 | bytes 4194304 | tf_op jit(solution)/shard_map/concatenate | solution.py:464
  (21 shorter events, 0.2 us)
Async XLA Ops:
  6.4 4.9 %collective-permute-start = (bf16[8,8,32,128]{3,2,1,0:T(8,128)(2,1)S(1)}, bf16[8,8,32,128]{3,2,1,0:T(8,128)(2,1)S(1)}, u32[]{:S(2)}, u32[]{:S(2)}) collective-permute-start(bf16[8,8,32,128]{3,2,1,0:T(8,128)(2,1)S(1)} %get-tuple-element.29), channel_id=1, source_target_pairs={{0,1},{1,0},{2,3},{3,2},{4,5},{5,4},{6,7},{7,6},{8,9},{9,8},{10,11... | collective-permute-start | bytes 1572872 | tf_op jit(solution)/shard_map/ppermute | solution.py:436
  11.3 13.7 %collective-permute-start.5 = (bf16[8,64,128]{2,1,0:T(8,128)(2,1)S(1)}, bf16[8,64,128]{2,1,0:T(8,128)(2,1)S(1)}, u32[]{:S(2)}, u32[]{:S(2)}) collective-permute-start(bf16[8,64,128]{2,1,0:T(8,128)(2,1)S(1)} %pad_maximum_fusion.5), channel_id=1, source_target_pairs={{0,96},{32,128},{64,160},{96,192},{128,224},{160,0},{192,32},{224,... | collective-permute-start | bytes 393224 | tf_op jit(solution)/shard_map/ppermute | solution.py:433
  14.0 11.8 %collective-permute-start.6 = (bf16[8,64,128]{2,1,0:T(8,128)(2,1)S(1)}, bf16[8,64,128]{2,1,0:T(8,128)(2,1)S(1)}, u32[]{:S(2)}, u32[]{:S(2)}) collective-permute-start(bf16[8,64,128]{2,1,0:T(8,128)(2,1)S(1)} %pad_maximum_fusion.6), channel_id=1, source_target_pairs={{0,160},{32,192},{64,224},{96,0},{128,32},{160,64},{192,96},{224,1... | collective-permute-start | bytes 393224 | tf_op jit(solution)/shard_map/ppermute | solution.py:433
  16.2 14.3 %collective-permute-start.7 = (bf16[8,64,128]{2,1,0:T(8,128)(2,1)S(1)}, bf16[8,64,128]{2,1,0:T(8,128)(2,1)S(1)}, u32[]{:S(2)}, u32[]{:S(2)}) collective-permute-start(bf16[8,64,128]{2,1,0:T(8,128)(2,1)S(1)} %pad_maximum_fusion.7), channel_id=1, source_target_pairs={{0,128},{32,160},{64,192},{96,224},{128,0},{160,32},{192,64},{224,... | collective-permute-start | bytes 393224 | tf_op jit(solution)/shard_map/ppermute | solution.py:433
  21.2 15.0 %collective-permute-start.4 = (bf16[8,64,128]{2,1,0:T(8,128)(2,1)S(1)}, bf16[8,64,128]{2,1,0:T(8,128)(2,1)S(1)}, u32[]{:S(2)}, u32[]{:S(2)}) collective-permute-start(bf16[8,64,128]{2,1,0:T(8,128)(2,1)S(1)} %pad_maximum_fusion.4), channel_id=1, source_target_pairs={{0,64},{32,96},{64,128},{96,160},{128,192},{160,224},{192,0},{224,... | collective-permute-start | bytes 393224 | tf_op jit(solution)/shard_map/ppermute | solution.py:433
  22.5 15.5 %collective-permute-start.3 = (bf16[8,64,128]{2,1,0:T(8,128)(2,1)S(1)}, bf16[8,64,128]{2,1,0:T(8,128)(2,1)S(1)}, u32[]{:S(2)}, u32[]{:S(2)}) collective-permute-start(bf16[8,64,128]{2,1,0:T(8,128)(2,1)S(1)} %pad_maximum_fusion.3), channel_id=1, source_target_pairs={{0,192},{32,224},{64,0},{96,32},{128,64},{160,96},{192,128},{224,1... | collective-permute-start | bytes 393224 | tf_op jit(solution)/shard_map/ppermute | solution.py:433
  25.0 13.4 %collective-permute-start.2 = (bf16[8,64,128]{2,1,0:T(8,128)(2,1)S(1)}, bf16[8,64,128]{2,1,0:T(8,128)(2,1)S(1)}, u32[]{:S(2)}, u32[]{:S(2)}) collective-permute-start(bf16[8,64,128]{2,1,0:T(8,128)(2,1)S(1)} %pad_maximum_fusion.2), channel_id=1, source_target_pairs={{0,32},{32,64},{64,96},{96,128},{128,160},{160,192},{192,224},{224... | collective-permute-start | bytes 393224 | tf_op jit(solution)/shard_map/ppermute | solution.py:433
  25.8 14.3 %collective-permute-start.1 = (bf16[8,64,128]{2,1,0:T(8,128)(2,1)S(1)}, bf16[8,64,128]{2,1,0:T(8,128)(2,1)S(1)}, u32[]{:S(2)}, u32[]{:S(2)}) collective-permute-start(bf16[8,64,128]{2,1,0:T(8,128)(2,1)S(1)} %pad_maximum_fusion.1), channel_id=1, source_target_pairs={{0,224},{32,0},{64,32},{96,64},{128,96},{160,128},{192,160},{224,1... | collective-permute-start | bytes 393224 | tf_op jit(solution)/shard_map/ppermute | solution.py:433
  40.3 7.9 %collective-permute-start.10 = (bf16[2,8,64,128]{3,2,1,0:T(8,128)(2,1)S(1)}, bf16[2,8,64,128]{3,2,1,0:T(8,128)(2,1)S(1)}, u32[]{:S(2)}, u32[]{:S(2)}) collective-permute-start(bf16[2,8,64,128]{3,2,1,0:T(8,128)(2,1)S(1)} %get-tuple-element.32), channel_id=1, source_target_pairs={{0,6},{1,7},{2,0},{3,1},{4,2},{5,3},{6,4},{7,5},{8,14},{9,15},{10,... | collective-permute-start | bytes 786440 | tf_op jit(solution)/shard_map/ppermute | solution.py:427
  42.9 8.7 %collective-permute-start.11 = (bf16[2,8,64,128]{3,2,1,0:T(8,128)(2,1)S(1)}, bf16[2,8,64,128]{3,2,1,0:T(8,128)(2,1)S(1)}, u32[]{:S(2)}, u32[]{:S(2)}) collective-permute-start(bf16[2,8,64,128]{3,2,1,0:T(8,128)(2,1)S(1)} %get-tuple-element.33), channel_id=1, source_target_pairs={{0,2},{1,3},{2,4},{3,5},{4,6},{5,7},{6,0},{7,1},{8,10},{9,11},{10,... | collective-permute-start | bytes 786440 | tf_op jit(solution)/shard_map/ppermute | solution.py:427
  42.9 12.6 %collective-permute-start.12 = (bf16[2,8,64,128]{3,2,1,0:T(8,128)(2,1)S(1)}, bf16[2,8,64,128]{3,2,1,0:T(8,128)(2,1)S(1)}, u32[]{:S(2)}, u32[]{:S(2)}) collective-permute-start(bf16[2,8,64,128]{3,2,1,0:T(8,128)(2,1)S(1)} %get-tuple-element.34), channel_id=1, source_target_pairs={{0,4},{1,5},{2,6},{3,7},{4,0},{5,1},{6,2},{7,3},{8,12},{9,13},{10,... | collective-permute-start | bytes 786440 | tf_op jit(solution)/shard_map/ppermute | solution.py:427
  44.6 10.8 %collective-permute-start.8 = (bf16[2,8,64,128]{3,2,1,0:T(8,128)(2,1)S(1)}, bf16[2,8,64,128]{3,2,1,0:T(8,128)(2,1)S(1)}, u32[]{:S(2)}, u32[]{:S(2)}) collective-permute-start(bf16[2,8,64,128]{3,2,1,0:T(8,128)(2,1)S(1)} %get-tuple-element.31.refs_2_), channel_id=1, source_target_pairs={{0,8},{8,16},{16,24},{24,0},{1,9},{9,17},{17,25},{25,1},{2,10},{10... | collective-permute-start | bytes 786440 | tf_op jit(solution)/shard_map/ppermute | solution.py:430
  45.9 9.5 %collective-permute-start.9 = (bf16[2,8,64,128]{3,2,1,0:T(8,128)(2,1)S(1)}, bf16[2,8,64,128]{3,2,1,0:T(8,128)(2,1)S(1)}, u32[]{:S(2)}, u32[]{:S(2)}) collective-permute-start(bf16[2,8,64,128]{3,2,1,0:T(8,128)(2,1)S(1)} %get-tuple-element.31.refs_2_), channel_id=1, source_target_pairs={{0,24},{8,0},{16,8},{24,16},{1,25},{9,1},{17,9},{25,17},{2,26},{10... | collective-permute-start | bytes 786440 | tf_op jit(solution)/shard_map/ppermute | solution.py:430
  55.7 17.4 %collective-permute-start.13 = (bf16[3,2,8,64,128]{4,3,2,1,0:T(8,128)(2,1)S(1)}, bf16[3,2,8,64,128]{4,3,2,1,0:T(8,128)(2,1)S(1)}, u32[]{:S(2)}, u32[]{:S(2)}) collective-permute-start(bf16[3,2,8,64,128]{4,3,2,1,0:T(8,128)(2,1)S(1)} %get-tuple-element.35.refs_3_), channel_id=1, source_target_pairs={{0,8},{8,16},{16,24},{24,0},{1,9},{9,17},{17,25},{25,1},{2,10},{10... | collective-permute-start | bytes 2359304 | tf_op jit(solution)/shard_map/ppermute | solution.py:430
  57.0 16.0 %collective-permute-start.14 = (bf16[3,2,8,64,128]{4,3,2,1,0:T(8,128)(2,1)S(1)}, bf16[3,2,8,64,128]{4,3,2,1,0:T(8,128)(2,1)S(1)}, u32[]{:S(2)}, u32[]{:S(2)}) collective-permute-start(bf16[3,2,8,64,128]{4,3,2,1,0:T(8,128)(2,1)S(1)} %get-tuple-element.35.refs_3_), channel_id=1, source_target_pairs={{0,24},{8,0},{16,8},{24,16},{1,25},{9,1},{17,9},{25,17},{2,26},{10... | collective-permute-start | bytes 2359304 | tf_op jit(solution)/shard_map/ppermute | solution.py:430
  58.5 16.8 %collective-permute-start.15 = (bf16[6,8,64,128]{3,2,1,0:T(8,128)(2,1)S(1)}, bf16[6,8,64,128]{3,2,1,0:T(8,128)(2,1)S(1)}, u32[]{:S(2)}, u32[]{:S(2)}) collective-permute-start(bf16[6,8,64,128]{3,2,1,0:T(8,128)(2,1)S(1)} %get-tuple-element.36), channel_id=1, source_target_pairs={{0,2},{1,3},{2,4},{3,5},{4,6},{5,7},{6,0},{7,1},{8,10},{9,11},{10,... | collective-permute-start | bytes 2359304 | tf_op jit(solution)/shard_map/ppermute | solution.py:427
  58.5 16.8 %collective-permute-start.16 = (bf16[6,8,64,128]{3,2,1,0:T(8,128)(2,1)S(1)}, bf16[6,8,64,128]{3,2,1,0:T(8,128)(2,1)S(1)}, u32[]{:S(2)}, u32[]{:S(2)}) collective-permute-start(bf16[6,8,64,128]{3,2,1,0:T(8,128)(2,1)S(1)} %get-tuple-element.37), channel_id=1, source_target_pairs={{0,6},{1,7},{2,0},{3,1},{4,2},{5,3},{6,4},{7,5},{8,14},{9,15},{10,... | collective-permute-start | bytes 2359304 | tf_op jit(solution)/shard_map/ppermute | solution.py:427
  75.5 10.9 %collective-permute-start.17 = (bf16[2,2,8,64,128]{4,3,2,1,0:T(8,128)(2,1)S(1)}, bf16[2,2,8,64,128]{4,3,2,1,0:T(8,128)(2,1)S(1)}, u32[]{:S(2)}, u32[]{:S(2)}) collective-permute-start(bf16[2,2,8,64,128]{4,3,2,1,0:T(8,128)(2,1)S(1)} %get-tuple-element.41), channel_id=1, source_target_pairs={{0,8},{8,16},{16,24},{24,0},{1,9},{9,17},{17,25},{25,1},{2,10},{10... | collective-permute-start | bytes 1572872 | tf_op jit(solution)/shard_map/ppermute | solution.py:430
  75.5 10.8 %collective-permute-start.18 = (bf16[2,2,8,64,128]{4,3,2,1,0:T(8,128)(2,1)S(1)}, bf16[2,2,8,64,128]{4,3,2,1,0:T(8,128)(2,1)S(1)}, u32[]{:S(2)}, u32[]{:S(2)}) collective-permute-start(bf16[2,2,8,64,128]{4,3,2,1,0:T(8,128)(2,1)S(1)} %get-tuple-element.42), channel_id=1, source_target_pairs={{0,24},{8,0},{16,8},{24,16},{1,25},{9,1},{17,9},{25,17},{2,26},{10... | collective-permute-start | bytes 1572872 | tf_op jit(solution)/shard_map/ppermute | solution.py:430
  78.2 8.1 %collective-permute-start.19 = (bf16[3,8,64,128]{3,2,1,0:T(8,128)(2,1)S(1)}, bf16[3,8,64,128]{3,2,1,0:T(8,128)(2,1)S(1)}, u32[]{:S(2)}, u32[]{:S(2)}) collective-permute-start(bf16[3,8,64,128]{3,2,1,0:T(8,128)(2,1)S(1)} %get-tuple-element.43), channel_id=1, source_target_pairs={{0,2},{1,3},{2,4},{3,5},{4,6},{5,7},{6,0},{7,1},{8,10},{9,11},{10,... | collective-permute-start | bytes 1179656 | tf_op jit(solution)/shard_map/ppermute | solution.py:427
  79.1 7.2 %collective-permute-start.20 = (bf16[3,8,64,128]{3,2,1,0:T(8,128)(2,1)S(1)}, bf16[3,8,64,128]{3,2,1,0:T(8,128)(2,1)S(1)}, u32[]{:S(2)}, u32[]{:S(2)}) collective-permute-start(bf16[3,8,64,128]{3,2,1,0:T(8,128)(2,1)S(1)} %get-tuple-element.44), channel_id=1, source_target_pairs={{0,6},{1,7},{2,0},{3,1},{4,2},{5,3},{6,4},{7,5},{8,14},{9,15},{10,... | collective-permute-start | bytes 1179656 | tf_op jit(solution)/shard_map/ppermute | solution.py:427
  88.2 7.4 %collective-permute-start.21 = (f32[2,2,128,256]{3,2,1,0:T(8,128)S(1)}, f32[2,2,128,256]{3,2,1,0:T(8,128)S(1)}, u32[]{:S(2)}, u32[]{:S(2)}) collective-permute-start(f32[2,2,128,256]{3,2,1,0:T(8,128)S(1)} %get-tuple-element.46), channel_id=1, source_target_pairs={{0,1},{1,0},{2,3},{3,2},{4,5},{5,4},{6,7},{7,6},{8,9},{9,8},{10,11... | collective-permute-start | bytes 1572872 | tf_op jit(solution)/shard_map/ppermute | solution.py:436
  95.5 2.0 %collective-permute-start.22 = (f32[2,2,128,256]{3,2,1,0:T(8,128)S(1)}, f32[2,2,128,256]{3,2,1,0:T(8,128)S(1)}, u32[]{:S(2)}, u32[]{:S(2)}) collective-permute-start(f32[2,2,128,256]{3,2,1,0:T(8,128)S(1)} %get-tuple-element.50), channel_id=1, source_target_pairs={{0,1},{1,0},{2,3},{3,2},{4,5},{5,4},{6,7},{7,6},{8,9},{9,8},{10,11... | collective-permute-start | bytes 1572872 | tf_op jit(solution)/shard_map/ppermute | solution.py:436
